TPU v7x, 32 devices: a whole 2x2x4 slice. The times are simulated.
32 devices in a mesh: oct: 4 (over y, x), cube: 8 (over z, core).
Axes of the slice: x: 2, y: 2, z: 4, core: 2. Of those that a mesh axis runs over, the one named last changes fastest.
Arguments:
- charges: bfloat16 [8192, 128], P(('oct', 'cube')), may hold values from -6 to 6
- panel_counts: int32 [8192], P(('oct', 'cube')), may hold values from 32 to 128
- positions: float32 [3, 8192, 128], P(None, ('oct', 'cube')), may hold values from 0 to 2
- moment_map: bfloat16 [128, 128], replicated, may hold values from -0.5 to 0.5
- translations: bfloat16 [16, 128, 128], replicated, may hold values from -0.15625 to 0.15625
- evaluation: bfloat16 [128, 128], replicated, may hold values from -0.5 to 0.5
- near_boxes: int32 [8192, 4], P(('oct', 'cube')), may hold values from 0 to 255
- group_sources: int32 [8192, 8], P(('oct', 'cube')), may hold values from 0 to 2047
- group_patterns: int32 [8192, 8], P(('oct', 'cube')), may hold values from 0 to 15
- remote_sources: int32 [4, 8, 4, 64, 4], P('oct', 'cube'), may hold values from 0 to 255
- remote_patterns: int32 [4, 8, 4, 64, 4], P('oct', 'cube'), may hold values from 0 to 15
- remote_targets: int32 [4, 8, 4, 64], P('oct', 'cube'), may hold values from 0 to 255
Outputs:
- potential: float32 [8192, 128], P(('oct', 'cube'))
All inputs are finite; a program needn't handle non-finite values.
Results may differ from a plain program's by a relative error of at most 0.0024.
Values may be sent and summed in bfloat16 or wider, within the bound.
No kernel may reach another device: no remote copies, remote signals or barrier semaphores. Data moves between devices by JAX's collectives and lax.ppermute only.
A program may use at most 64 MiB of HBM per device.

v0:
```python
import math

import jax
import jax.numpy as jnp
from jax import lax
from jax.sharding import PartitionSpec as P


def pattern_sums(rows, patterns, count):
    onehot = (patterns[..., None] == jnp.arange(count, dtype=jnp.int32)).astype(jnp.bfloat16)
    summed = jnp.einsum("nkp,nkc->npc", onehot, rows, preferred_element_type=jnp.float32)
    return summed.astype(jnp.bfloat16).reshape(rows.shape[0], count * rows.shape[2])


def near_block(args):
    target_pos, source_pos, source_q = args
    diffs = target_pos[:, :, None, :, None] - source_pos[:, :, :, None, :]
    dist_sq = jnp.sum(diffs * diffs, axis=0) + 0.0025
    kernel = source_q[:, :, None, :] * lax.rsqrt(dist_sq)
    return jnp.sum(kernel, axis=(1, 3))


def body(
    charges,
    panel_counts,
    positions,
    moment_map,
    translations,
    evaluation,
    near_boxes,
    group_sources,
    group_patterns,
    remote_sources,
    remote_patterns,
    remote_targets,
):
    boxes = charges.shape[0]
    panels = charges.shape[1]
    width = moment_map.shape[1]
    operator_count = translations.shape[0]
    operators = translations.reshape(operator_count * width, width)
    slot_index = jnp.arange(panels, dtype=jnp.int32)
    live = slot_index[None, :] < panel_counts[:, None]
    strength = jnp.where(live, charges, jnp.zeros_like(charges))
    multipole = jnp.dot(strength, moment_map, preferred_element_type=jnp.float32).astype(
        jnp.bfloat16
    )
    group_all = lax.all_gather(multipole, "cube", axis=0, tiled=True)
    group_sum = pattern_sums(group_all[group_sources], group_patterns, operator_count)
    near_local = jnp.dot(group_sum, operators, preferred_element_type=jnp.float32)
    sources = remote_sources[0, 0]
    patterns = remote_patterns[0, 0]
    targets = remote_targets[0, 0]
    groups = sources.shape[0]
    slots = sources.shape[1]
    fanin = sources.shape[2]
    rows = multipole[sources.reshape(-1)].reshape(groups, slots, fanin, width)
    got_rows = lax.all_to_all(rows, "oct", split_axis=0, concat_axis=0, tiled=True)
    got_patterns = lax.all_to_all(patterns, "oct", split_axis=0, concat_axis=0, tiled=True)
    got_targets = lax.all_to_all(targets, "oct", split_axis=0, concat_axis=0, tiled=True)
    count = got_rows.shape[1]
    flat = pattern_sums(
        got_rows.reshape(-1, fanin, width), got_patterns.reshape(-1, fanin), operator_count
    )
    result = jnp.dot(flat, operators, preferred_element_type=jnp.float32)
    received, got_targets = (result.reshape(groups, count, width), got_targets)
    remote_local = jax.ops.segment_sum(
        received.reshape(-1, width), got_targets.reshape(-1), num_segments=boxes
    )
    local = (near_local + remote_local).astype(jnp.bfloat16)
    far = jnp.dot(local, evaluation, preferred_element_type=jnp.float32)
    block = min(boxes, 16)
    count = boxes // block
    strength_f = strength.astype(jnp.float32)
    target_pos = positions.reshape(3, count, block, panels).transpose(1, 0, 2, 3)
    flat_near = near_boxes.reshape(-1)
    knear = near_boxes.shape[1]
    source_pos = (
        positions[:, flat_near].reshape(3, count, block, knear, panels).transpose(1, 0, 2, 3, 4)
    )
    source_q = strength_f[flat_near].reshape(count, block, knear, panels)
    near = lax.map(near_block, (target_pos, source_pos, source_q)).reshape(boxes, panels)
    total = near * (1.0 / (4.0 * math.pi)) + far
    return jnp.where(live, total, jnp.zeros_like(total))


def solution(mesh):
    return jax.shard_map(
        body,
        mesh=mesh,
        in_specs=(
            P(("oct", "cube"), None),
            P(("oct", "cube")),
            P(None, ("oct", "cube"), None),
            P(),
            P(),
            P(),
            P(("oct", "cube"), None),
            P(("oct", "cube"), None),
            P(("oct", "cube"), None),
            P("oct", "cube", None, None, None),
            P("oct", "cube", None, None, None),
            P("oct", "cube", None, None),
        ),
        out_specs=P(("oct", "cube"), None),
        check_vma=False,
    )
```

profile of v0, /device:TPU:0, one launch (start us, length us, event | category | flops | bytes accessed | tf_op | source)
XLA Modules:
  0.0 128.6 jit_solution(18188685768193097701)
XLA Ops:
  0.0 5.3 %all-to-all-start = ((s32[4,1,64]{2,1,0:T(1,128)}), s32[4,1,64]{2,1,0:T(1,128)S(1)}, u32[]{:S(2)}, u32[]{:S(2)}) async-start(s32[4,1,64]{2,1,0:T(1,128)} %bitcast.64), calls=%async_computation | async-start | bytes 4096 | tf_op jit(solution)/shard_map/all_to_all | solution.py:60
  10.1 3.9 %gather_fusion.1 = f32[1024,3,128]{2,0,1:T(8,128)S(1)} fusion(f32[3,256,128]{2,1,0:T(8,128)S(1)} %copy-done.1, s32[1024]{0:T(1024)S(1)} %broadcast_clamp_fusion.2), kind=kCustom, calls=%fused_computation.1 | custom fusion | bytes 3149824 | tf_op jit(solution)/shard_map/gather | solution.py:79
  14.0 68.3 %while.10 = (s32[]{:T(128)}, f32[16,16,128]{2,1,0:T(8,128)S(1)}, f32[16,16,4,128]{3,2,1,0:T(4,128)S(1)}, f32[16,3,16,128]{3,2,0,1:T(8,128)S(1)}, f32[16,3,16,4,128]{4,3,2,0,1:T(4,128)S(1)}, /*index=5*/s32[]{:T(128)}) while((s32[]{:T(128)}, f32[16,16,128]{2,1,0:T(8,128)S(1)}, f32[16,16,4,128]{3,2,1,0:T(4,128)S(1)}, ...), condition=%wide.region_3.4_spmd, body=%wide.region_0.3_spmd.sunk | while | flops 11532290 | bytes 8880221 | solution.py:82
  14.1 3.5 %multiply_reduce_fusion.4 = f32[16,4,128,128]{3,2,1,0:T(8,128)S(1)} fusion(f32[3,16,4,128]{3,2,1,0:T(4,128)S(1)} %dynamic-slice_bitcast_fusion.6, f32[3,16,128]{2,1,0:T(8,128)S(1)} %dynamic-slice_bitcast_fusion.7), kind=kLoop, calls=%fused_computation.5.clone.1 | loop fusion | flops 8388608 | bytes 4317184 | tf_op jit(solution)/shard_map/while/body/eval_jaxpr/reduce_sum | solution.py:18
  18.3 3.5 %multiply_reduce_fusion.4 = f32[16,4,128,128]{3,2,1,0:T(8,128)S(1)} fusion(f32[3,16,4,128]{3,2,1,0:T(4,128)S(1)} %dynamic-slice_bitcast_fusion.6, f32[3,16,128]{2,1,0:T(8,128)S(1)} %dynamic-slice_bitcast_fusion.7), kind=kLoop, calls=%fused_computation.5.clone.1 | loop fusion | flops 8388608 | bytes 4317184 | tf_op jit(solution)/shard_map/while/body/eval_jaxpr/reduce_sum | solution.py:18
  22.6 3.5 %multiply_reduce_fusion.4 = f32[16,4,128,128]{3,2,1,0:T(8,128)S(1)} fusion(f32[3,16,4,128]{3,2,1,0:T(4,128)S(1)} %dynamic-slice_bitcast_fusion.6, f32[3,16,128]{2,1,0:T(8,128)S(1)} %dynamic-slice_bitcast_fusion.7), kind=kLoop, calls=%fused_computation.5.clone.1 | loop fusion | flops 8388608 | bytes 4317184 | tf_op jit(solution)/shard_map/while/body/eval_jaxpr/reduce_sum | solution.py:18
  26.9 3.5 %multiply_reduce_fusion.4 = f32[16,4,128,128]{3,2,1,0:T(8,128)S(1)} fusion(f32[3,16,4,128]{3,2,1,0:T(4,128)S(1)} %dynamic-slice_bitcast_fusion.6, f32[3,16,128]{2,1,0:T(8,128)S(1)} %dynamic-slice_bitcast_fusion.7), kind=kLoop, calls=%fused_computation.5.clone.1 | loop fusion | flops 8388608 | bytes 4317184 | tf_op jit(solution)/shard_map/while/body/eval_jaxpr/reduce_sum | solution.py:18
  31.2 3.5 %multiply_reduce_fusion.4 = f32[16,4,128,128]{3,2,1,0:T(8,128)S(1)} fusion(f32[3,16,4,128]{3,2,1,0:T(4,128)S(1)} %dynamic-slice_bitcast_fusion.6, f32[3,16,128]{2,1,0:T(8,128)S(1)} %dynamic-slice_bitcast_fusion.7), kind=kLoop, calls=%fused_computation.5.clone.1 | loop fusion | flops 8388608 | bytes 4317184 | tf_op jit(solution)/shard_map/while/body/eval_jaxpr/reduce_sum | solution.py:18
  35.4 3.5 %multiply_reduce_fusion.4 = f32[16,4,128,128]{3,2,1,0:T(8,128)S(1)} fusion(f32[3,16,4,128]{3,2,1,0:T(4,128)S(1)} %dynamic-slice_bitcast_fusion.6, f32[3,16,128]{2,1,0:T(8,128)S(1)} %dynamic-slice_bitcast_fusion.7), kind=kLoop, calls=%fused_computation.5.clone.1 | loop fusion | flops 8388608 | bytes 4317184 | tf_op jit(solution)/shard_map/while/body/eval_jaxpr/reduce_sum | solution.py:18
  39.7 3.5 %multiply_reduce_fusion.4 = f32[16,4,128,128]{3,2,1,0:T(8,128)S(1)} fusion(f32[3,16,4,128]{3,2,1,0:T(4,128)S(1)} %dynamic-slice_bitcast_fusion.6, f32[3,16,128]{2,1,0:T(8,128)S(1)} %dynamic-slice_bitcast_fusion.7), kind=kLoop, calls=%fused_computation.5.clone.1 | loop fusion | flops 8388608 | bytes 4317184 | tf_op jit(solution)/shard_map/while/body/eval_jaxpr/reduce_sum | solution.py:18
  44.0 3.5 %multiply_reduce_fusion.4 = f32[16,4,128,128]{3,2,1,0:T(8,128)S(1)} fusion(f32[3,16,4,128]{3,2,1,0:T(4,128)S(1)} %dynamic-slice_bitcast_fusion.6, f32[3,16,128]{2,1,0:T(8,128)S(1)} %dynamic-slice_bitcast_fusion.7), kind=kLoop, calls=%fused_computation.5.clone.1 | loop fusion | flops 8388608 | bytes 4317184 | tf_op jit(solution)/shard_map/while/body/eval_jaxpr/reduce_sum | solution.py:18
  48.2 3.5 %multiply_reduce_fusion.4 = f32[16,4,128,128]{3,2,1,0:T(8,128)S(1)} fusion(f32[3,16,4,128]{3,2,1,0:T(4,128)S(1)} %dynamic-slice_bitcast_fusion.6, f32[3,16,128]{2,1,0:T(8,128)S(1)} %dynamic-slice_bitcast_fusion.7), kind=kLoop, calls=%fused_computation.5.clone.1 | loop fusion | flops 8388608 | bytes 4317184 | tf_op jit(solution)/shard_map/while/body/eval_jaxpr/reduce_sum | solution.py:18
  52.5 3.5 %multiply_reduce_fusion.4 = f32[16,4,128,128]{3,2,1,0:T(8,128)S(1)} fusion(f32[3,16,4,128]{3,2,1,0:T(4,128)S(1)} %dynamic-slice_bitcast_fusion.6, f32[3,16,128]{2,1,0:T(8,128)S(1)} %dynamic-slice_bitcast_fusion.7), kind=kLoop, calls=%fused_computation.5.clone.1 | loop fusion | flops 8388608 | bytes 4317184 | tf_op jit(solution)/shard_map/while/body/eval_jaxpr/reduce_sum | solution.py:18
  56.8 3.5 %multiply_reduce_fusion.4 = f32[16,4,128,128]{3,2,1,0:T(8,128)S(1)} fusion(f32[3,16,4,128]{3,2,1,0:T(4,128)S(1)} %dynamic-slice_bitcast_fusion.6, f32[3,16,128]{2,1,0:T(8,128)S(1)} %dynamic-slice_bitcast_fusion.7), kind=kLoop, calls=%fused_computation.5.clone.1 | loop fusion | flops 8388608 | bytes 4317184 | tf_op jit(solution)/shard_map/while/body/eval_jaxpr/reduce_sum | solution.py:18
  61.0 3.5 %multiply_reduce_fusion.4 = f32[16,4,128,128]{3,2,1,0:T(8,128)S(1)} fusion(f32[3,16,4,128]{3,2,1,0:T(4,128)S(1)} %dynamic-slice_bitcast_fusion.6, f32[3,16,128]{2,1,0:T(8,128)S(1)} %dynamic-slice_bitcast_fusion.7), kind=kLoop, calls=%fused_computation.5.clone.1 | loop fusion | flops 8388608 | bytes 4317184 | tf_op jit(solution)/shard_map/while/body/eval_jaxpr/reduce_sum | solution.py:18
  65.3 3.5 %multiply_reduce_fusion.4 = f32[16,4,128,128]{3,2,1,0:T(8,128)S(1)} fusion(f32[3,16,4,128]{3,2,1,0:T(4,128)S(1)} %dynamic-slice_bitcast_fusion.6, f32[3,16,128]{2,1,0:T(8,128)S(1)} %dynamic-slice_bitcast_fusion.7), kind=kLoop, calls=%fused_computation.5.clone.1 | loop fusion | flops 8388608 | bytes 4317184 | tf_op jit(solution)/shard_map/while/body/eval_jaxpr/reduce_sum | solution.py:18
  69.6 3.5 %multiply_reduce_fusion.4 = f32[16,4,128,128]{3,2,1,0:T(8,128)S(1)} fusion(f32[3,16,4,128]{3,2,1,0:T(4,128)S(1)} %dynamic-slice_bitcast_fusion.6, f32[3,16,128]{2,1,0:T(8,128)S(1)} %dynamic-slice_bitcast_fusion.7), kind=kLoop, calls=%fused_computation.5.clone.1 | loop fusion | flops 8388608 | bytes 4317184 | tf_op jit(solution)/shard_map/while/body/eval_jaxpr/reduce_sum | solution.py:18
  73.8 3.5 %multiply_reduce_fusion.4 = f32[16,4,128,128]{3,2,1,0:T(8,128)S(1)} fusion(f32[3,16,4,128]{3,2,1,0:T(4,128)S(1)} %dynamic-slice_bitcast_fusion.6, f32[3,16,128]{2,1,0:T(8,128)S(1)} %dynamic-slice_bitcast_fusion.7), kind=kLoop, calls=%fused_computation.5.clone.1 | loop fusion | flops 8388608 | bytes 4317184 | tf_op jit(solution)/shard_map/while/body/eval_jaxpr/reduce_sum | solution.py:18
  78.1 3.5 %multiply_reduce_fusion.4 = f32[16,4,128,128]{3,2,1,0:T(8,128)S(1)} fusion(f32[3,16,4,128]{3,2,1,0:T(4,128)S(1)} %dynamic-slice_bitcast_fusion.6, f32[3,16,128]{2,1,0:T(8,128)S(1)} %dynamic-slice_bitcast_fusion.7), kind=kLoop, calls=%fused_computation.5.clone.1 | loop fusion | flops 8388608 | bytes 4317184 | tf_op jit(solution)/shard_map/while/body/eval_jaxpr/reduce_sum | solution.py:18
  82.6 15.1 %all_gather.3 = bf16[2048,128]{1,0:T(8,128)(2,1)S(1)} all-gather(bf16[256,128]{1,0:T(8,128)(2,1)S(1)} %convolution_convert_fusion.2), channel_id=1, replica_groups=mesh['oct'=4,'cube'=8] {'cube'}, dimensions={0}, use_global_device_ids=true | all-gather | bytes 589824 | tf_op jit(solution)/shard_map/all_gather | solution.py:48
  98.3 6.2 %gather_fusion.2 = bf16[2048,128]{1,0:T(8,128)(2,1)S(1)} fusion(bf16[2048,128]{1,0:T(8,128)(2,1)S(1)} %all_gather.3, s32[2048]{0:T(1024)S(1)} %broadcast_clamp_fusion), kind=kCustom, calls=%fused_computation.2 | custom fusion | bytes 1056768 | tf_op jit(solution)/shard_map/gather | solution.py:49
  106.3 4.2 %all-to-all-start.1 = ((s32[4,1,256]{2,1,0:T(1,128)}), s32[4,1,256]{2,1,0:T(1,128)S(1)}, u32[]{:S(2)}, u32[]{:S(2)}) async-start(s32[4,1,256]{2,1,0:T(1,128)} %reshape.153), calls=%async_computation.1 | async-start | bytes 8192 | tf_op jit(solution)/shard_map/all_to_all | solution.py:59
  110.5 4.3 %gather_fusion.3 = bf16[1024,128]{1,0:T(8,128)(2,1)} fusion(bf16[256,128]{1,0:T(8,128)(2,1)S(1)} %convolution_convert_fusion.2, s32[1024]{0:T(1024)S(1)} %broadcast_clamp_fusion.1), kind=kCustom, calls=%fused_computation.3 | custom fusion | bytes 528384 | tf_op jit(solution)/shard_map/gather | solution.py:57
  115.1 3.8 %all-to-all-start.2 = ((bf16[4,64,4,128]{3,2,1,0:T(4,128)(2,1)}), bf16[4,64,4,128]{3,2,1,0:T(4,128)(2,1)S(1)}, u32[]{:S(2)}, u32[]{:S(2)}) async-start(bf16[4,64,4,128]{3,2,1,0:T(4,128)(2,1)} %bitcast.18), calls=%async_computation.2 | async-start | bytes 524288 | tf_op jit(solution)/shard_map/all_to_all | solution.py:58
  (136 shorter events, 28.9 us)
Async XLA Ops:
  0.0 119.0 %copy-start = (bf16[16,128,128]{2,1,0:T(8,128)(2,1)S(1)}, bf16[16,128,128]{2,1,0:T(8,128)(2,1)}, u32[]{:S(2)}) copy-start(bf16[16,128,128]{2,1,0:T(8,128)(2,1)} %param.18) | copy-start | bytes 1572868
  0.0 10.1 %copy-start.1 = (f32[3,256,128]{2,1,0:T(8,128)S(1)}, f32[3,256,128]{2,1,0:T(8,128)}, u32[]{:S(2)}) copy-start(f32[3,256,128]{2,1,0:T(8,128)} %param.16) | copy-start | bytes 1179652
  0.0 106.3 %all-to-all-start = ((s32[4,1,64]{2,1,0:T(1,128)}), s32[4,1,64]{2,1,0:T(1,128)S(1)}, u32[]{:S(2)}, u32[]{:S(2)}) async-start(s32[4,1,64]{2,1,0:T(1,128)} %bitcast.64), calls=%async_computation | async-start | bytes 4096 | tf_op jit(solution)/shard_map/all_to_all | solution.py:60
  13.9 68.4 %copy-start.2 = (bf16[256,128]{1,0:T(8,128)(2,1)S(1)}, bf16[256,128]{1,0:T(8,128)(2,1)}, u32[]{:S(2)}) copy-start(bf16[256,128]{1,0:T(8,128)(2,1)} %param.14) | copy-start | bytes 196612
  14.0 68.4 %copy-start.8 = (s32[256]{0:T(256)S(1)}, s32[256]{0:T(256)}, u32[]{:S(2)}) copy-start(s32[256]{0:T(256)} %param.15) | copy-start | bytes 3076
  14.0 68.4 %copy-start.9 = (bf16[128,128]{1,0:T(8,128)(2,1)S(1)}, bf16[128,128]{1,0:T(8,128)(2,1)}, u32[]{:S(2)}) copy-start(bf16[128,128]{1,0:T(8,128)(2,1)} %param.17) | copy-start | bytes 98308
  14.0 83.7 %copy-start.6 = (s32[256,8]{0,1:T(8,128)S(1)}, s32[256,8]{0,1:T(8,128)}, u32[]{:S(2)}) copy-start(s32[256,8]{0,1:T(8,128)} %param.21) | copy-start | bytes 24580
  14.0 83.9 %copy-start.4 = (s32[256,8]{0,1:T(8,128)S(1)}, s32[256,8]{0,1:T(8,128)}, u32[]{:S(2)}) copy-start(s32[256,8]{0,1:T(8,128)} %param.22) | copy-start | bytes 24580
  14.0 84.0 %copy-start.5 = (s32[1,1,4,64,4]{3,4,2,1,0:T(4,128)S(1)}, s32[1,1,4,64,4]{3,4,2,1,0:T(4,128)}, u32[]{:S(2)}) copy-start(s32[1,1,4,64,4]{3,4,2,1,0:T(4,128)} %param.23) | copy-start | bytes 12292
  14.0 84.3 %copy-start.7 = (s32[1,1,4,64,4]{3,4,2,1,0:T(4,128)S(1)}, s32[1,1,4,64,4]{3,4,2,1,0:T(4,128)}, u32[]{:S(2)}) copy-start(s32[1,1,4,64,4]{3,4,2,1,0:T(4,128)} %param.24) | copy-start | bytes 12292
  106.3 8.9 %all-to-all-start.1 = ((s32[4,1,256]{2,1,0:T(1,128)}), s32[4,1,256]{2,1,0:T(1,128)S(1)}, u32[]{:S(2)}, u32[]{:S(2)}) async-start(s32[4,1,256]{2,1,0:T(1,128)} %reshape.153), calls=%async_computation.1 | async-start | bytes 8192 | tf_op jit(solution)/shard_map/all_to_all | solution.py:59
  115.1 9.2 %all-to-all-start.2 = ((bf16[4,64,4,128]{3,2,1,0:T(4,128)(2,1)}), bf16[4,64,4,128]{3,2,1,0:T(4,128)(2,1)S(1)}, u32[]{:S(2)}, u32[]{:S(2)}) async-start(bf16[4,64,4,128]{3,2,1,0:T(4,128)(2,1)} %bitcast.18), calls=%async_computation.2 | async-start | bytes 524288 | tf_op jit(solution)/shard_map/all_to_all | solution.py:58
  119.0 8.9 %copy-start.3 = (bf16[128,128]{1,0:T(8,128)(2,1)S(1)}, bf16[128,128]{1,0:T(8,128)(2,1)}, u32[]{:S(2)}) copy-start(bf16[128,128]{1,0:T(8,128)(2,1)} %param.19) | copy-start | bytes 98308
where the time goes:
time: 129 us
  other arithmetic  71.1 us (55%)
  local copies, waits for them, and re-layouts  21.4 us (17%)
  blocking collectives  15.1 us (12%)
  starting transfers between devices  13.3 us (10%)
  matrix products  3.98 us (3%)
  waiting for transfers between devices  2.67 us (2%)
    reduce_sum x16, other arithmetic, near_block(): dist_sq = jnp.sum(diffs * diffs, axis=0) + 0.0025  55.8 us
    all_gather x1, blocking collectives, body(): group_all = lax.all_gather(multipole, 'cube', axis=0, tiled=True)  15.1 us
    reduce_sum x16, other arithmetic, near_block(): return jnp.sum(kernel, axis=(1, 3))  10.9 us
    gather x1, local copies, waits for them, and re-layouts, body(): group_all[group_sources]  6.18 us
    all_to_all x1, starting transfers between devices, body(): lax.all_to_all(targets, 'oct', split_axis=0, concat_axis=0, tiled=True)  5.29 us
    gather x1, local copies, waits for them, and re-layouts, body(): rows = multipole[sources.reshape(-1)].reshape(groups, slots, fanin, width)  4.29 us
    all_to_all x1, starting transfers between devices, body(): lax.all_to_all(patterns, 'oct', split_axis=0, concat_axis=0, tiled=True)  4.19 us
    gather x1, local copies, waits for them, and re-layouts, body(): positions[:, flat_near].reshape(3, count, block, knear, panels)  3.87 us
  transfers between devices with their start and end apart: 3, of which 2 were waited for; matrix products, arithmetic and copies ran while one was open for 72% of the time, Pallas kernels for 0%

commit v1 on v0

v1 whole, which is shorter than its diff:
```python
import functools
import math

import jax
import jax.numpy as jnp
from jax import lax
from jax.experimental import pallas as pl
from jax.experimental.pallas import tpu as pltpu
from jax.sharding import PartitionSpec as P

F32 = jnp.float32
BF16 = jnp.bfloat16
LANES = 128
EPS = 0.0025


def iota(shape, dim):
    return lax.broadcasted_iota(jnp.int32, shape, dim)


def count_columns(cnt_ref, boxes):
    eye = iota((LANES, LANES), 0) == iota((LANES, LANES), 1)
    cols = [
        jnp.sum(jnp.where(eye, cnt_ref[i : i + 1, :], 0), axis=1, keepdims=True)
        for i in range(boxes // LANES)
    ]
    return jnp.concatenate(cols, axis=0)


def code_columns(codes):
    rows = codes.shape[0]
    padded = jnp.concatenate([codes, jnp.zeros((LANES - rows, LANES), codes.dtype)], axis=0)
    return padded.T


def onehot(local, width):
    lane = iota((LANES, LANES), 1)
    parts = [
        jnp.where(local == lane + LANES * i, 1.0, 0.0).astype(BF16) for i in range(width // LANES)
    ]
    return jnp.concatenate(parts, axis=1)


def pattern_matrix(pattern_row, targets, fanin, patterns):
    eye = iota((targets, LANES), 0) == iota((targets, LANES), 1) // fanin
    own = jnp.where(eye, jnp.broadcast_to(pattern_row, (targets, LANES)), -1)
    parts = [jnp.where(own == p, 1.0, 0.0).astype(BF16) for p in range(patterns)]
    return jnp.concatenate(parts, axis=0)


def dot(a, b):
    return jnp.dot(a, b, preferred_element_type=F32)


def slot_kernel(m_ref, code_ref, targets_ref, ops_ref, out_ref, sums):
    boxes = m_ref.shape[0]
    width = m_ref.shape[1]
    patterns = ops_ref.shape[0] // width
    groups, rows, _ = out_ref.shape
    slots = targets_ref.shape[1] // 2
    tiles = code_ref.shape[0]
    fanin = tiles * LANES // (groups * slots)
    per = LANES // fanin
    m = m_ref[...]
    for base in range(0, tiles, LANES):
        codes = code_ref[base : min(base + LANES, tiles), :]
        here = codes.shape[0]
        cols = code_columns(codes)
        for i in range(here):
            col = jnp.broadcast_to(cols[:, i : i + 1], (LANES, LANES))
            got = dot(onehot(lax.rem(col, boxes), boxes), m).astype(BF16)
            pat = pattern_matrix(codes[i : i + 1, :] // boxes, per, fanin, patterns)
            s = dot(pat, got).astype(BF16)
            for p in range(patterns):
                sums[(base + i) * per : (base + i + 1) * per, p * width : (p + 1) * width] = s[
                    p * per : (p + 1) * per
                ]
    result = dot(sums[...], ops_ref[...])
    hi = result.astype(BF16)
    lo = (result - hi.astype(F32)).astype(BF16)
    for d in range(groups):
        out_ref[d, 0:slots, :] = hi[d * slots : (d + 1) * slots]
        out_ref[d, slots : 2 * slots, :] = lo[d * slots : (d + 1) * slots]
        out_ref[d, 2 * slots : rows, :] = jnp.broadcast_to(
            targets_ref[d : d + 1, :].astype(F32), (rows - 2 * slots, 2 * slots)
        ).astype(BF16)


def near_kernel(nb_ref, cnt_ref, chg_ref, pos_ref, out_ref, feat, left, qcol):
    boxes = chg_ref.shape[0]
    knear = nb_ref.shape[0]
    live = iota((boxes, LANES), 1) < count_columns(cnt_ref, boxes)
    feat[7] = jnp.where(live, chg_ref[...].astype(F32), 0.0)
    norm = jnp.zeros((boxes, LANES), F32)
    for c in range(3):
        u = pos_ref[c] - 1.0
        h = u.astype(BF16).astype(F32)
        m = (u - h).astype(BF16).astype(F32)
        feat[2 * c] = h
        feat[2 * c + 1] = m
        v = h + m
        norm = norm + v * v
    feat[6] = norm

    masks = [
        jnp.where(iota((LANES, LANES), 1) % 8 == j, 1.0, 0.0).astype(BF16) for j in range(8)
    ]

    def build(g, carry):
        rows = pl.ds(pl.multiple_of(g * 8, 8), 8)
        parts = []
        for c in range(3):
            h = -2.0 * feat[2 * c, rows, :]
            m = -2.0 * feat[2 * c + 1, rows, :]
            parts += [h, h, m, m]
        n = feat[6, rows, :]
        n1 = n.astype(BF16).astype(F32)
        n2 = (n - n1).astype(BF16).astype(F32)
        parts += [n1, n2, n - n1 - n2, feat[7, rows, :]]
        turned = jnp.concatenate(parts, axis=0).T
        packed = turned.astype(BF16)
        for j in range(8):
            left[g * 8 + j] = packed * masks[j]
            qcol[g * 8 + j] = jnp.broadcast_to(
                turned[:, 120 + j : 121 + j], (LANES, LANES)
            )
        return carry

    lax.fori_loop(0, boxes // 8, build, 0)

    zero = jnp.zeros((LANES, LANES), BF16)
    one8 = jnp.ones((24, LANES), F32)
    zero8 = jnp.zeros((8, LANES), F32)

    def weights(tile, r):
        parts = []
        for c in range(3):
            h = jnp.broadcast_to(tile[2 * c][r : r + 1], (8, LANES))
            m = jnp.broadcast_to(tile[2 * c + 1][r : r + 1], (8, LANES))
            parts += [h, m, h, m]
        return jnp.concatenate(parts + [one8, zero8], axis=0).astype(BF16)

    def group(g, carry):
        rows = pl.ds(pl.multiple_of(g * 8, 8), 8)
        tile = [feat[f, rows, :] for f in range(7)]
        shift = tile[6] + EPS
        outs = []
        for pair in range(4):
            pick = [2 * pair, 2 * pair + 1]
            w1, w2 = [weights(tile, r) for r in pick]
            right = jnp.concatenate(
                [jnp.concatenate([w1, zero], axis=1), jnp.concatenate([zero, w2], axis=1)], axis=0
            )
            near = [[nb_ref[k, g * 8 + r] for k in range(knear)] for r in pick]
            lhs = jnp.concatenate(
                [
                    jnp.concatenate([left[near[0][k]], left[near[1][k]]], axis=1)
                    for k in range(knear)
                ],
                axis=0,
            )
            dist = dot(lhs, right)
            for side in range(2):
                row = shift[pick[side] : pick[side] + 1]
                inv = lax.rsqrt(dist[:, side * LANES : (side + 1) * LANES] + row)
                acc = inv[0:LANES] * qcol[near[side][0]]
                for k in range(1, knear):
                    acc = acc + inv[k * LANES : (k + 1) * LANES] * qcol[near[side][k]]
                outs.append(jnp.sum(acc, axis=0, keepdims=True))
        out_ref[rows, :] = jnp.concatenate(outs, axis=0)
        return carry

    lax.fori_loop(0, boxes // 8, group, 0)


def far_kernel(*refs, blocks, groups, fanin):
    code_ref, cnt_ref, near_ref, ops_ref, eval_ref = refs[:5]
    m_refs = refs[5 : 5 + blocks]
    pay_refs = refs[5 + blocks : 5 + blocks + groups]
    out_ref, sums = refs[5 + blocks + groups :]
    boxes, width = m_refs[0].shape
    patterns = ops_ref.shape[0] // width
    per = LANES // fanin
    tiles = code_ref.shape[0]
    span = 2 * boxes
    pages = blocks // 2
    table = jnp.concatenate(
        [
            jnp.concatenate([m_refs[2 * j][...], m_refs[2 * j + 1][...]], axis=0)
            for j in range(pages)
        ],
        axis=1,
    )
    codes = code_ref[...]
    cols = code_columns(codes)
    for i in range(tiles):
        col = jnp.broadcast_to(cols[:, i : i + 1], (LANES, LANES))
        wide = dot(onehot(col & (span - 1), span), table)
        page = (col // span) & (pages - 1)
        got = wide[:, 0:width]
        for j in range(1, pages):
            got = jnp.where(page == j, wide[:, j * width : (j + 1) * width], got)
        pat = pattern_matrix(codes[i : i + 1, :] // (blocks * boxes), per, fanin, patterns)
        s = dot(pat, got.astype(BF16)).astype(BF16)
        for p in range(patterns):
            sums[i * per : (i + 1) * per, p * width : (p + 1) * width] = s[
                p * per : (p + 1) * per
            ]
    local = dot(sums[...], ops_ref[...])
    hits = []
    values = []
    for pay in pay_refs:
        depth = pay.shape[0] - 16
        target = pay[depth : depth + 16, :].astype(F32)[0:1]
        box = iota((boxes, depth), 0).astype(F32)
        hits.append(jnp.where(box == target, 1.0, 0.0).astype(BF16))
        values.append(pay[0:depth, :])
    local = local + dot(jnp.concatenate(hits, axis=1), jnp.concatenate(values, axis=0))
    far = dot(local.astype(BF16), eval_ref[...])
    total = near_ref[...] * (1.0 / (4.0 * math.pi)) + far
    live = iota((boxes, LANES), 1) < count_columns(cnt_ref, boxes)
    out_ref[...] = jnp.where(live, total, 0.0)


VMEM = pl.BlockSpec(memory_space=pltpu.VMEM)
SMEM = pl.BlockSpec(memory_space=pltpu.SMEM)
MIB = 1024 * 1024


def body(
    n_oct,
    n_cube,
    charges,
    panel_counts,
    positions,
    moment_map,
    translations,
    evaluation,
    near_boxes,
    group_sources,
    group_patterns,
    remote_sources,
    remote_patterns,
    remote_targets,
):
    boxes, panels = charges.shape
    width = moment_map.shape[1]
    patterns = translations.shape[0]
    operators = translations.reshape(patterns * width, width)
    counts = panel_counts.reshape(boxes // LANES, LANES)
    slot_index = jnp.arange(panels, dtype=jnp.int32)
    live = slot_index[None, :] < panel_counts[:, None]
    strength = jnp.where(live, charges, jnp.zeros_like(charges))
    multipole = jnp.dot(strength, moment_map, preferred_element_type=F32).astype(BF16)

    me = lax.axis_index("cube")
    blocks = [multipole] + [
        lax.ppermute(multipole, "cube", [(i, i ^ k) for i in range(n_cube)])
        for k in range(1, n_cube)
    ]

    slots, fanin = remote_sources.shape[3:]
    slot_code = (remote_sources[0, 0] + boxes * remote_patterns[0, 0]).reshape(-1, LANES)
    targets = jnp.concatenate([remote_targets[0, 0]] * 2, axis=1)
    sent = pl.pallas_call(
        slot_kernel,
        out_shape=jax.ShapeDtypeStruct((n_oct, 2 * slots + 16, width), BF16),
        in_specs=[VMEM] * 4,
        out_specs=VMEM,
        scratch_shapes=[pltpu.VMEM((n_oct * slots, patterns * width), BF16)],
        compiler_params=pltpu.CompilerParams(vmem_limit_bytes=16 * MIB),
        cost_estimate=pl.CostEstimate(
            flops=1_000_000_000, bytes_accessed=1_000_000, transcendentals=0
        ),
        name="slots",
    )(multipole, slot_code, targets, operators)
    mine = lax.axis_index("oct")
    payloads = []
    for k in range(n_oct):
        part = lax.dynamic_index_in_dim(sent, mine ^ k, 0, keepdims=False)
        if k > 0:
            part = lax.ppermute(part, "oct", [(i, i ^ k) for i in range(n_oct)])
        payloads.append(part)

    near = pl.pallas_call(
        near_kernel,
        out_shape=jax.ShapeDtypeStruct((boxes, panels), F32),
        in_specs=[SMEM, VMEM, VMEM, VMEM],
        out_specs=VMEM,
        scratch_shapes=[
            pltpu.VMEM((8, boxes, panels), F32),
            pltpu.VMEM((boxes, panels, LANES), BF16),
            pltpu.VMEM((boxes, panels, LANES), F32),
        ],
        compiler_params=pltpu.CompilerParams(vmem_limit_bytes=48 * MIB),
        cost_estimate=pl.CostEstimate(
            flops=15_000_000_000, bytes_accessed=1_000_000, transcendentals=16_000_000
        ),
        name="near",
    )(near_boxes.T, counts, charges, positions)

    klist = group_sources.shape[1]
    group = n_cube * boxes
    code = (group_sources ^ (me * boxes)) + group * group_patterns
    return pl.pallas_call(
        functools.partial(far_kernel, blocks=n_cube, groups=n_oct, fanin=klist),
        out_shape=jax.ShapeDtypeStruct((boxes, panels), F32),
        in_specs=[VMEM] * (5 + n_cube + n_oct),
        out_specs=VMEM,
        scratch_shapes=[pltpu.VMEM((boxes, patterns * width), BF16)],
        compiler_params=pltpu.CompilerParams(vmem_limit_bytes=24 * MIB),
        cost_estimate=pl.CostEstimate(
            flops=3_000_000_000, bytes_accessed=2_000_000, transcendentals=0
        ),
        name="far",
    )(code.reshape(-1, LANES), counts, near, operators, evaluation, *blocks, *payloads)


def solution(mesh):
    n_oct = mesh.shape["oct"]
    n_cube = mesh.shape["cube"]

    def run(*arrays):
        return body(n_oct, n_cube, *arrays)

    return jax.shard_map(
        run,
        mesh=mesh,
        in_specs=(
            P(("oct", "cube"), None),
            P(("oct", "cube")),
            P(None, ("oct", "cube"), None),
            P(),
            P(),
            P(),
            P(("oct", "cube"), None),
            P(("oct", "cube"), None),
            P(("oct", "cube"), None),
            P("oct", "cube", None, None, None),
            P("oct", "cube", None, None, None),
            P("oct", "cube", None, None),
        ),
        out_specs=P(("oct", "cube"), None),
        check_vma=False,
    )
```

time: 129 us -> 59.2 us (0.46)
  the two profiles are of different devices: /device:TPU:0 before, /device:TPU:19 now
where the time goes in v1:
time: 59.2 us; the launch traced here: 58.9 us
  Pallas kernels  33.9 us (57%)
  starting transfers between devices  10.5 us (18%)
  waiting for transfers between devices  9.85 us (17%)
  local copies, waits for them, and re-layouts  1.95 us (3%)
  other arithmetic  1.56 us (3%)
  matrix products  1.06 us (2%)
    pallas_call x1, Pallas kernels, body(): pl.pallas_call(near_kernel, out_shape=jax.ShapeDtypeStruct((boxes, panels...  27.2 us
    ppermute x7, waiting for transfers between devices, body(): lax.ppermute(multipole, 'cube', [(i, i ^ k) for i in range(n_cube)])  9.85 us
    ppermute x7, starting transfers between devices, body(): lax.ppermute(multipole, 'cube', [(i, i ^ k) for i in range(n_cube)])  7.77 us
    pallas_call x1, Pallas kernels, body(): pl.pallas_call(functools.partial(far_kernel, blocks=n_cube, groups=n_oct,...  5.16 us
    ppermute x3, starting transfers between devices, body(): part = lax.ppermute(part, 'oct', [(i, i ^ k) for i in range(n_oct)])  2.71 us
    pallas_call x1, Pallas kernels, body(): pl.pallas_call(slot_kernel, out_shape=jax.ShapeDtypeStruct((n_oct, 2 * sl...  1.54 us
    unnamed x18, local copies, waits for them, and re-layouts  1.46 us
  transfers between devices with their start and end apart: 10, of which 3 were waited for; matrix products, arithmetic and copies ran while one was open for 3% of the time, Pallas kernels for 49%

profile of v1, /device:TPU:19, one launch (start us, length us, event | category | flops | bytes accessed | tf_op | source)
XLA Modules:
  0.0 58.9 jit_solution(218615060269477438)
XLA Ops:
  0.0 0.8 %copy-done = bf16[128,128]{1,0:T(8,128)(2,1)S(1)} copy-done((bf16[128,128]{1,0:T(8,128)(2,1)S(1)}, bf16[128,128]{1,0:T(8,128)(2,1)}, u32[]{:S(2)}) %copy-start) | copy-done | bytes 32792
  0.8 1.1 %convolution_convert_fusion.m_ref.refs_5_ = bf16[256,128]{1,0:T(8,128)(2,1)S(1)} fusion(bf16[128,128]{1,0:T(8,128)(2,1)S(1)} %copy-done, bf16[256,128]{1,0:T(8,128)(2,1)} %chg_ref.1, s32[256]{0:T(256)} %param.13), kind=kOutput, calls=%fused_computation | convolution fusion | flops 8486912 | bytes 164864 | tf_op jit(solution)/shard_map/dot_general | solution.py:254
  1.8 0.7 %collective-permute-start = (bf16[256,128]{1,0:T(8,128)(2,1)S(1)}, bf16[256,128]{1,0:T(8,128)(2,1)S(1)}, u32[]{:S(2)}, u32[]{:S(2)}) collective-permute-start(bf16[256,128]{1,0:T(8,128)(2,1)S(1)} %convolution_convert_fusion.m_ref.refs_5_), channel_id=1, source_target_pairs={{0,1},{1,0},{2,3},{3,2},{4,5},{5,4},{6,7},{7,6},{8,9},{9,8},{10,11... | collective-permute-start | bytes 196616 | tf_op jit(solution)/shard_map/ppermute | solution.py:258
  2.6 1.3 %collective-permute-start.1 = (bf16[256,128]{1,0:T(8,128)(2,1)S(1)}, bf16[256,128]{1,0:T(8,128)(2,1)S(1)}, u32[]{:S(2)}, u32[]{:S(2)}) collective-permute-start(bf16[256,128]{1,0:T(8,128)(2,1)S(1)} %convolution_convert_fusion.m_ref.refs_5_), channel_id=1, source_target_pairs={{0,2},{1,3},{2,0},{3,1},{4,6},{5,7},{6,4},{7,5},{8,10},{9,11},{10,... | collective-permute-start | bytes 196616 | tf_op jit(solution)/shard_map/ppermute | solution.py:258
  3.9 0.7 %multiply_add_fusion = s32[1,1,4,64,4]{3,4,2,1,0:T(4,128)S(1)} fusion(s32[1,1,4,64,4]{3,4,2,1,0:T(4,128)} %param.21, s32[1,1,4,64,4]{3,4,2,1,0:T(4,128)} %param.22), kind=kLoop, calls=%fused_computation.9 | loop fusion | flops 2048 | bytes 12288 | tf_op jit(solution)/shard_map/add | solution.py:263
  4.6 0.1 copy.16
  4.7 0.1 add.25.code_ref
  4.8 0.8 %pad_add_fusion.targets_ref = s32[4,128]{1,0:T(4,128)S(1)} fusion(s32[4,64]{1,0:T(4,128)} %bitcast.20), kind=kLoop, calls=%fused_computation.11 | loop fusion | flops 512 | bytes 3072 | tf_op jit(solution)/shard_map/concatenate | solution.py:264
  5.7 1.5 %slots.1 = bf16[4,144,128]{2,1,0:T(8,128)(2,1)S(1)} custom-call(bf16[256,128]{1,0:T(8,128)(2,1)S(1)} %convolution_convert_fusion.m_ref.refs_5_, s32[8,128]{1,0:T(8,128)S(1)} %add.25.code_ref, s32[4,128]{1,0:T(4,128)S(1)} %pad_add_fusion.targets_ref, bf16[2048,128]{1,0:T(8,128)(2,1)S(1)} %bitcast.15), custom_call_target="tpu_custom_call" | custom-call | flops 1000000000 | bytes 1000000 | tf_op jit(solution)/shard_map/slots/pallas_call | solution.py:265
  7.3 0.3 collective-permute-start.7
  7.6 1.2 %collective-permute-start.8 = (bf16[144,128]{1,0:T(8,128)(2,1)S(1)}, bf16[144,128]{1,0:T(8,128)(2,1)S(1)}, u32[]{:S(2)}, u32[]{:S(2)}) collective-permute-start(bf16[144,128]{1,0:T(8,128)(2,1)S(1)} %get-tuple-element.6), channel_id=1, source_target_pairs={{0,16},{8,24},{16,0},{24,8},{1,17},{9,25},{17,1},{25,9},{2,18},{10... | collective-permute-start | bytes 110600 | tf_op jit(solution)/shard_map/ppermute | solution.py:282
  8.8 1.2 %collective-permute-start.9 = (bf16[144,128]{1,0:T(8,128)(2,1)S(1)}, bf16[144,128]{1,0:T(8,128)(2,1)S(1)}, u32[]{:S(2)}, u32[]{:S(2)}) collective-permute-start(bf16[144,128]{1,0:T(8,128)(2,1)S(1)} %get-tuple-element.5), channel_id=1, source_target_pairs={{0,24},{8,16},{16,8},{24,0},{1,25},{9,17},{17,9},{25,1},{2,26},{10... | collective-permute-start | bytes 110600 | tf_op jit(solution)/shard_map/ppermute | solution.py:282
  10.0 0.7 %copy-done.6 = s32[256]{0:T(256)S(1)} copy-done((s32[256]{0:T(256)S(1)}, s32[256]{0:T(256)}, u32[]{:S(2)}) %copy-start.6) | copy-done | bytes 1048
  10.7 27.2 %near.1.refs_2_ = f32[256,128]{1,0:T(8,128)S(1)} custom-call(s32[4,256]{1,0:T(4,128)S(1)} %bitcast.17, s32[2,128]{1,0:T(2,128)S(1)} %bitcast.18, bf16[256,128]{1,0:T(8,128)(2,1)S(1)} %copy-done.3, f32[3,256,128]{2,1,0:T(8,128)S(1)} %copy-done.2), custom_call_target="tpu_custom_call" | custom-call | flops 15000000512 | bytes 1000000 | tf_op jit(solution)/shard_map/near/pallas_call | solution.py:285
  37.9 1.3 %collective-permute-start.2 = (bf16[256,128]{1,0:T(8,128)(2,1)S(1)}, bf16[256,128]{1,0:T(8,128)(2,1)S(1)}, u32[]{:S(2)}, u32[]{:S(2)}) collective-permute-start(bf16[256,128]{1,0:T(8,128)(2,1)S(1)} %convolution_convert_fusion.m_ref.refs_5_), channel_id=1, source_target_pairs={{0,3},{1,2},{2,1},{3,0},{4,7},{5,6},{6,5},{7,4},{8,11},{9,10},{10,... | collective-permute-start | bytes 196616 | tf_op jit(solution)/shard_map/ppermute | solution.py:258
  39.2 0.1 collective-permute-start.3
  39.2 2.5 %collective-permute-start.4 = (bf16[256,128]{1,0:T(8,128)(2,1)S(1)}, bf16[256,128]{1,0:T(8,128)(2,1)S(1)}, u32[]{:S(2)}, u32[]{:S(2)}) collective-permute-start(bf16[256,128]{1,0:T(8,128)(2,1)S(1)} %convolution_convert_fusion.m_ref.refs_5_), channel_id=1, source_target_pairs={{0,5},{1,4},{2,7},{3,6},{4,1},{5,0},{6,3},{7,2},{8,13},{9,12},{10,... | collective-permute-start | bytes 196616 | tf_op jit(solution)/shard_map/ppermute | solution.py:258
  41.8 1.8 %collective-permute-start.6 = (bf16[256,128]{1,0:T(8,128)(2,1)S(1)}, bf16[256,128]{1,0:T(8,128)(2,1)S(1)}, u32[]{:S(2)}, u32[]{:S(2)}) collective-permute-start(bf16[256,128]{1,0:T(8,128)(2,1)S(1)} %convolution_convert_fusion.m_ref.refs_5_), channel_id=1, source_target_pairs={{0,7},{1,6},{2,5},{3,4},{4,3},{5,2},{6,1},{7,0},{8,15},{9,14},{10,... | collective-permute-start | bytes 196616 | tf_op jit(solution)/shard_map/ppermute | solution.py:258
  43.6 0.1 copy.15
  43.8 0.1 reshape.16.refs_0_
  43.9 4.6 %collective-permute-done.4.refs_10_ = bf16[256,128]{1,0:T(8,128)(2,1)S(1)} collective-permute-done((bf16[256,128]{1,0:T(8,128)(2,1)S(1)}, bf16[256,128]{1,0:T(8,128)(2,1)S(1)}, u32[]{:S(2)}, u32[]{:S(2)}) %collective-permute-start.4) | collective-permute-done | bytes 65568 | tf_op jit(solution)/shard_map/ppermute | solution.py:258
  48.5 4.0 %collective-permute-done.5.refs_11_ = bf16[256,128]{1,0:T(8,128)(2,1)S(1)} collective-permute-done((bf16[256,128]{1,0:T(8,128)(2,1)S(1)}, bf16[256,128]{1,0:T(8,128)(2,1)S(1)}, u32[]{:S(2)}, u32[]{:S(2)}) %collective-permute-start.5) | collective-permute-done | bytes 65568 | tf_op jit(solution)/shard_map/ppermute | solution.py:258
  52.4 1.3 %collective-permute-done.6.refs_12_ = bf16[256,128]{1,0:T(8,128)(2,1)S(1)} collective-permute-done((bf16[256,128]{1,0:T(8,128)(2,1)S(1)}, bf16[256,128]{1,0:T(8,128)(2,1)S(1)}, u32[]{:S(2)}, u32[]{:S(2)}) %collective-permute-start.6) | collective-permute-done | bytes 65568 | tf_op jit(solution)/shard_map/ppermute | solution.py:258
  53.7 5.2 %far.1 = f32[256,128]{1,0:T(8,128)} custom-call(s32[16,128]{1,0:T(8,128)S(1)} %reshape.16.refs_0_, s32[2,128]{1,0:T(2,128)S(1)} %bitcast.19, f32[256,128]{1,0:T(8,128)S(1)} %near.1.refs_2_, bf16[2048,128]{1,0:T(8,128)(2,1)S(1)} %bitcast.16, bf16[128,128]{1,0:T(8,128)(2,1)S(1)} %copy-done.4, bf16[256,128]{1,0:T(8,128)(2,1)S(1)} %convolution_convert_fusion.m_ref.refs_5_, ...), custom_call_target="tpu_custom_call" | custom-call | flops 3000000000 | bytes 2000000 | tf_op jit(solution)/shard_map/far/pallas_call | solution.py:305
  (26 shorter events, 0.1 us)
Async XLA Ops:
  0.0 0.8 %copy-start = (bf16[128,128]{1,0:T(8,128)(2,1)S(1)}, bf16[128,128]{1,0:T(8,128)(2,1)}, u32[]{:S(2)}) copy-start(bf16[128,128]{1,0:T(8,128)(2,1)} %param.15) | copy-start | bytes 98308
  0.0 5.7 %copy-start.1 = (bf16[16,128,128]{2,1,0:T(8,128)(2,1)S(1)}, bf16[16,128,128]{2,1,0:T(8,128)(2,1)}, u32[]{:S(2)}) copy-start(bf16[16,128,128]{2,1,0:T(8,128)(2,1)} %param.16) | copy-start | bytes 1572868
  1.8 39.9 %collective-permute-start = (bf16[256,128]{1,0:T(8,128)(2,1)S(1)}, bf16[256,128]{1,0:T(8,128)(2,1)S(1)}, u32[]{:S(2)}, u32[]{:S(2)}) collective-permute-start(bf16[256,128]{1,0:T(8,128)(2,1)S(1)} %convolution_convert_fusion.m_ref.refs_5_), channel_id=1, source_target_pairs={{0,1},{1,0},{2,3},{3,2},{4,5},{5,4},{6,7},{7,6},{8,9},{9,8},{10,11... | collective-permute-start | bytes 196616 | tf_op jit(solution)/shard_map/ppermute | solution.py:258
  2.6 39.2 %collective-permute-start.1 = (bf16[256,128]{1,0:T(8,128)(2,1)S(1)}, bf16[256,128]{1,0:T(8,128)(2,1)S(1)}, u32[]{:S(2)}, u32[]{:S(2)}) collective-permute-start(bf16[256,128]{1,0:T(8,128)(2,1)S(1)} %convolution_convert_fusion.m_ref.refs_5_), channel_id=1, source_target_pairs={{0,2},{1,3},{2,0},{3,1},{4,6},{5,7},{6,4},{7,5},{8,10},{9,11},{10,... | collective-permute-start | bytes 196616 | tf_op jit(solution)/shard_map/ppermute | solution.py:258
  5.7 4.3 %copy-start.2 = (f32[3,256,128]{2,1,0:T(8,128)S(1)}, f32[3,256,128]{2,1,0:T(8,128)}, u32[]{:S(2)}) copy-start(f32[3,256,128]{2,1,0:T(8,128)} %pos_ref.1) | copy-start | bytes 1179652
  7.2 2.8 %copy-start.3 = (bf16[256,128]{1,0:T(8,128)(2,1)S(1)}, bf16[256,128]{1,0:T(8,128)(2,1)}, u32[]{:S(2)}) copy-start(bf16[256,128]{1,0:T(8,128)(2,1)} %chg_ref.1) | copy-start | bytes 196612
  7.3 2.7 %copy-start.5 = (s32[256,4]{0,1:T(4,128)S(1)}, s32[256,4]{0,1:T(4,128)}, u32[]{:S(2)}) copy-start(s32[256,4]{0,1:T(4,128)} %param.18) | copy-start | bytes 12292
  7.3 30.6 %collective-permute-start.7 = (bf16[144,128]{1,0:T(8,128)(2,1)S(1)}, bf16[144,128]{1,0:T(8,128)(2,1)S(1)}, u32[]{:S(2)}, u32[]{:S(2)}) collective-permute-start(bf16[144,128]{1,0:T(8,128)(2,1)S(1)} %get-tuple-element.7), channel_id=1, source_target_pairs={{0,8},{8,0},{16,24},{24,16},{1,9},{9,1},{17,25},{25,17},{2,10},{10... | collective-permute-start | bytes 110600 | tf_op jit(solution)/shard_map/ppermute | solution.py:282
  7.6 31.6 %collective-permute-start.8 = (bf16[144,128]{1,0:T(8,128)(2,1)S(1)}, bf16[144,128]{1,0:T(8,128)(2,1)S(1)}, u32[]{:S(2)}, u32[]{:S(2)}) collective-permute-start(bf16[144,128]{1,0:T(8,128)(2,1)S(1)} %get-tuple-element.6), channel_id=1, source_target_pairs={{0,16},{8,24},{16,0},{24,8},{1,17},{9,25},{17,1},{25,9},{2,18},{10... | collective-permute-start | bytes 110600 | tf_op jit(solution)/shard_map/ppermute | solution.py:282
  8.8 30.4 %collective-permute-start.9 = (bf16[144,128]{1,0:T(8,128)(2,1)S(1)}, bf16[144,128]{1,0:T(8,128)(2,1)S(1)}, u32[]{:S(2)}, u32[]{:S(2)}) collective-permute-start(bf16[144,128]{1,0:T(8,128)(2,1)S(1)} %get-tuple-element.5), channel_id=1, source_target_pairs={{0,24},{8,16},{16,8},{24,0},{1,25},{9,17},{17,9},{25,1},{2,26},{10... | collective-permute-start | bytes 110600 | tf_op jit(solution)/shard_map/ppermute | solution.py:282
  10.0 0.7 %copy-start.6 = (s32[256]{0:T(256)S(1)}, s32[256]{0:T(256)}, u32[]{:S(2)}) copy-start(s32[256]{0:T(256)} %param.13) | copy-start | bytes 3076
  10.7 32.9 %copy-start.7 = (s32[256,8]{0,1:T(8,128)S(1)}, s32[256,8]{0,1:T(8,128)}, u32[]{:S(2)}) copy-start(s32[256,8]{0,1:T(8,128)} %param.20) | copy-start | bytes 24580
  10.7 32.9 %copy-start.8 = (s32[256,8]{0,1:T(8,128)S(1)}, s32[256,8]{0,1:T(8,128)}, u32[]{:S(2)}) copy-start(s32[256,8]{0,1:T(8,128)} %param.19) | copy-start | bytes 24580
  37.9 6.0 %collective-permute-start.2 = (bf16[256,128]{1,0:T(8,128)(2,1)S(1)}, bf16[256,128]{1,0:T(8,128)(2,1)S(1)}, u32[]{:S(2)}, u32[]{:S(2)}) collective-permute-start(bf16[256,128]{1,0:T(8,128)(2,1)S(1)} %convolution_convert_fusion.m_ref.refs_5_), channel_id=1, source_target_pairs={{0,3},{1,2},{2,1},{3,0},{4,7},{5,6},{6,5},{7,4},{8,11},{9,10},{10,... | collective-permute-start | bytes 196616 | tf_op jit(solution)/shard_map/ppermute | solution.py:258
  39.2 4.7 %collective-permute-start.3 = (bf16[256,128]{1,0:T(8,128)(2,1)S(1)}, bf16[256,128]{1,0:T(8,128)(2,1)S(1)}, u32[]{:S(2)}, u32[]{:S(2)}) collective-permute-start(bf16[256,128]{1,0:T(8,128)(2,1)S(1)} %convolution_convert_fusion.m_ref.refs_5_), channel_id=1, source_target_pairs={{0,4},{1,5},{2,6},{3,7},{4,0},{5,1},{6,2},{7,3},{8,12},{9,13},{10,... | collective-permute-start | bytes 196616 | tf_op jit(solution)/shard_map/ppermute | solution.py:258
  39.2 9.2 %collective-permute-start.4 = (bf16[256,128]{1,0:T(8,128)(2,1)S(1)}, bf16[256,128]{1,0:T(8,128)(2,1)S(1)}, u32[]{:S(2)}, u32[]{:S(2)}) collective-permute-start(bf16[256,128]{1,0:T(8,128)(2,1)S(1)} %convolution_convert_fusion.m_ref.refs_5_), channel_id=1, source_target_pairs={{0,5},{1,4},{2,7},{3,6},{4,1},{5,0},{6,3},{7,2},{8,13},{9,12},{10,... | collective-permute-start | bytes 196616 | tf_op jit(solution)/shard_map/ppermute | solution.py:258
  41.7 10.7 %collective-permute-start.5 = (bf16[256,128]{1,0:T(8,128)(2,1)S(1)}, bf16[256,128]{1,0:T(8,128)(2,1)S(1)}, u32[]{:S(2)}, u32[]{:S(2)}) collective-permute-start(bf16[256,128]{1,0:T(8,128)(2,1)S(1)} %convolution_convert_fusion.m_ref.refs_5_), channel_id=1, source_target_pairs={{0,6},{1,7},{2,4},{3,5},{4,2},{5,3},{6,0},{7,1},{8,14},{9,15},{10,... | collective-permute-start | bytes 196616 | tf_op jit(solution)/shard_map/ppermute | solution.py:258
  41.8 12.0 %collective-permute-start.6 = (bf16[256,128]{1,0:T(8,128)(2,1)S(1)}, bf16[256,128]{1,0:T(8,128)(2,1)S(1)}, u32[]{:S(2)}, u32[]{:S(2)}) collective-permute-start(bf16[256,128]{1,0:T(8,128)(2,1)S(1)} %convolution_convert_fusion.m_ref.refs_5_), channel_id=1, source_target_pairs={{0,7},{1,6},{2,5},{3,4},{4,3},{5,2},{6,1},{7,0},{8,15},{9,14},{10,... | collective-permute-start | bytes 196616 | tf_op jit(solution)/shard_map/ppermute | solution.py:258
  43.7 10.0 %copy-start.4 = (bf16[128,128]{1,0:T(8,128)(2,1)S(1)}, bf16[128,128]{1,0:T(8,128)(2,1)}, u32[]{:S(2)}) copy-start(bf16[128,128]{1,0:T(8,128)(2,1)} %refs_4_.1) | copy-start | bytes 98308

commit v2 on v1

v2 whole, which is shorter than its diff:
```python
import functools
import math

import jax
import jax.numpy as jnp
from jax import lax
from jax.experimental import pallas as pl
from jax.experimental.pallas import tpu as pltpu
from jax.sharding import PartitionSpec as P

F32 = jnp.float32
BF16 = jnp.bfloat16
LANES = 128
EPS = 0.0025


def iota(shape, dim):
    return lax.broadcasted_iota(jnp.int32, shape, dim)


def count_columns(cnt_ref, boxes):
    eye = iota((LANES, LANES), 0) == iota((LANES, LANES), 1)
    cols = [
        jnp.sum(jnp.where(eye, cnt_ref[i : i + 1, :], 0), axis=1, keepdims=True)
        for i in range(boxes // LANES)
    ]
    return jnp.concatenate(cols, axis=0)


def log2(value):
    return value.bit_length() - 1


def code_columns(codes):
    rows = codes.shape[0]
    padded = jnp.concatenate([codes, jnp.zeros((LANES - rows, LANES), codes.dtype)], axis=0)
    return padded.T


def onehot(local, width):
    lane = iota((LANES, LANES), 1)
    parts = [
        jnp.where(local == lane + LANES * i, 1.0, 0.0).astype(BF16) for i in range(width // LANES)
    ]
    return jnp.concatenate(parts, axis=1)


def pattern_matrix(pattern_row, eye, patterns):
    own = jnp.where(eye, jnp.broadcast_to(pattern_row, eye.shape), -1)
    parts = [jnp.where(own == p, 1.0, 0.0).astype(BF16) for p in range(patterns)]
    return jnp.concatenate(parts, axis=0)


def dot(a, b):
    return jnp.dot(a, b, preferred_element_type=F32)


def slot_kernel(m_ref, src_ref, pat_ref, tgt_ref, ops_ref, out_ref, sums):
    boxes, width = m_ref.shape
    patterns = ops_ref.shape[0] // width
    groups, fanin, slots = src_ref.shape
    rows = out_ref.shape[1]
    pack = LANES // slots
    tiles = fanin // pack
    m = m_ref[...]

    def packed(ref, d, h):
        return jnp.concatenate([ref[d, h * pack + i : h * pack + i + 1, :] for i in range(pack)], axis=1)

    sources = [packed(src_ref, d, h) for d in range(groups) for h in range(tiles)]
    cols = code_columns(jnp.concatenate(sources, axis=0))
    eye = iota((slots, LANES), 0) == (iota((slots, LANES), 1) & (slots - 1))
    for d in range(groups):
        ones = []
        pats = []
        for h in range(tiles):
            i = d * tiles + h
            ones.append(onehot(jnp.broadcast_to(cols[:, i : i + 1], (LANES, LANES)), boxes))
            pats.append(pattern_matrix(packed(pat_ref, d, h), eye, patterns))
        got = dot(jnp.concatenate(ones, axis=0), m).astype(BF16)
        s = dot(jnp.concatenate(pats, axis=1), got).astype(BF16)
        for p in range(patterns):
            sums[d * slots : (d + 1) * slots, p * width : (p + 1) * width] = s[
                p * slots : (p + 1) * slots
            ]
    result = dot(sums[...], ops_ref[...])
    hi = result.astype(BF16)
    lo = (result - hi.astype(F32)).astype(BF16)
    for d in range(groups):
        target = tgt_ref[d : d + 1, :].astype(F32)
        out_ref[d, 0:slots, :] = hi[d * slots : (d + 1) * slots]
        out_ref[d, slots : 2 * slots, :] = lo[d * slots : (d + 1) * slots]
        out_ref[d, 2 * slots : rows, :] = jnp.broadcast_to(
            jnp.concatenate([target, target], axis=1), (rows - 2 * slots, 2 * slots)
        ).astype(BF16)


def near_kernel(nb_ref, cnt_ref, chg_ref, pos_ref, out_ref, feat, right, left):
    boxes = chg_ref.shape[0]
    knear = nb_ref.shape[0]
    live = iota((boxes, LANES), 1) < count_columns(cnt_ref, boxes)
    feat[7] = jnp.where(live, chg_ref[...].astype(F32), 0.0)
    norm = jnp.zeros((boxes, LANES), F32)
    for c in range(3):
        u = pos_ref[c] - 1.0
        h = u.astype(BF16).astype(F32)
        m = (u - h).astype(BF16).astype(F32)
        feat[2 * c] = h
        feat[2 * c + 1] = m
        v = h + m
        norm = norm + v * v
    feat[6] = norm

    def build(g, carry):
        rows = pl.ds(pl.multiple_of(g * 8, 8), 8)
        tile = [feat[f, rows, :] for f in range(7)]
        parts = []
        for c in range(3):
            h = -2.0 * tile[2 * c]
            m = -2.0 * tile[2 * c + 1]
            parts += [h, h, m, m]
        n = tile[6] + EPS
        n1 = n.astype(BF16).astype(F32)
        n2 = (n - n1).astype(BF16).astype(F32)
        parts += [n1, n2, n - n1 - n2, jnp.zeros((8, LANES), F32)]
        left[g] = jnp.concatenate(parts, axis=0).T.astype(BF16)
        for r in range(8):
            for c in range(3):
                h = jnp.broadcast_to(tile[2 * c][r : r + 1], (8, LANES))
                m = jnp.broadcast_to(tile[2 * c + 1][r : r + 1], (8, LANES))
                right[g * 8 + r, 16 * c : 16 * c + 16, :] = jnp.concatenate(
                    [h, m], axis=0
                ).astype(BF16)
        return carry

    lax.fori_loop(0, boxes // 8, build, 0)

    masks = [
        jnp.where((iota((LANES, LANES), 1) & 7) == j, 1.0, 0.0).astype(BF16) for j in range(8)
    ]
    eye = iota((LANES, LANES), 0) == iota((LANES, LANES), 1)
    ones = jnp.where(iota((32, LANES), 0) < 24, 1.0, 0.0).astype(BF16)

    def operand(box):
        x, y, z = [right[box, 16 * c : 16 * c + 16, :] for c in range(3)]
        return jnp.concatenate([x, x, y, y, z, z, ones], axis=0)

    def group(g, carry):
        turned = left[g]
        outs = []
        for r in range(8):
            lhs = turned * masks[r]
            acc = None
            for k in range(0, knear, 2):
                pair = [nb_ref[k + i, g * 8 + r] for i in range(2)]
                dist = dot(lhs, jnp.concatenate([operand(b) for b in pair], axis=1))
                for i in range(2):
                    shift = feat[6, pl.ds(pair[i], 1), :]
                    q = feat[7, pl.ds(pair[i], 1), :]
                    term = lax.rsqrt(dist[:, i * LANES : (i + 1) * LANES] + shift) * q
                    acc = term if acc is None else acc + term
            total = jnp.sum(acc, axis=1, keepdims=True)
            outs.append(jnp.sum(jnp.where(eye, total, 0.0), axis=0, keepdims=True))
        out_ref[pl.ds(pl.multiple_of(g * 8, 8), 8), :] = jnp.concatenate(outs, axis=0)
        return carry

    lax.fori_loop(0, boxes // 8, group, 0, unroll=2)


def group_kernel(*refs, blocks, fanin):
    code_ref, ops_ref, mine_ref, other_ref, out_ref, sums = refs
    width = mine_ref.shape[1]
    boxes = mine_ref.shape[0] // (blocks // 2)
    patterns = ops_ref.shape[0] // width
    per = LANES // fanin
    tiles = code_ref.shape[0]
    span = 2 * boxes
    pages = blocks // 2
    table = jnp.concatenate(
        [
            jnp.concatenate(
                [mine_ref[j * boxes : (j + 1) * boxes], other_ref[j * boxes : (j + 1) * boxes]], axis=0
            )
            for j in range(pages)
        ],
        axis=1,
    )
    codes = code_ref[...]
    cols = code_columns(codes)
    eye = iota((per, LANES), 0) == (iota((per, LANES), 1) >> log2(fanin))
    batch = 4
    for base in range(0, tiles, batch):
        picks = [
            jnp.broadcast_to(cols[:, i : i + 1], (LANES, LANES)) for i in range(base, base + batch)
        ]
        wide = dot(jnp.concatenate([onehot(c & (span - 1), span) for c in picks], axis=0), table)
        for n in range(batch):
            i = base + n
            page = (picks[n] >> log2(span)) & (pages - 1)
            part = wide[n * LANES : (n + 1) * LANES]
            got = part[:, 0:width]
            for j in range(1, pages):
                got = jnp.where(page == j, part[:, j * width : (j + 1) * width], got)
            pat = pattern_matrix(codes[i : i + 1, :] >> log2(blocks * boxes), eye, patterns)
            s = dot(pat, got.astype(BF16)).astype(BF16)
            for p in range(patterns):
                sums[i * per : (i + 1) * per, p * width : (p + 1) * width] = s[
                    p * per : (p + 1) * per
                ]
    out_ref[...] = dot(sums[...], ops_ref[...])


def final_kernel(*refs):
    cnt_ref, near_ref, local_ref, eval_ref = refs[:4]
    pay_refs = refs[4:-1]
    out_ref = refs[-1]
    boxes = local_ref.shape[0]
    hits = []
    values = []
    for pay in pay_refs:
        depth = pay.shape[0] - 16
        target = pay[depth : depth + 16, :].astype(F32)[0:1]
        box = iota((boxes, depth), 0).astype(F32)
        hits.append(jnp.where(box == target, 1.0, 0.0).astype(BF16))
        values.append(pay[0:depth, :])
    local = local_ref[...] + dot(jnp.concatenate(hits, axis=1), jnp.concatenate(values, axis=0))
    far = dot(local.astype(BF16), eval_ref[...])
    total = near_ref[...] * (1.0 / (4.0 * math.pi)) + far
    live = iota((boxes, LANES), 1) < count_columns(cnt_ref, boxes)
    out_ref[...] = jnp.where(live, total, 0.0)


VMEM = pl.BlockSpec(memory_space=pltpu.VMEM)
SMEM = pl.BlockSpec(memory_space=pltpu.SMEM)
MIB = 1024 * 1024


def body(
    n_oct,
    n_cube,
    charges,
    panel_counts,
    positions,
    moment_map,
    translations,
    evaluation,
    near_boxes,
    group_sources,
    group_patterns,
    remote_sources,
    remote_patterns,
    remote_targets,
):
    boxes, panels = charges.shape
    width = moment_map.shape[1]
    patterns = translations.shape[0]
    operators = translations.reshape(patterns * width, width)
    counts = panel_counts.reshape(boxes // LANES, LANES)
    slot_index = jnp.arange(panels, dtype=jnp.int32)
    live = slot_index[None, :] < panel_counts[:, None]
    strength = jnp.where(live, charges, jnp.zeros_like(charges))
    multipole = jnp.dot(strength, moment_map, preferred_element_type=F32).astype(BF16)

    me = lax.axis_index("cube")
    along = [multipole] + [
        lax.ppermute(multipole, "cube", [(i, i ^ k) for i in range(n_cube)])
        for k in range(2, n_cube, 2)
    ]

    near = pl.pallas_call(
        near_kernel,
        out_shape=jax.ShapeDtypeStruct((boxes, panels), F32),
        in_specs=[SMEM, VMEM, VMEM, VMEM],
        out_specs=VMEM,
        scratch_shapes=[
            pltpu.VMEM((8, boxes, panels), F32),
            pltpu.VMEM((boxes, 48, panels), BF16),
            pltpu.VMEM((boxes // 8, panels, LANES), BF16),
        ],
        compiler_params=pltpu.CompilerParams(vmem_limit_bytes=24 * MIB),
        cost_estimate=pl.CostEstimate(
            flops=15_000_000_000, bytes_accessed=1_000_000, transcendentals=16_000_000
        ),
        name="near",
    )(near_boxes.T, counts, charges, positions)

    near, base, *along = lax.optimization_barrier((near, multipole, *along))
    mine = jnp.concatenate(along, axis=0)
    other = lax.ppermute(mine, "cube", [(i, i ^ 1) for i in range(n_cube)])

    slots, fanin = remote_sources.shape[3:]
    sent = pl.pallas_call(
        slot_kernel,
        out_shape=jax.ShapeDtypeStruct((n_oct, 2 * slots + 16, width), BF16),
        in_specs=[VMEM] * 5,
        out_specs=VMEM,
        scratch_shapes=[pltpu.VMEM((n_oct * slots, patterns * width), BF16)],
        compiler_params=pltpu.CompilerParams(vmem_limit_bytes=16 * MIB),
        cost_estimate=pl.CostEstimate(
            flops=1_000_000_000, bytes_accessed=1_000_000, transcendentals=0
        ),
        name="slots",
    )(
        base,
        remote_sources[0, 0].transpose(0, 2, 1),
        remote_patterns[0, 0].transpose(0, 2, 1),
        remote_targets[0, 0],
        operators,
    )
    octant = lax.axis_index("oct")
    payloads = []
    for k in range(n_oct):
        part = lax.dynamic_index_in_dim(sent, octant ^ k, 0, keepdims=False)
        if k > 0:
            part = lax.ppermute(part, "oct", [(i, i ^ k) for i in range(n_oct)])
        payloads.append(part)

    klist = group_sources.shape[1]
    group = n_cube * boxes
    code = (group_sources ^ (me * boxes)) + group * group_patterns
    near_local = pl.pallas_call(
        functools.partial(group_kernel, blocks=n_cube, fanin=klist),
        out_shape=jax.ShapeDtypeStruct((boxes, width), F32),
        in_specs=[VMEM] * 4,
        out_specs=VMEM,
        scratch_shapes=[pltpu.VMEM((boxes, patterns * width), BF16)],
        compiler_params=pltpu.CompilerParams(vmem_limit_bytes=24 * MIB),
        cost_estimate=pl.CostEstimate(
            flops=3_000_000_000, bytes_accessed=2_000_000, transcendentals=0
        ),
        name="group",
    )(code.reshape(-1, LANES), operators, mine, other)

    return pl.pallas_call(
        final_kernel,
        out_shape=jax.ShapeDtypeStruct((boxes, panels), F32),
        in_specs=[VMEM] * (4 + n_oct),
        out_specs=VMEM,
        compiler_params=pltpu.CompilerParams(vmem_limit_bytes=16 * MIB),
        cost_estimate=pl.CostEstimate(
            flops=200_000_000, bytes_accessed=600_000, transcendentals=0
        ),
        name="final",
    )(counts, near, near_local, evaluation, *payloads)


def solution(mesh):
    n_oct = mesh.shape["oct"]
    n_cube = mesh.shape["cube"]

    def run(*arrays):
        return body(n_oct, n_cube, *arrays)

    return jax.shard_map(
        run,
        mesh=mesh,
        in_specs=(
            P(("oct", "cube"), None),
            P(("oct", "cube")),
            P(None, ("oct", "cube"), None),
            P(),
            P(),
            P(),
            P(("oct", "cube"), None),
            P(("oct", "cube"), None),
            P(("oct", "cube"), None),
            P("oct", "cube", None, None, None),
            P("oct", "cube", None, None, None),
            P("oct", "cube", None, None),
        ),
        out_specs=P(("oct", "cube"), None),
        check_vma=False,
    )
```

time: 59.2 us -> 40.2 us (0.68)
  the two profiles are of different devices: /device:TPU:19 before, /device:TPU:0 now
where the time goes in v2:
time: 40.2 us; the launch traced here: 39.9 us
  Pallas kernels  23.6 us (59%)
  starting transfers between devices  9.3 us (23%)
  local copies, waits for them, and re-layouts  3.47 us (9%)
  waiting for transfers between devices  2.19 us (5%)
  matrix products  1.06 us (3%)
    pallas_call x1, Pallas kernels, body(): pl.pallas_call(near_kernel, out_shape=jax.ShapeDtypeStruct((boxes, panels...  18.6 us
    ppermute x3, starting transfers between devices, body(): lax.ppermute(multipole, 'cube', [(i, i ^ k) for i in range(n_cube)])  5.68 us
    ppermute x3, starting transfers between devices, body(): part = lax.ppermute(part, 'oct', [(i, i ^ k) for i in range(n_oct)])  3.55 us
    unnamed x27, local copies, waits for them, and re-layouts  3.2 us
    pallas_call x1, Pallas kernels, body(): pl.pallas_call(functools.partial(group_kernel, blocks=n_cube, fanin=klist...  2.36 us
    ppermute x3, waiting for transfers between devices, body(): part = lax.ppermute(part, 'oct', [(i, i ^ k) for i in range(n_oct)])  2.18 us
    pallas_call x1, Pallas kernels, body(): pl.pallas_call(slot_kernel, out_shape=jax.ShapeDtypeStruct((n_oct, 2 * sl...  1.59 us
    dot_general x1, matrix products, body(): jnp.dot(strength, moment_map, preferred_element_type=F32).astype(BF16)  1.06 us
  transfers between devices with their start and end apart: 7, of which 1 were waited for; matrix products, arithmetic and copies ran while one was open for 1% of the time, Pallas kernels for 57%

profile of v2, /device:TPU:0, one launch (start us, length us, event | category | flops | bytes accessed | tf_op | source)
XLA Modules:
  0.0 39.9 jit_solution(13163369906260983953)
XLA Ops:
  0.0 0.8 %copy-done = bf16[128,128]{1,0:T(8,128)(2,1)S(1)} copy-done((bf16[128,128]{1,0:T(8,128)(2,1)S(1)}, bf16[128,128]{1,0:T(8,128)(2,1)}, u32[]{:S(2)}) %copy-start) | copy-done | bytes 32792
  0.8 1.1 %convolution_convert_fusion.m_ref = bf16[256,128]{1,0:T(8,128)(2,1)S(1)} fusion(bf16[128,128]{1,0:T(8,128)(2,1)S(1)} %copy-done, bf16[256,128]{1,0:T(8,128)(2,1)} %chg_ref.1, s32[256]{0:T(256)} %param.13), kind=kOutput, calls=%fused_computation | convolution fusion | flops 8486912 | bytes 164864 | tf_op jit(solution)/shard_map/dot_general | solution.py:262
  1.8 3.1 %collective-permute-start = (bf16[256,128]{1,0:T(8,128)(2,1)S(1)}, bf16[256,128]{1,0:T(8,128)(2,1)S(1)}, u32[]{:S(2)}, u32[]{:S(2)}) collective-permute-start(bf16[256,128]{1,0:T(8,128)(2,1)S(1)} %convolution_convert_fusion.m_ref), channel_id=1, source_target_pairs={{0,2},{1,3},{2,0},{3,1},{4,6},{5,7},{6,4},{7,5},{8,10},{9,11},{10,... | collective-permute-start | bytes 196616 | tf_op jit(solution)/shard_map/ppermute | solution.py:266
  4.9 2.6 %collective-permute-start.1 = (bf16[256,128]{1,0:T(8,128)(2,1)S(1)}, bf16[256,128]{1,0:T(8,128)(2,1)S(1)}, u32[]{:S(2)}, u32[]{:S(2)}) collective-permute-start(bf16[256,128]{1,0:T(8,128)(2,1)S(1)} %convolution_convert_fusion.m_ref), channel_id=1, source_target_pairs={{0,4},{1,5},{2,6},{3,7},{4,0},{5,1},{6,2},{7,3},{8,12},{9,13},{10,... | collective-permute-start | bytes 196616 | tf_op jit(solution)/shard_map/ppermute | solution.py:266
  7.5 0.7 %copy-done.9 = s32[256]{0:T(256)S(1)} copy-done((s32[256]{0:T(256)S(1)}, s32[256]{0:T(256)}, u32[]{:S(2)}) %copy-start.9) | copy-done | bytes 1048
  8.2 1.0 %copy-done.2 = f32[3,256,128]{2,1,0:T(8,128)S(1)} copy-done((f32[3,256,128]{2,1,0:T(8,128)S(1)}, f32[3,256,128]{2,1,0:T(8,128)}, u32[]{:S(2)}) %copy-start.2) | copy-done | bytes 393240
  9.2 18.6 %near.1.refs_1_ = f32[256,128]{1,0:T(8,128)S(1)} custom-call(s32[4,256]{1,0:T(4,128)S(1)} %bitcast.23, s32[2,128]{1,0:T(2,128)S(1)} %bitcast.25, bf16[256,128]{1,0:T(8,128)(2,1)S(1)} %copy-done.3, f32[3,256,128]{2,1,0:T(8,128)S(1)} %copy-done.2), custom_call_target="tpu_custom_call" | custom-call | flops 15000000512 | bytes 1000000 | tf_op jit(solution)/shard_map/near/pallas_call | solution.py:270
  27.8 0.0 copy-start.1
  27.9 0.1 collective-permute-start.3
  28.1 0.1 copy.14
  28.2 0.0 copy-start.6
  28.2 0.1 reshape.11.refs_0_
  28.3 0.0 copy-start.8
  28.4 0.5 %copy-done.1 = bf16[16,128,128]{2,1,0:T(8,128)(2,1)S(1)} copy-done((bf16[16,128,128]{2,1,0:T(8,128)(2,1)S(1)}, bf16[16,128,128]{2,1,0:T(8,128)(2,1)}, u32[]{:S(2)}) %copy-start.1) | copy-done | bytes 524312
  28.9 0.1 copy-done.6
  28.9 0.1 copy-done.5
  29.1 0.0 copy-done.8
  29.1 1.6 %slots.1 = bf16[4,144,128]{2,1,0:T(8,128)(2,1)S(1)} custom-call(bf16[256,128]{1,0:T(8,128)(2,1)S(1)} %convolution_convert_fusion.m_ref, s32[4,4,64]{2,1,0:T(4,128)S(1)} %bitcast.21, s32[4,4,64]{2,1,0:T(4,128)S(1)} %bitcast.22, s32[4,64]{1,0:T(4,128)S(1)} %bitcast.24, bf16[2048,128]{1,0:T(8,128)(2,1)S(1)} %bitcast.19), custom_call_target="tpu_custom_call" | custom-call | flops 1000000000 | bytes 1000000 | tf_op jit(solution)/shard_map/slots/pallas_call | solution.py:292
  30.7 1.8 %collective-permute-start.4 = (bf16[144,128]{1,0:T(8,128)(2,1)S(1)}, bf16[144,128]{1,0:T(8,128)(2,1)S(1)}, u32[]{:S(2)}, u32[]{:S(2)}) collective-permute-start(bf16[144,128]{1,0:T(8,128)(2,1)S(1)} %get-tuple-element.19), channel_id=1, source_target_pairs={{0,8},{8,0},{16,24},{24,16},{1,9},{9,1},{17,25},{25,17},{2,10},{10... | collective-permute-start | bytes 110600 | tf_op jit(solution)/shard_map/ppermute | solution.py:315
  32.5 1.5 %collective-permute-start.5 = (bf16[144,128]{1,0:T(8,128)(2,1)S(1)}, bf16[144,128]{1,0:T(8,128)(2,1)S(1)}, u32[]{:S(2)}, u32[]{:S(2)}) collective-permute-start(bf16[144,128]{1,0:T(8,128)(2,1)S(1)} %get-tuple-element.18), channel_id=1, source_target_pairs={{0,16},{8,24},{16,0},{24,8},{1,17},{9,25},{17,1},{25,9},{2,18},{10... | collective-permute-start | bytes 110600 | tf_op jit(solution)/shard_map/ppermute | solution.py:315
  34.0 0.3 collective-permute-start.6
  34.3 2.4 %group.1.refs_2_ = f32[256,128]{1,0:T(8,128)S(1)} custom-call(s32[16,128]{1,0:T(8,128)S(1)} %reshape.11.refs_0_, bf16[2048,128]{1,0:T(8,128)(2,1)S(1)} %bitcast.20, bf16[1024,128]{1,0:T(8,128)(2,1)S(1)} %constant_dynamic-update-slice_fusion.refs_2_, bf16[1024,128]{1,0:T(8,128)(2,1)S(1)} %collective-permute-done.3.refs_3_), custom_call_target="tpu_custom_call" | custom-call | flops 3000000000 | bytes 2000000 | tf_op jit(solution)/shard_map/group/pallas_call | solution.py:321
  36.6 2.2 %collective-permute-done.6.refs_7_ = bf16[144,128]{1,0:T(8,128)(2,1)S(1)} collective-permute-done((bf16[144,128]{1,0:T(8,128)(2,1)S(1)}, bf16[144,128]{1,0:T(8,128)(2,1)S(1)}, u32[]{:S(2)}, u32[]{:S(2)}) %collective-permute-start.6) | collective-permute-done | bytes 36896 | tf_op jit(solution)/shard_map/ppermute | solution.py:315
  38.8 1.0 %final.1 = f32[256,128]{1,0:T(8,128)} custom-call(s32[2,128]{1,0:T(2,128)S(1)} %bitcast.26, f32[256,128]{1,0:T(8,128)S(1)} %near.1.refs_1_, f32[256,128]{1,0:T(8,128)S(1)} %group.1.refs_2_, bf16[128,128]{1,0:T(8,128)(2,1)S(1)} %copy-done.4, bf16[144,128]{1,0:T(8,128)(2,1)S(1)} %get-tuple-element.20.refs_4_, ...), custom_call_target="tpu_custom_call" | custom-call | flops 200000000 | bytes 600000 | tf_op jit(solution)/shard_map/final/pallas_call | solution.py:334
  (27 shorter events, 0.1 us)
Async XLA Ops:
  0.0 0.8 %copy-start = (bf16[128,128]{1,0:T(8,128)(2,1)S(1)}, bf16[128,128]{1,0:T(8,128)(2,1)}, u32[]{:S(2)}) copy-start(bf16[128,128]{1,0:T(8,128)(2,1)} %param.15) | copy-start | bytes 98308
  0.0 7.5 %copy-start.3 = (bf16[256,128]{1,0:T(8,128)(2,1)S(1)}, bf16[256,128]{1,0:T(8,128)(2,1)}, u32[]{:S(2)}) copy-start(bf16[256,128]{1,0:T(8,128)(2,1)} %chg_ref.1) | copy-start | bytes 196612
  0.0 7.5 %copy-start.7 = (s32[256,4]{0,1:T(4,128)S(1)}, s32[256,4]{0,1:T(4,128)}, u32[]{:S(2)}) copy-start(s32[256,4]{0,1:T(4,128)} %param.18) | copy-start | bytes 12292
  1.8 26.0 %collective-permute-start = (bf16[256,128]{1,0:T(8,128)(2,1)S(1)}, bf16[256,128]{1,0:T(8,128)(2,1)S(1)}, u32[]{:S(2)}, u32[]{:S(2)}) collective-permute-start(bf16[256,128]{1,0:T(8,128)(2,1)S(1)} %convolution_convert_fusion.m_ref), channel_id=1, source_target_pairs={{0,2},{1,3},{2,0},{3,1},{4,6},{5,7},{6,4},{7,5},{8,10},{9,11},{10,... | collective-permute-start | bytes 196616 | tf_op jit(solution)/shard_map/ppermute | solution.py:266
  4.9 22.9 %collective-permute-start.1 = (bf16[256,128]{1,0:T(8,128)(2,1)S(1)}, bf16[256,128]{1,0:T(8,128)(2,1)S(1)}, u32[]{:S(2)}, u32[]{:S(2)}) collective-permute-start(bf16[256,128]{1,0:T(8,128)(2,1)S(1)} %convolution_convert_fusion.m_ref), channel_id=1, source_target_pairs={{0,4},{1,5},{2,6},{3,7},{4,0},{5,1},{6,2},{7,3},{8,12},{9,13},{10,... | collective-permute-start | bytes 196616 | tf_op jit(solution)/shard_map/ppermute | solution.py:266
  7.5 20.4 %collective-permute-start.2 = (bf16[256,128]{1,0:T(8,128)(2,1)S(1)}, bf16[256,128]{1,0:T(8,128)(2,1)S(1)}, u32[]{:S(2)}, u32[]{:S(2)}) collective-permute-start(bf16[256,128]{1,0:T(8,128)(2,1)S(1)} %convolution_convert_fusion.m_ref), channel_id=1, source_target_pairs={{0,6},{1,7},{2,4},{3,5},{4,2},{5,3},{6,0},{7,1},{8,14},{9,15},{10,... | collective-permute-start | bytes 196616 | tf_op jit(solution)/shard_map/ppermute | solution.py:266
  7.5 0.7 %copy-start.9 = (s32[256]{0:T(256)S(1)}, s32[256]{0:T(256)}, u32[]{:S(2)}) copy-start(s32[256]{0:T(256)} %param.13) | copy-start | bytes 3076
  8.2 1.0 %copy-start.2 = (f32[3,256,128]{2,1,0:T(8,128)S(1)}, f32[3,256,128]{2,1,0:T(8,128)}, u32[]{:S(2)}) copy-start(f32[3,256,128]{2,1,0:T(8,128)} %pos_ref.1) | copy-start | bytes 1179652
  9.2 18.8 %copy-start.10 = (s32[256,8]{0,1:T(8,128)S(1)}, s32[256,8]{0,1:T(8,128)}, u32[]{:S(2)}) copy-start(s32[256,8]{0,1:T(8,128)} %param.20) | copy-start | bytes 24580
  9.2 18.8 %copy-start.11 = (s32[256,8]{0,1:T(8,128)S(1)}, s32[256,8]{0,1:T(8,128)}, u32[]{:S(2)}) copy-start(s32[256,8]{0,1:T(8,128)} %param.19) | copy-start | bytes 24580
  27.8 1.0 %copy-start.1 = (bf16[16,128,128]{2,1,0:T(8,128)(2,1)S(1)}, bf16[16,128,128]{2,1,0:T(8,128)(2,1)}, u32[]{:S(2)}) copy-start(bf16[16,128,128]{2,1,0:T(8,128)(2,1)} %param.16) | copy-start | bytes 1572868
  27.9 6.3 %collective-permute-start.3 = (bf16[1024,128]{1,0:T(8,128)(2,1)S(1)}, bf16[1024,128]{1,0:T(8,128)(2,1)S(1)}, u32[]{:S(2)}, u32[]{:S(2)}) collective-permute-start(bf16[1024,128]{1,0:T(8,128)(2,1)S(1)} %constant_dynamic-update-slice_fusion.refs_2_), channel_id=1, source_target_pairs={{0,1},{1,0},{2,3},{3,2},{4,5},{5,4},{6,7},{7,6},{8,9},{9,8},{10,11... | collective-permute-start | bytes 786440 | tf_op jit(solution)/shard_map/ppermute | solution.py:289
  28.2 0.7 %copy-start.6 = (s32[1,1,4,64,4]{3,4,2,1,0:T(4,128)S(1)}, s32[1,1,4,64,4]{3,4,2,1,0:T(4,128)}, u32[]{:S(2)}) copy-start(s32[1,1,4,64,4]{3,4,2,1,0:T(4,128)} %param.22) | copy-start | bytes 12292
  28.3 0.7 %copy-start.5 = (s32[1,1,4,64,4]{3,4,2,1,0:T(4,128)S(1)}, s32[1,1,4,64,4]{3,4,2,1,0:T(4,128)}, u32[]{:S(2)}) copy-start(s32[1,1,4,64,4]{3,4,2,1,0:T(4,128)} %param.21) | copy-start | bytes 12292
  28.3 0.7 %copy-start.8 = (s32[1,1,4,64]{3,2,1,0:T(4,128)S(1)}, s32[1,1,4,64]{3,2,1,0:T(4,128)}, u32[]{:S(2)}) copy-start(s32[1,1,4,64]{3,2,1,0:T(4,128)} %param.23) | copy-start | bytes 3076
  30.7 5.9 %collective-permute-start.4 = (bf16[144,128]{1,0:T(8,128)(2,1)S(1)}, bf16[144,128]{1,0:T(8,128)(2,1)S(1)}, u32[]{:S(2)}, u32[]{:S(2)}) collective-permute-start(bf16[144,128]{1,0:T(8,128)(2,1)S(1)} %get-tuple-element.19), channel_id=1, source_target_pairs={{0,8},{8,0},{16,24},{24,16},{1,9},{9,1},{17,25},{25,17},{2,10},{10... | collective-permute-start | bytes 110600 | tf_op jit(solution)/shard_map/ppermute | solution.py:315
  32.5 4.1 %collective-permute-start.5 = (bf16[144,128]{1,0:T(8,128)(2,1)S(1)}, bf16[144,128]{1,0:T(8,128)(2,1)S(1)}, u32[]{:S(2)}, u32[]{:S(2)}) collective-permute-start(bf16[144,128]{1,0:T(8,128)(2,1)S(1)} %get-tuple-element.18), channel_id=1, source_target_pairs={{0,16},{8,24},{16,0},{24,8},{1,17},{9,25},{17,1},{25,9},{2,18},{10... | collective-permute-start | bytes 110600 | tf_op jit(solution)/shard_map/ppermute | solution.py:315
  34.0 4.9 %copy-start.4 = (bf16[128,128]{1,0:T(8,128)(2,1)S(1)}, bf16[128,128]{1,0:T(8,128)(2,1)}, u32[]{:S(2)}) copy-start(bf16[128,128]{1,0:T(8,128)(2,1)} %refs_3_.1) | copy-start | bytes 98308
  34.0 4.9 %collective-permute-start.6 = (bf16[144,128]{1,0:T(8,128)(2,1)S(1)}, bf16[144,128]{1,0:T(8,128)(2,1)S(1)}, u32[]{:S(2)}, u32[]{:S(2)}) collective-permute-start(bf16[144,128]{1,0:T(8,128)(2,1)S(1)} %get-tuple-element.17), channel_id=1, source_target_pairs={{0,24},{8,16},{16,8},{24,0},{1,25},{9,17},{17,9},{25,1},{2,26},{10... | collective-permute-start | bytes 110600 | tf_op jit(solution)/shard_map/ppermute | solution.py:315

commit v3 on v2

--- a/solution.py
+++ b/solution.py
@@ -111,6 +111,13 @@
         norm = norm + v * v
     feat[6] = norm
 
+    def split(n):
+        n1 = n.astype(BF16).astype(F32)
+        n2 = (n - n1).astype(BF16).astype(F32)
+        return n1, n2, n - n1 - n2
+
+    zero8 = jnp.zeros((8, LANES), F32)
+
     def build(g, carry):
         rows = pl.ds(pl.multiple_of(g * 8, 8), 8)
         tile = [feat[f, rows, :] for f in range(7)]
@@ -119,52 +126,72 @@
             h = -2.0 * tile[2 * c]
             m = -2.0 * tile[2 * c + 1]
             parts += [h, h, m, m]
-        n = tile[6] + EPS
-        n1 = n.astype(BF16).astype(F32)
-        n2 = (n - n1).astype(BF16).astype(F32)
-        parts += [n1, n2, n - n1 - n2, jnp.zeros((8, LANES), F32)]
+        parts += [*split(tile[6] + EPS), zero8]
         left[g] = jnp.concatenate(parts, axis=0).T.astype(BF16)
+        columns = tile[:6] + list(split(tile[6]))
         for r in range(8):
-            for c in range(3):
-                h = jnp.broadcast_to(tile[2 * c][r : r + 1], (8, LANES))
-                m = jnp.broadcast_to(tile[2 * c + 1][r : r + 1], (8, LANES))
-                right[g * 8 + r, 16 * c : 16 * c + 16, :] = jnp.concatenate(
-                    [h, m], axis=0
+            wide = [jnp.broadcast_to(v[r : r + 1], (8, LANES)) for v in columns] + [zero8]
+            for i in range(5):
+                right[g * 8 + r, 16 * i : 16 * i + 16, :] = jnp.concatenate(
+                    wide[2 * i : 2 * i + 2], axis=0
                 ).astype(BF16)
         return carry
 
     lax.fori_loop(0, boxes // 8, build, 0)
 
-    masks = [
-        jnp.where((iota((LANES, LANES), 1) & 7) == j, 1.0, 0.0).astype(BF16) for j in range(8)
-    ]
-    eye = iota((LANES, LANES), 0) == iota((LANES, LANES), 1)
+    lane = iota((LANES, LANES), 1)
+    own = [jnp.where((lane & 7) == j, 1.0, 0.0).astype(BF16) for j in range(8)]
+    unit = [jnp.where(((lane & 7) == j) & (lane < 24), 1.0, 0.0).astype(BF16) for j in range(8)]
+    eye = iota((LANES, LANES), 0) == lane
     ones = jnp.where(iota((32, LANES), 0) < 24, 1.0, 0.0).astype(BF16)
+    none = jnp.zeros((96, LANES), BF16)
 
     def operand(box):
-        x, y, z = [right[box, 16 * c : 16 * c + 16, :] for c in range(3)]
-        return jnp.concatenate([x, x, y, y, z, z, ones], axis=0)
-
-    def group(g, carry):
-        turned = left[g]
-        outs = []
-        for r in range(8):
-            lhs = turned * masks[r]
-            acc = None
-            for k in range(0, knear, 2):
-                pair = [nb_ref[k + i, g * 8 + r] for i in range(2)]
-                dist = dot(lhs, jnp.concatenate([operand(b) for b in pair], axis=1))
-                for i in range(2):
-                    shift = feat[6, pl.ds(pair[i], 1), :]
-                    q = feat[7, pl.ds(pair[i], 1), :]
-                    term = lax.rsqrt(dist[:, i * LANES : (i + 1) * LANES] + shift) * q
-                    acc = term if acc is None else acc + term
-            total = jnp.sum(acc, axis=1, keepdims=True)
-            outs.append(jnp.sum(jnp.where(eye, total, 0.0), axis=0, keepdims=True))
-        out_ref[pl.ds(pl.multiple_of(g * 8, 8), 8), :] = jnp.concatenate(outs, axis=0)
-        return carry
-
-    lax.fori_loop(0, boxes // 8, group, 0, unroll=2)
+        x, y, z, n, t = [right[box, 16 * c : 16 * c + 16, :] for c in range(5)]
+        return jnp.concatenate([x, x, y, y, z, z, ones, n, t, none], axis=0)
+
+    assert knear == 4
+    last = boxes // 8 - 1
+
+    def issue(accs, g, r, slot):
+        box = g * 8 + r
+        lhs = jnp.concatenate([left[g] * own[r], unit[r]], axis=1)
+        for side in range(2):
+            pair = [operand(nb_ref[2 * side + i, box]) for i in range(2)]
+            pltpu.matmul_push_rhs(jnp.concatenate(pair, axis=1), slot, side)
+            pltpu.matmul_acc_lhs(accs[2 * side + slot], lhs, load_staged_rhs=slot)
+
+    def collect(accs, g, r, slot):
+        box = g * 8 + r
+        acc = None
+        for side in range(2):
+            dist = pltpu.matmul_pop(accs[2 * side + slot])
+            for i in range(2):
+                q = feat[7, pl.ds(nb_ref[2 * side + i, box], 1), :]
+                term = lax.rsqrt(dist[:, i * LANES : (i + 1) * LANES]) * q
+                acc = term if acc is None else acc + term
+        total = jnp.sum(acc, axis=1, keepdims=True)
+        return jnp.sum(jnp.where(eye, total, 0.0), axis=0, keepdims=True)
+
+    def run(*accs):
+        issue(accs, 0, 0, 0)
+
+        def group(g, carry):
+            outs = []
+            for r in range(8):
+                if r < 7:
+                    issue(accs, g, r + 1, (r + 1) % 2)
+                else:
+                    issue(accs, jnp.minimum(g + 1, last), 0, 0)
+                outs.append(collect(accs, g, r, r % 2))
+            out_ref[pl.ds(pl.multiple_of(g * 8, 8), 8), :] = jnp.concatenate(outs, axis=0)
+            return carry
+
+        lax.fori_loop(0, boxes // 8, group, 0)
+        for side in range(2):
+            pltpu.matmul_pop(accs[2 * side])
+
+    pl.run_scoped(run, *[pltpu.ACC(i // 2)((LANES, 2 * LANES), F32) for i in range(4)])
 
 
 def group_kernel(*refs, blocks, fanin):
@@ -274,7 +301,7 @@
         out_specs=VMEM,
         scratch_shapes=[
             pltpu.VMEM((8, boxes, panels), F32),
-            pltpu.VMEM((boxes, 48, panels), BF16),
+            pltpu.VMEM((boxes, 80, panels), BF16),
             pltpu.VMEM((boxes // 8, panels, LANES), BF16),
         ],
         compiler_params=pltpu.CompilerParams(vmem_limit_bytes=24 * MIB),

time: 40.2 us -> 47.8 us (1.19)
  Pallas kernels: 23.6 us -> 31.2 us
    pallas_call x1, Pallas kernels: 18.6 us -> 26.3 us  [body(): pl.pallas_call(near_kernel, out_shape=jax.ShapeDtypeStruct((boxes, panels...]
  transfers between devices with their start and end apart: 7 -> 7, of which waited for: 1 -> 1; matrix products, arithmetic and copies ran while one was open for 1% -> 1% of each run, Pallas kernels for 57% -> 63%
where the time goes in v3:
time: 47.8 us; the launch traced here: 47.6 us
  Pallas kernels  31.2 us (65%)
  starting transfers between devices  9.3 us (19%)
  local copies, waits for them, and re-layouts  3.47 us (7%)
  waiting for transfers between devices  2.26 us (5%)
  matrix products  1.06 us (2%)
    pallas_call x1, Pallas kernels, body(): pl.pallas_call(near_kernel, out_shape=jax.ShapeDtypeStruct((boxes, panels...  26.3 us
    ppermute x3, starting transfers between devices, body(): lax.ppermute(multipole, 'cube', [(i, i ^ k) for i in range(n_cube)])  5.68 us
    ppermute x3, starting transfers between devices, body(): part = lax.ppermute(part, 'oct', [(i, i ^ k) for i in range(n_oct)])  3.55 us
    unnamed x27, local copies, waits for them, and re-layouts  3.2 us
    pallas_call x1, Pallas kernels, body(): pl.pallas_call(functools.partial(group_kernel, blocks=n_cube, fanin=klist...  2.36 us
    ppermute x3, waiting for transfers between devices, body(): part = lax.ppermute(part, 'oct', [(i, i ^ k) for i in range(n_oct)])  2.25 us
    pallas_call x1, Pallas kernels, body(): pl.pallas_call(slot_kernel, out_shape=jax.ShapeDtypeStruct((n_oct, 2 * sl...  1.59 us
    dot_general x1, matrix products, body(): jnp.dot(strength, moment_map, preferred_element_type=F32).astype(BF16)  1.06 us
  transfers between devices with their start and end apart: 7, of which 1 were waited for; matrix products, arithmetic and copies ran while one was open for 1% of the time, Pallas kernels for 63%

profile of v3, /device:TPU:0, one launch (start us, length us, event | category | flops | bytes accessed | tf_op | source)
XLA Modules:
  0.0 47.6 jit_solution(10546099822085796933)
XLA Ops:
  0.0 0.8 %copy-done = bf16[128,128]{1,0:T(8,128)(2,1)S(1)} copy-done((bf16[128,128]{1,0:T(8,128)(2,1)S(1)}, bf16[128,128]{1,0:T(8,128)(2,1)}, u32[]{:S(2)}) %copy-start) | copy-done | bytes 32792
  0.8 1.1 %convolution_convert_fusion.m_ref = bf16[256,128]{1,0:T(8,128)(2,1)S(1)} fusion(bf16[128,128]{1,0:T(8,128)(2,1)S(1)} %copy-done, bf16[256,128]{1,0:T(8,128)(2,1)} %chg_ref.1, s32[256]{0:T(256)} %param.13), kind=kOutput, calls=%fused_computation | convolution fusion | flops 8486912 | bytes 164864 | tf_op jit(solution)/shard_map/dot_general | solution.py:289
  1.8 3.1 %collective-permute-start = (bf16[256,128]{1,0:T(8,128)(2,1)S(1)}, bf16[256,128]{1,0:T(8,128)(2,1)S(1)}, u32[]{:S(2)}, u32[]{:S(2)}) collective-permute-start(bf16[256,128]{1,0:T(8,128)(2,1)S(1)} %convolution_convert_fusion.m_ref), channel_id=1, source_target_pairs={{0,2},{1,3},{2,0},{3,1},{4,6},{5,7},{6,4},{7,5},{8,10},{9,11},{10,... | collective-permute-start | bytes 196616 | tf_op jit(solution)/shard_map/ppermute | solution.py:293
  4.9 2.6 %collective-permute-start.1 = (bf16[256,128]{1,0:T(8,128)(2,1)S(1)}, bf16[256,128]{1,0:T(8,128)(2,1)S(1)}, u32[]{:S(2)}, u32[]{:S(2)}) collective-permute-start(bf16[256,128]{1,0:T(8,128)(2,1)S(1)} %convolution_convert_fusion.m_ref), channel_id=1, source_target_pairs={{0,4},{1,5},{2,6},{3,7},{4,0},{5,1},{6,2},{7,3},{8,12},{9,13},{10,... | collective-permute-start | bytes 196616 | tf_op jit(solution)/shard_map/ppermute | solution.py:293
  7.5 0.7 %copy-done.9 = s32[256]{0:T(256)S(1)} copy-done((s32[256]{0:T(256)S(1)}, s32[256]{0:T(256)}, u32[]{:S(2)}) %copy-start.9) | copy-done | bytes 1048
  8.2 1.0 %copy-done.2 = f32[3,256,128]{2,1,0:T(8,128)S(1)} copy-done((f32[3,256,128]{2,1,0:T(8,128)S(1)}, f32[3,256,128]{2,1,0:T(8,128)}, u32[]{:S(2)}) %copy-start.2) | copy-done | bytes 393240
  9.2 26.3 %near.1.refs_1_ = f32[256,128]{1,0:T(8,128)S(1)} custom-call(s32[4,256]{1,0:T(4,128)S(1)} %bitcast.23, s32[2,128]{1,0:T(2,128)S(1)} %bitcast.25, bf16[256,128]{1,0:T(8,128)(2,1)S(1)} %copy-done.3, f32[3,256,128]{2,1,0:T(8,128)S(1)} %copy-done.2), custom_call_target="tpu_custom_call" | custom-call | flops 15000000512 | bytes 1000000 | tf_op jit(solution)/shard_map/near/pallas_call | solution.py:297
  35.4 0.0 copy-start.1
  35.6 0.1 collective-permute-start.3
  35.7 0.1 copy.14
  35.8 0.0 copy-start.6
  35.8 0.1 reshape.11.refs_0_
  36.0 0.0 copy-start.8
  36.0 0.5 %copy-done.1 = bf16[16,128,128]{2,1,0:T(8,128)(2,1)S(1)} copy-done((bf16[16,128,128]{2,1,0:T(8,128)(2,1)S(1)}, bf16[16,128,128]{2,1,0:T(8,128)(2,1)}, u32[]{:S(2)}) %copy-start.1) | copy-done | bytes 524312
  36.5 0.1 copy-done.6
  36.6 0.1 copy-done.5
  36.7 0.0 copy-done.8
  36.7 1.6 %slots.1 = bf16[4,144,128]{2,1,0:T(8,128)(2,1)S(1)} custom-call(bf16[256,128]{1,0:T(8,128)(2,1)S(1)} %convolution_convert_fusion.m_ref, s32[4,4,64]{2,1,0:T(4,128)S(1)} %bitcast.21, s32[4,4,64]{2,1,0:T(4,128)S(1)} %bitcast.22, s32[4,64]{1,0:T(4,128)S(1)} %bitcast.24, bf16[2048,128]{1,0:T(8,128)(2,1)S(1)} %bitcast.19), custom_call_target="tpu_custom_call" | custom-call | flops 1000000000 | bytes 1000000 | tf_op jit(solution)/shard_map/slots/pallas_call | solution.py:319
  38.3 1.8 %collective-permute-start.4 = (bf16[144,128]{1,0:T(8,128)(2,1)S(1)}, bf16[144,128]{1,0:T(8,128)(2,1)S(1)}, u32[]{:S(2)}, u32[]{:S(2)}) collective-permute-start(bf16[144,128]{1,0:T(8,128)(2,1)S(1)} %get-tuple-element.19), channel_id=1, source_target_pairs={{0,8},{8,0},{16,24},{24,16},{1,9},{9,1},{17,25},{25,17},{2,10},{10... | collective-permute-start | bytes 110600 | tf_op jit(solution)/shard_map/ppermute | solution.py:342
  40.1 1.5 %collective-permute-start.5 = (bf16[144,128]{1,0:T(8,128)(2,1)S(1)}, bf16[144,128]{1,0:T(8,128)(2,1)S(1)}, u32[]{:S(2)}, u32[]{:S(2)}) collective-permute-start(bf16[144,128]{1,0:T(8,128)(2,1)S(1)} %get-tuple-element.18), channel_id=1, source_target_pairs={{0,16},{8,24},{16,0},{24,8},{1,17},{9,25},{17,1},{25,9},{2,18},{10... | collective-permute-start | bytes 110600 | tf_op jit(solution)/shard_map/ppermute | solution.py:342
  41.7 0.2 collective-permute-start.6
  41.9 2.4 %group.1.refs_2_ = f32[256,128]{1,0:T(8,128)S(1)} custom-call(s32[16,128]{1,0:T(8,128)S(1)} %reshape.11.refs_0_, bf16[2048,128]{1,0:T(8,128)(2,1)S(1)} %bitcast.20, bf16[1024,128]{1,0:T(8,128)(2,1)S(1)} %constant_dynamic-update-slice_fusion.refs_2_, bf16[1024,128]{1,0:T(8,128)(2,1)S(1)} %collective-permute-done.3.refs_3_), custom_call_target="tpu_custom_call" | custom-call | flops 3000000000 | bytes 2000000 | tf_op jit(solution)/shard_map/group/pallas_call | solution.py:348
  44.3 2.2 %collective-permute-done.6.refs_7_ = bf16[144,128]{1,0:T(8,128)(2,1)S(1)} collective-permute-done((bf16[144,128]{1,0:T(8,128)(2,1)S(1)}, bf16[144,128]{1,0:T(8,128)(2,1)S(1)}, u32[]{:S(2)}, u32[]{:S(2)}) %collective-permute-start.6) | collective-permute-done | bytes 36896 | tf_op jit(solution)/shard_map/ppermute | solution.py:342
  46.5 1.0 %final.1 = f32[256,128]{1,0:T(8,128)} custom-call(s32[2,128]{1,0:T(2,128)S(1)} %bitcast.26, f32[256,128]{1,0:T(8,128)S(1)} %near.1.refs_1_, f32[256,128]{1,0:T(8,128)S(1)} %group.1.refs_2_, bf16[128,128]{1,0:T(8,128)(2,1)S(1)} %copy-done.4, bf16[144,128]{1,0:T(8,128)(2,1)S(1)} %get-tuple-element.20.refs_4_, ...), custom_call_target="tpu_custom_call" | custom-call | flops 200000000 | bytes 600000 | tf_op jit(solution)/shard_map/final/pallas_call | solution.py:361
  (27 shorter events, 0.1 us)
Async XLA Ops:
  0.0 0.8 %copy-start = (bf16[128,128]{1,0:T(8,128)(2,1)S(1)}, bf16[128,128]{1,0:T(8,128)(2,1)}, u32[]{:S(2)}) copy-start(bf16[128,128]{1,0:T(8,128)(2,1)} %param.15) | copy-start | bytes 98308
  0.0 7.5 %copy-start.3 = (bf16[256,128]{1,0:T(8,128)(2,1)S(1)}, bf16[256,128]{1,0:T(8,128)(2,1)}, u32[]{:S(2)}) copy-start(bf16[256,128]{1,0:T(8,128)(2,1)} %chg_ref.1) | copy-start | bytes 196612
  0.0 7.5 %copy-start.7 = (s32[256,4]{0,1:T(4,128)S(1)}, s32[256,4]{0,1:T(4,128)}, u32[]{:S(2)}) copy-start(s32[256,4]{0,1:T(4,128)} %param.18) | copy-start | bytes 12292
  1.8 33.6 %collective-permute-start = (bf16[256,128]{1,0:T(8,128)(2,1)S(1)}, bf16[256,128]{1,0:T(8,128)(2,1)S(1)}, u32[]{:S(2)}, u32[]{:S(2)}) collective-permute-start(bf16[256,128]{1,0:T(8,128)(2,1)S(1)} %convolution_convert_fusion.m_ref), channel_id=1, source_target_pairs={{0,2},{1,3},{2,0},{3,1},{4,6},{5,7},{6,4},{7,5},{8,10},{9,11},{10,... | collective-permute-start | bytes 196616 | tf_op jit(solution)/shard_map/ppermute | solution.py:293
  4.9 30.6 %collective-permute-start.1 = (bf16[256,128]{1,0:T(8,128)(2,1)S(1)}, bf16[256,128]{1,0:T(8,128)(2,1)S(1)}, u32[]{:S(2)}, u32[]{:S(2)}) collective-permute-start(bf16[256,128]{1,0:T(8,128)(2,1)S(1)} %convolution_convert_fusion.m_ref), channel_id=1, source_target_pairs={{0,4},{1,5},{2,6},{3,7},{4,0},{5,1},{6,2},{7,3},{8,12},{9,13},{10,... | collective-permute-start | bytes 196616 | tf_op jit(solution)/shard_map/ppermute | solution.py:293
  7.5 28.0 %collective-permute-start.2 = (bf16[256,128]{1,0:T(8,128)(2,1)S(1)}, bf16[256,128]{1,0:T(8,128)(2,1)S(1)}, u32[]{:S(2)}, u32[]{:S(2)}) collective-permute-start(bf16[256,128]{1,0:T(8,128)(2,1)S(1)} %convolution_convert_fusion.m_ref), channel_id=1, source_target_pairs={{0,6},{1,7},{2,4},{3,5},{4,2},{5,3},{6,0},{7,1},{8,14},{9,15},{10,... | collective-permute-start | bytes 196616 | tf_op jit(solution)/shard_map/ppermute | solution.py:293
  7.5 0.7 %copy-start.9 = (s32[256]{0:T(256)S(1)}, s32[256]{0:T(256)}, u32[]{:S(2)}) copy-start(s32[256]{0:T(256)} %param.13) | copy-start | bytes 3076
  8.2 1.0 %copy-start.2 = (f32[3,256,128]{2,1,0:T(8,128)S(1)}, f32[3,256,128]{2,1,0:T(8,128)}, u32[]{:S(2)}) copy-start(f32[3,256,128]{2,1,0:T(8,128)} %pos_ref.1) | copy-start | bytes 1179652
  9.2 26.5 %copy-start.10 = (s32[256,8]{0,1:T(8,128)S(1)}, s32[256,8]{0,1:T(8,128)}, u32[]{:S(2)}) copy-start(s32[256,8]{0,1:T(8,128)} %param.20) | copy-start | bytes 24580
  9.2 26.5 %copy-start.11 = (s32[256,8]{0,1:T(8,128)S(1)}, s32[256,8]{0,1:T(8,128)}, u32[]{:S(2)}) copy-start(s32[256,8]{0,1:T(8,128)} %param.19) | copy-start | bytes 24580
  35.4 1.1 %copy-start.1 = (bf16[16,128,128]{2,1,0:T(8,128)(2,1)S(1)}, bf16[16,128,128]{2,1,0:T(8,128)(2,1)}, u32[]{:S(2)}) copy-start(bf16[16,128,128]{2,1,0:T(8,128)(2,1)} %param.16) | copy-start | bytes 1572868
  35.6 6.3 %collective-permute-start.3 = (bf16[1024,128]{1,0:T(8,128)(2,1)S(1)}, bf16[1024,128]{1,0:T(8,128)(2,1)S(1)}, u32[]{:S(2)}, u32[]{:S(2)}) collective-permute-start(bf16[1024,128]{1,0:T(8,128)(2,1)S(1)} %constant_dynamic-update-slice_fusion.refs_2_), channel_id=1, source_target_pairs={{0,1},{1,0},{2,3},{3,2},{4,5},{5,4},{6,7},{7,6},{8,9},{9,8},{10,11... | collective-permute-start | bytes 786440 | tf_op jit(solution)/shard_map/ppermute | solution.py:316
  35.8 0.7 %copy-start.6 = (s32[1,1,4,64,4]{3,4,2,1,0:T(4,128)S(1)}, s32[1,1,4,64,4]{3,4,2,1,0:T(4,128)}, u32[]{:S(2)}) copy-start(s32[1,1,4,64,4]{3,4,2,1,0:T(4,128)} %param.22) | copy-start | bytes 12292
  35.9 0.7 %copy-start.5 = (s32[1,1,4,64,4]{3,4,2,1,0:T(4,128)S(1)}, s32[1,1,4,64,4]{3,4,2,1,0:T(4,128)}, u32[]{:S(2)}) copy-start(s32[1,1,4,64,4]{3,4,2,1,0:T(4,128)} %param.21) | copy-start | bytes 12292
  36.0 0.7 %copy-start.8 = (s32[1,1,4,64]{3,2,1,0:T(4,128)S(1)}, s32[1,1,4,64]{3,2,1,0:T(4,128)}, u32[]{:S(2)}) copy-start(s32[1,1,4,64]{3,2,1,0:T(4,128)} %param.23) | copy-start | bytes 3076
  38.3 5.9 %collective-permute-start.4 = (bf16[144,128]{1,0:T(8,128)(2,1)S(1)}, bf16[144,128]{1,0:T(8,128)(2,1)S(1)}, u32[]{:S(2)}, u32[]{:S(2)}) collective-permute-start(bf16[144,128]{1,0:T(8,128)(2,1)S(1)} %get-tuple-element.19), channel_id=1, source_target_pairs={{0,8},{8,0},{16,24},{24,16},{1,9},{9,1},{17,25},{25,17},{2,10},{10... | collective-permute-start | bytes 110600 | tf_op jit(solution)/shard_map/ppermute | solution.py:342
  40.1 4.2 %collective-permute-start.5 = (bf16[144,128]{1,0:T(8,128)(2,1)S(1)}, bf16[144,128]{1,0:T(8,128)(2,1)S(1)}, u32[]{:S(2)}, u32[]{:S(2)}) collective-permute-start(bf16[144,128]{1,0:T(8,128)(2,1)S(1)} %get-tuple-element.18), channel_id=1, source_target_pairs={{0,16},{8,24},{16,0},{24,8},{1,17},{9,25},{17,1},{25,9},{2,18},{10... | collective-permute-start | bytes 110600 | tf_op jit(solution)/shard_map/ppermute | solution.py:342
  41.7 4.9 %copy-start.4 = (bf16[128,128]{1,0:T(8,128)(2,1)S(1)}, bf16[128,128]{1,0:T(8,128)(2,1)}, u32[]{:S(2)}) copy-start(bf16[128,128]{1,0:T(8,128)(2,1)} %refs_3_.1) | copy-start | bytes 98308
  41.7 4.9 %collective-permute-start.6 = (bf16[144,128]{1,0:T(8,128)(2,1)S(1)}, bf16[144,128]{1,0:T(8,128)(2,1)S(1)}, u32[]{:S(2)}, u32[]{:S(2)}) collective-permute-start(bf16[144,128]{1,0:T(8,128)(2,1)S(1)} %get-tuple-element.17), channel_id=1, source_target_pairs={{0,24},{8,16},{16,8},{24,0},{1,25},{9,17},{17,9},{25,1},{2,26},{10... | collective-permute-start | bytes 110600 | tf_op jit(solution)/shard_map/ppermute | solution.py:342

commit v4 on v2

--- a/solution.py
+++ b/solution.py
@@ -59,7 +59,6 @@
     boxes, width = m_ref.shape
     patterns = ops_ref.shape[0] // width
     groups, fanin, slots = src_ref.shape
-    rows = out_ref.shape[1]
     pack = LANES // slots
     tiles = fanin // pack
     m = m_ref[...]
@@ -86,13 +85,14 @@
     result = dot(sums[...], ops_ref[...])
     hi = result.astype(BF16)
     lo = (result - hi.astype(F32)).astype(BF16)
+    box = iota((boxes, slots), 0)
     for d in range(groups):
-        target = tgt_ref[d : d + 1, :].astype(F32)
-        out_ref[d, 0:slots, :] = hi[d * slots : (d + 1) * slots]
-        out_ref[d, slots : 2 * slots, :] = lo[d * slots : (d + 1) * slots]
-        out_ref[d, 2 * slots : rows, :] = jnp.broadcast_to(
-            jnp.concatenate([target, target], axis=1), (rows - 2 * slots, 2 * slots)
-        ).astype(BF16)
+        hit = jnp.where(box == tgt_ref[d : d + 1, :], 1.0, 0.0)
+        hit = jnp.concatenate([hit, hit], axis=1).astype(BF16)
+        part = slice(d * slots, (d + 1) * slots)
+        out_ref[d * boxes : (d + 1) * boxes, :] = dot(
+            hit, jnp.concatenate([hi[part], lo[part]], axis=0)
+        )
 
 
 def near_kernel(nb_ref, cnt_ref, chg_ref, pos_ref, out_ref, feat, right, left):
@@ -151,14 +151,13 @@
         for r in range(8):
             lhs = turned * masks[r]
             acc = None
-            for k in range(0, knear, 2):
-                pair = [nb_ref[k + i, g * 8 + r] for i in range(2)]
-                dist = dot(lhs, jnp.concatenate([operand(b) for b in pair], axis=1))
-                for i in range(2):
-                    shift = feat[6, pl.ds(pair[i], 1), :]
-                    q = feat[7, pl.ds(pair[i], 1), :]
-                    term = lax.rsqrt(dist[:, i * LANES : (i + 1) * LANES] + shift) * q
-                    acc = term if acc is None else acc + term
+            near = [nb_ref[k, g * 8 + r] for k in range(knear)]
+            dist = dot(lhs, jnp.concatenate([operand(b) for b in near], axis=1))
+            for k in range(knear):
+                shift = feat[6, pl.ds(near[k], 1), :]
+                q = feat[7, pl.ds(near[k], 1), :]
+                term = lax.rsqrt(dist[:, k * LANES : (k + 1) * LANES] + shift) * q
+                acc = term if acc is None else acc + term
             total = jnp.sum(acc, axis=1, keepdims=True)
             outs.append(jnp.sum(jnp.where(eye, total, 0.0), axis=0, keepdims=True))
         out_ref[pl.ds(pl.multiple_of(g * 8, 8), 8), :] = jnp.concatenate(outs, axis=0)
@@ -167,24 +166,17 @@
     lax.fori_loop(0, boxes // 8, group, 0, unroll=2)
 
 
-def group_kernel(*refs, blocks, fanin):
-    code_ref, ops_ref, mine_ref, other_ref, out_ref, sums = refs
-    width = mine_ref.shape[1]
-    boxes = mine_ref.shape[0] // (blocks // 2)
+def far_kernel(
+    code_ref, cnt_ref, near_ref, remote_ref, ops_ref, eval_ref, all_ref, out_ref, sums, *, fanin
+):
+    boxes, width = out_ref.shape
+    sources = all_ref.shape[0]
     patterns = ops_ref.shape[0] // width
     per = LANES // fanin
     tiles = code_ref.shape[0]
     span = 2 * boxes
-    pages = blocks // 2
-    table = jnp.concatenate(
-        [
-            jnp.concatenate(
-                [mine_ref[j * boxes : (j + 1) * boxes], other_ref[j * boxes : (j + 1) * boxes]], axis=0
-            )
-            for j in range(pages)
-        ],
-        axis=1,
-    )
+    pages = sources // span
+    table = jnp.concatenate([all_ref[j * span : (j + 1) * span] for j in range(pages)], axis=1)
     codes = code_ref[...]
     cols = code_columns(codes)
     eye = iota((per, LANES), 0) == (iota((per, LANES), 1) >> log2(fanin))
@@ -201,29 +193,13 @@
             got = part[:, 0:width]
             for j in range(1, pages):
                 got = jnp.where(page == j, part[:, j * width : (j + 1) * width], got)
-            pat = pattern_matrix(codes[i : i + 1, :] >> log2(blocks * boxes), eye, patterns)
+            pat = pattern_matrix(codes[i : i + 1, :] >> log2(sources), eye, patterns)
             s = dot(pat, got.astype(BF16)).astype(BF16)
             for p in range(patterns):
                 sums[i * per : (i + 1) * per, p * width : (p + 1) * width] = s[
                     p * per : (p + 1) * per
                 ]
-    out_ref[...] = dot(sums[...], ops_ref[...])
-
-
-def final_kernel(*refs):
-    cnt_ref, near_ref, local_ref, eval_ref = refs[:4]
-    pay_refs = refs[4:-1]
-    out_ref = refs[-1]
-    boxes = local_ref.shape[0]
-    hits = []
-    values = []
-    for pay in pay_refs:
-        depth = pay.shape[0] - 16
-        target = pay[depth : depth + 16, :].astype(F32)[0:1]
-        box = iota((boxes, depth), 0).astype(F32)
-        hits.append(jnp.where(box == target, 1.0, 0.0).astype(BF16))
-        values.append(pay[0:depth, :])
-    local = local_ref[...] + dot(jnp.concatenate(hits, axis=1), jnp.concatenate(values, axis=0))
+    local = dot(sums[...], ops_ref[...]) + remote_ref[...]
     far = dot(local.astype(BF16), eval_ref[...])
     total = near_ref[...] * (1.0 / (4.0 * math.pi)) + far
     live = iota((boxes, LANES), 1) < count_columns(cnt_ref, boxes)
@@ -261,11 +237,28 @@
     strength = jnp.where(live, charges, jnp.zeros_like(charges))
     multipole = jnp.dot(strength, moment_map, preferred_element_type=F32).astype(BF16)
 
-    me = lax.axis_index("cube")
-    along = [multipole] + [
-        lax.ppermute(multipole, "cube", [(i, i ^ k) for i in range(n_cube)])
-        for k in range(2, n_cube, 2)
-    ]
+    gathered = lax.all_gather(multipole, "cube", axis=0, tiled=True)
+
+    slots, fanin = remote_sources.shape[3:]
+    sent = pl.pallas_call(
+        slot_kernel,
+        out_shape=jax.ShapeDtypeStruct((n_oct * boxes, width), F32),
+        in_specs=[VMEM] * 5,
+        out_specs=VMEM,
+        scratch_shapes=[pltpu.VMEM((n_oct * slots, patterns * width), BF16)],
+        compiler_params=pltpu.CompilerParams(vmem_limit_bytes=16 * MIB),
+        cost_estimate=pl.CostEstimate(
+            flops=1_000_000_000, bytes_accessed=1_000_000, transcendentals=0
+        ),
+        name="slots",
+    )(
+        multipole,
+        remote_sources[0, 0].transpose(0, 2, 1),
+        remote_patterns[0, 0].transpose(0, 2, 1),
+        remote_targets[0, 0],
+        operators,
+    )
+    remote_local = lax.psum_scatter(sent, "oct", scatter_dimension=0, tiled=True)
 
     near = pl.pallas_call(
         near_kernel,
@@ -284,64 +277,21 @@
         name="near",
     )(near_boxes.T, counts, charges, positions)
 
-    near, base, *along = lax.optimization_barrier((near, multipole, *along))
-    mine = jnp.concatenate(along, axis=0)
-    other = lax.ppermute(mine, "cube", [(i, i ^ 1) for i in range(n_cube)])
-
-    slots, fanin = remote_sources.shape[3:]
-    sent = pl.pallas_call(
-        slot_kernel,
-        out_shape=jax.ShapeDtypeStruct((n_oct, 2 * slots + 16, width), BF16),
-        in_specs=[VMEM] * 5,
-        out_specs=VMEM,
-        scratch_shapes=[pltpu.VMEM((n_oct * slots, patterns * width), BF16)],
-        compiler_params=pltpu.CompilerParams(vmem_limit_bytes=16 * MIB),
-        cost_estimate=pl.CostEstimate(
-            flops=1_000_000_000, bytes_accessed=1_000_000, transcendentals=0
-        ),
-        name="slots",
-    )(
-        base,
-        remote_sources[0, 0].transpose(0, 2, 1),
-        remote_patterns[0, 0].transpose(0, 2, 1),
-        remote_targets[0, 0],
-        operators,
-    )
-    octant = lax.axis_index("oct")
-    payloads = []
-    for k in range(n_oct):
-        part = lax.dynamic_index_in_dim(sent, octant ^ k, 0, keepdims=False)
-        if k > 0:
-            part = lax.ppermute(part, "oct", [(i, i ^ k) for i in range(n_oct)])
-        payloads.append(part)
-
     klist = group_sources.shape[1]
-    group = n_cube * boxes
-    code = (group_sources ^ (me * boxes)) + group * group_patterns
-    near_local = pl.pallas_call(
-        functools.partial(group_kernel, blocks=n_cube, fanin=klist),
-        out_shape=jax.ShapeDtypeStruct((boxes, width), F32),
-        in_specs=[VMEM] * 4,
+    code = group_sources + (n_cube * boxes) * group_patterns
+    near, gathered, remote_local = lax.optimization_barrier((near, gathered, remote_local))
+    return pl.pallas_call(
+        functools.partial(far_kernel, fanin=klist),
+        out_shape=jax.ShapeDtypeStruct((boxes, panels), F32),
+        in_specs=[VMEM] * 7,
         out_specs=VMEM,
         scratch_shapes=[pltpu.VMEM((boxes, patterns * width), BF16)],
         compiler_params=pltpu.CompilerParams(vmem_limit_bytes=24 * MIB),
         cost_estimate=pl.CostEstimate(
             flops=3_000_000_000, bytes_accessed=2_000_000, transcendentals=0
         ),
-        name="group",
-    )(code.reshape(-1, LANES), operators, mine, other)
-
-    return pl.pallas_call(
-        final_kernel,
-        out_shape=jax.ShapeDtypeStruct((boxes, panels), F32),
-        in_specs=[VMEM] * (4 + n_oct),
-        out_specs=VMEM,
-        compiler_params=pltpu.CompilerParams(vmem_limit_bytes=16 * MIB),
-        cost_estimate=pl.CostEstimate(
-            flops=200_000_000, bytes_accessed=600_000, transcendentals=0
-        ),
-        name="final",
-    )(counts, near, near_local, evaluation, *payloads)
+        name="far",
+    )(code.reshape(-1, LANES), counts, near, remote_local, operators, evaluation, gathered)
 
 
 def solution(mesh):

time: 40.2 us -> 60.3 us (1.50)
  blocking collectives: 0 us -> 16.7 us
  between operations: 0.21 us -> 13.5 us
  starting transfers between devices: 9.3 us -> 0.01 us
  waiting for transfers between devices: 2.19 us -> 0.04 us
  local copies, waits for them, and re-layouts: 3.47 us -> 4.32 us
  Pallas kernels: 23.6 us -> 24.3 us
    all_gather x0 -> x1, blocking collectives: none -> 16.7 us  [body(): gathered = lax.all_gather(multipole, 'cube', axis=0, tiled=True)]
    ppermute x7 -> x0, starting transfers between devices: 9.3 us -> none  [the longest x3 5.68 us: body(): lax.ppermute(multipole, 'cube', [(i, i ^ k) for i in range(n_cube)])]
    ppermute x7 -> x0, waiting for transfers between devices: 2.19 us -> none  [the longest x3 2.18 us: body(): part = lax.ppermute(part, 'oct', [(i, i ^ k) for i in range(n_oct)])]
    unnamed x27 -> x28, local copies, waits for them, and re-layouts: 3.2 us -> 4.09 us
    pallas_call x3 -> x2, Pallas kernels: 5 us -> 5.67 us  [the longest x1 3.11 us: body(): pl.pallas_call(functools.partial(far_kernel, fanin=klist), out_shape=jax....]
  transfers between devices with their start and end apart: 7 -> 1, of which waited for: 1 -> 0; matrix products, arithmetic and copies ran while one was open for 1% -> 0% of each run, Pallas kernels for 57% -> 31%
where the time goes in v4:
time: 60.3 us; the launch traced here: 59.9 us
  Pallas kernels  24.3 us (40%)
  blocking collectives  16.7 us (28%)
  between operations  13.5 us (22%)
  local copies, waits for them, and re-layouts  4.32 us (7%)
  matrix products  1.06 us (2%)
    pallas_call x1, Pallas kernels, body(): pl.pallas_call(near_kernel, out_shape=jax.ShapeDtypeStruct((boxes, panels...  18.6 us
    all_gather x1, blocking collectives, body(): gathered = lax.all_gather(multipole, 'cube', axis=0, tiled=True)  16.7 us
    unnamed x28, local copies, waits for them, and re-layouts  4.09 us
    pallas_call x1, Pallas kernels, body(): pl.pallas_call(functools.partial(far_kernel, fanin=klist), out_shape=jax....  3.11 us
    pallas_call x1, Pallas kernels, body(): pl.pallas_call(slot_kernel, out_shape=jax.ShapeDtypeStruct((n_oct * boxes...  2.56 us
  transfers between devices with their start and end apart: 1, of which 0 were waited for; matrix products, arithmetic and copies ran while one was open for 0% of the time, Pallas kernels for 31%

profile of v4, /device:TPU:0, one launch (start us, length us, event | category | flops | bytes accessed | tf_op | source)
XLA Modules:
  0.0 59.9 jit_solution(8047314160712934907)
XLA Ops:
  6.5 0.7 %copy-done = bf16[128,128]{1,0:T(8,128)(2,1)S(1)} copy-done((bf16[128,128]{1,0:T(8,128)(2,1)S(1)}, bf16[128,128]{1,0:T(8,128)(2,1)}, u32[]{:S(2)}) %copy-start) | copy-done | bytes 32792
  7.3 1.1 %convolution_convert_fusion.m_ref = bf16[256,128]{1,0:T(8,128)(2,1)S(1)} fusion(bf16[128,128]{1,0:T(8,128)(2,1)S(1)} %copy-done, bf16[256,128]{1,0:T(8,128)(2,1)} %chg_ref.1, s32[256]{0:T(256)} %param.13), kind=kOutput, calls=%fused_computation | convolution fusion | flops 8486912 | bytes 164864 | tf_op jit(solution)/shard_map/dot_general | solution.py:238
  8.4 0.0 copy-start.10
  8.4 0.7 %copy-done.10 = s32[1,1,4,64]{3,2,1,0:T(4,128)S(1)} copy-done((s32[1,1,4,64]{3,2,1,0:T(4,128)S(1)}, s32[1,1,4,64]{3,2,1,0:T(4,128)}, u32[]{:S(2)}) %copy-start.10) | copy-done | bytes 1048
  9.0 1.0 %copy-done.1 = bf16[16,128,128]{2,1,0:T(8,128)(2,1)S(1)} copy-done((bf16[16,128,128]{2,1,0:T(8,128)(2,1)S(1)}, bf16[16,128,128]{2,1,0:T(8,128)(2,1)}, u32[]{:S(2)}) %copy-start.1) | copy-done | bytes 524312
  10.1 2.6 %slots.1 = f32[1024,128]{1,0:T(8,128)} custom-call(bf16[256,128]{1,0:T(8,128)(2,1)S(1)} %convolution_convert_fusion.m_ref, s32[4,4,64]{2,1,0:T(4,128)S(1)} %bitcast.13, s32[4,4,64]{2,1,0:T(4,128)S(1)} %bitcast.14, s32[4,64]{1,0:T(4,128)S(1)} %bitcast.16, bf16[2048,128]{1,0:T(8,128)(2,1)S(1)} %bitcast.11), custom_call_target="tpu_custom_call" | custom-call | flops 1000000000 | bytes 1000000 | tf_op jit(solution)/shard_map/slots/pallas_call | solution.py:243
  12.6 0.0 reduce-scatter.2.cloned.1.call-update
  12.7 0.0 copy-start.12
  12.7 0.0 copy-start.13
  12.7 0.0 copy-start.3
  12.7 16.7 %all_gather.3.all_ref = bf16[2048,128]{1,0:T(8,128)(2,1)S(1)} all-gather(bf16[256,128]{1,0:T(8,128)(2,1)S(1)} %convolution_convert_fusion.m_ref), channel_id=1, replica_groups=mesh['oct'=4,'cube'=8] {'cube'}, dimensions={0}, use_global_device_ids=true | all-gather | bytes 589824 | tf_op jit(solution)/shard_map/all_gather | solution.py:240
  29.4 0.0 copy-done.12
  29.4 0.1 copy.14
  29.6 0.0 copy-start.5
  29.6 0.0 copy-start.9
  29.6 0.1 reshape.10.code_ref
  29.7 0.0 copy-start.11
  29.7 0.7 %copy-done.5 = bf16[256,128]{1,0:T(8,128)(2,1)S(1)} copy-done((bf16[256,128]{1,0:T(8,128)(2,1)S(1)}, bf16[256,128]{1,0:T(8,128)(2,1)}, u32[]{:S(2)}) %copy-start.5) | copy-done | bytes 65560
  30.4 18.6 %near.1.near_ref = f32[256,128]{1,0:T(8,128)S(1)} custom-call(s32[4,256]{1,0:T(4,128)S(1)} %bitcast.15, s32[2,128]{1,0:T(2,128)S(1)} %bitcast.17, bf16[256,128]{1,0:T(8,128)(2,1)S(1)} %copy-done.5, f32[3,256,128]{2,1,0:T(8,128)S(1)} %copy-done.3), custom_call_target="tpu_custom_call" | custom-call | flops 15000000512 | bytes 1000000 | tf_op jit(solution)/shard_map/near/pallas_call | solution.py:263
  49.0 0.0 reduce-scatter.2.cloned.1.call-done.remote_ref
  49.1 0.0 copy-done.2
  49.1 0.0 copy-done.6
  49.1 0.9 %copy-done.4 = f32[256,128]{1,0:T(8,128)S(1)} copy-done((f32[256,128]{1,0:T(8,128)S(1)}, f32[256,128]{1,0:T(8,128)}, u32[]{:S(2)}) %copy-start.4) | copy-done | bytes 131096
  50.0 3.1 %far.1 = f32[256,128]{1,0:T(8,128)} custom-call(s32[16,128]{1,0:T(8,128)S(1)} %reshape.10.code_ref, s32[2,128]{1,0:T(2,128)S(1)} %bitcast.18, f32[256,128]{1,0:T(8,128)S(1)} %near.1.near_ref, f32[256,128]{1,0:T(8,128)S(1)} %copy-done.4, bf16[2048,128]{1,0:T(8,128)(2,1)S(1)} %bitcast.12, bf16[128,128]{1,0:T(8,128)(2,1)S(1)} %copy-done.6, ...), custom_call_target="tpu_custom_call" | custom-call | flops 3000000000 | bytes 2000000 | tf_op jit(solution)/shard_map/far/pallas_call | solution.py:283
  (15 shorter events, 0.0 us)
Async XLA Ops:
  6.5 0.8 %copy-start = (bf16[128,128]{1,0:T(8,128)(2,1)S(1)}, bf16[128,128]{1,0:T(8,128)(2,1)}, u32[]{:S(2)}) copy-start(bf16[128,128]{1,0:T(8,128)(2,1)} %param.15) | copy-start | bytes 98308
  6.5 1.8 %copy-start.8 = (s32[1,1,4,64,4]{3,4,2,1,0:T(4,128)S(1)}, s32[1,1,4,64,4]{3,4,2,1,0:T(4,128)}, u32[]{:S(2)}) copy-start(s32[1,1,4,64,4]{3,4,2,1,0:T(4,128)} %param.22) | copy-start | bytes 12292
  6.5 1.8 %copy-start.7 = (s32[1,1,4,64,4]{3,4,2,1,0:T(4,128)S(1)}, s32[1,1,4,64,4]{3,4,2,1,0:T(4,128)}, u32[]{:S(2)}) copy-start(s32[1,1,4,64,4]{3,4,2,1,0:T(4,128)} %param.21) | copy-start | bytes 12292
  6.5 42.5 %reduce-scatter.2.cloned.1.call-start = ((), (), s32[]{:S(2)}) async-start(), calls=%async_computation.1 | async-start | bytes 655360 | tf_op jit(solution)/shard_map/reduce_scatter | solution.py:261
  8.4 0.7 %copy-start.10 = (s32[1,1,4,64]{3,2,1,0:T(4,128)S(1)}, s32[1,1,4,64]{3,2,1,0:T(4,128)}, u32[]{:S(2)}) copy-start(s32[1,1,4,64]{3,2,1,0:T(4,128)} %param.23) | copy-start | bytes 3076
  9.0 1.0 %copy-start.1 = (bf16[16,128,128]{2,1,0:T(8,128)(2,1)S(1)}, bf16[16,128,128]{2,1,0:T(8,128)(2,1)}, u32[]{:S(2)}) copy-start(bf16[16,128,128]{2,1,0:T(8,128)(2,1)} %param.16) | copy-start | bytes 1572868
  12.7 16.7 %copy-start.12 = (s32[256,8]{0,1:T(8,128)S(1)}, s32[256,8]{0,1:T(8,128)}, u32[]{:S(2)}) copy-start(s32[256,8]{0,1:T(8,128)} %param.19) | copy-start | bytes 24580
  12.7 16.7 %copy-start.13 = (s32[256,8]{0,1:T(8,128)S(1)}, s32[256,8]{0,1:T(8,128)}, u32[]{:S(2)}) copy-start(s32[256,8]{0,1:T(8,128)} %param.20) | copy-start | bytes 24580
  12.7 17.0 %copy-start.3 = (f32[3,256,128]{2,1,0:T(8,128)S(1)}, f32[3,256,128]{2,1,0:T(8,128)}, u32[]{:S(2)}) copy-start(f32[3,256,128]{2,1,0:T(8,128)} %pos_ref.1) | copy-start | bytes 1179652
  29.6 0.8 %copy-start.5 = (bf16[256,128]{1,0:T(8,128)(2,1)S(1)}, bf16[256,128]{1,0:T(8,128)(2,1)}, u32[]{:S(2)}) copy-start(bf16[256,128]{1,0:T(8,128)(2,1)} %chg_ref.1) | copy-start | bytes 196612
  29.6 0.8 %copy-start.9 = (s32[256,4]{0,1:T(4,128)S(1)}, s32[256,4]{0,1:T(4,128)}, u32[]{:S(2)}) copy-start(s32[256,4]{0,1:T(4,128)} %param.18) | copy-start | bytes 12292
  29.7 0.7 %copy-start.11 = (s32[256]{0:T(256)S(1)}, s32[256]{0:T(256)}, u32[]{:S(2)}) copy-start(s32[256]{0:T(256)} %param.13) | copy-start | bytes 3076
  30.4 18.7 %copy-start.2 = (bf16[16,128,128]{2,1,0:T(8,128)(2,1)S(1)}, bf16[16,128,128]{2,1,0:T(8,128)(2,1)}, u32[]{:S(2)}) copy-start(bf16[16,128,128]{2,1,0:T(8,128)(2,1)} %param.16) | copy-start | bytes 1572868
  30.4 18.7 %copy-start.6 = (bf16[128,128]{1,0:T(8,128)(2,1)S(1)}, bf16[128,128]{1,0:T(8,128)(2,1)}, u32[]{:S(2)}) copy-start(bf16[128,128]{1,0:T(8,128)(2,1)} %eval_ref.1) | copy-start | bytes 98308
  49.1 0.9 %copy-start.4 = (f32[256,128]{1,0:T(8,128)S(1)}, f32[256,128]{1,0:T(8,128)}, u32[]{:S(2)}) copy-start(f32[256,128]{1,0:T(8,128)} %reduce-scatter.2.cloned.1.call-done.remote_ref) | copy-start | bytes 393220
Sparse Core Ops, SparseCore 0:
  12.8 27.5 reduce-scatter.1

commit v5 on v2

--- a/solution.py
+++ b/solution.py
@@ -133,12 +133,14 @@
                 ).astype(BF16)
         return carry
 
-    lax.fori_loop(0, boxes // 8, build, 0)
+    lax.fori_loop(0, boxes // 8, build, 0, unroll=4)
 
     masks = [
         jnp.where((iota((LANES, LANES), 1) & 7) == j, 1.0, 0.0).astype(BF16) for j in range(8)
     ]
-    eye = iota((LANES, LANES), 0) == iota((LANES, LANES), 1)
+    select = [
+        jnp.where(iota((16, 2 * LANES), 0) == j, 1.0, 0.0).astype(BF16) for j in range(8)
+    ]
     ones = jnp.where(iota((32, LANES), 0) < 24, 1.0, 0.0).astype(BF16)
 
     def operand(box):
@@ -147,7 +149,7 @@
 
     def group(g, carry):
         turned = left[g]
-        outs = []
+        out = jnp.zeros((16, LANES), F32)
         for r in range(8):
             lhs = turned * masks[r]
             acc = None
@@ -159,9 +161,15 @@
                     q = feat[7, pl.ds(pair[i], 1), :]
                     term = lax.rsqrt(dist[:, i * LANES : (i + 1) * LANES] + shift) * q
                     acc = term if acc is None else acc + term
-            total = jnp.sum(acc, axis=1, keepdims=True)
-            outs.append(jnp.sum(jnp.where(eye, total, 0.0), axis=0, keepdims=True))
-        out_ref[pl.ds(pl.multiple_of(g * 8, 8), 8), :] = jnp.concatenate(outs, axis=0)
+            hi = acc.astype(BF16)
+            lo = (acc - hi.astype(F32)).astype(BF16)
+            out = out + lax.dot_general(
+                select[r],
+                jnp.concatenate([hi, lo], axis=1),
+                (((1,), (1,)), ((), ())),
+                preferred_element_type=F32,
+            )
+        out_ref[pl.ds(pl.multiple_of(g * 8, 8), 8), :] = out[0:8]
         return carry
 
     lax.fori_loop(0, boxes // 8, group, 0, unroll=2)

time: 40.2 us -> 58.9 us (1.47)
  Pallas kernels: 23.6 us -> 42.4 us
    pallas_call x1, Pallas kernels: 18.6 us -> 37.4 us  [body(): pl.pallas_call(near_kernel, out_shape=jax.ShapeDtypeStruct((boxes, panels...]
  transfers between devices with their start and end apart: 7 -> 7, of which waited for: 1 -> 1; matrix products, arithmetic and copies ran while one was open for 1% -> 0% of each run, Pallas kernels for 57% -> 70%
where the time goes in v5:
time: 58.9 us; the launch traced here: 58.7 us
  Pallas kernels  42.4 us (72%)
  starting transfers between devices  9.3 us (16%)
  local copies, waits for them, and re-layouts  3.47 us (6%)
  waiting for transfers between devices  2.24 us (4%)
  matrix products  1.06 us (2%)
    pallas_call x1, Pallas kernels, body(): pl.pallas_call(near_kernel, out_shape=jax.ShapeDtypeStruct((boxes, panels...  37.4 us
    ppermute x3, starting transfers between devices, body(): lax.ppermute(multipole, 'cube', [(i, i ^ k) for i in range(n_cube)])  5.68 us
    ppermute x3, starting transfers between devices, body(): part = lax.ppermute(part, 'oct', [(i, i ^ k) for i in range(n_oct)])  3.55 us
    unnamed x27, local copies, waits for them, and re-layouts  3.2 us
    pallas_call x1, Pallas kernels, body(): pl.pallas_call(functools.partial(group_kernel, blocks=n_cube, fanin=klist...  2.36 us
    ppermute x3, waiting for transfers between devices, body(): part = lax.ppermute(part, 'oct', [(i, i ^ k) for i in range(n_oct)])  2.23 us
    pallas_call x1, Pallas kernels, body(): pl.pallas_call(slot_kernel, out_shape=jax.ShapeDtypeStruct((n_oct, 2 * sl...  1.59 us
  transfers between devices with their start and end apart: 7, of which 1 were waited for; matrix products, arithmetic and copies ran while one was open for 0% of the time, Pallas kernels for 70%

profile of v5, /device:TPU:0, one launch (start us, length us, event | category | flops | bytes accessed | tf_op | source)
XLA Modules:
  0.0 58.7 jit_solution(9476033547497936664)
XLA Ops:
  0.0 0.8 %copy-done = bf16[128,128]{1,0:T(8,128)(2,1)S(1)} copy-done((bf16[128,128]{1,0:T(8,128)(2,1)S(1)}, bf16[128,128]{1,0:T(8,128)(2,1)}, u32[]{:S(2)}) %copy-start) | copy-done | bytes 32792
  0.8 1.1 %convolution_convert_fusion.m_ref = bf16[256,128]{1,0:T(8,128)(2,1)S(1)} fusion(bf16[128,128]{1,0:T(8,128)(2,1)S(1)} %copy-done, bf16[256,128]{1,0:T(8,128)(2,1)} %chg_ref.1, s32[256]{0:T(256)} %param.13), kind=kOutput, calls=%fused_computation | convolution fusion | flops 8486912 | bytes 164864 | tf_op jit(solution)/shard_map/dot_general | solution.py:270
  1.8 3.1 %collective-permute-start = (bf16[256,128]{1,0:T(8,128)(2,1)S(1)}, bf16[256,128]{1,0:T(8,128)(2,1)S(1)}, u32[]{:S(2)}, u32[]{:S(2)}) collective-permute-start(bf16[256,128]{1,0:T(8,128)(2,1)S(1)} %convolution_convert_fusion.m_ref), channel_id=1, source_target_pairs={{0,2},{1,3},{2,0},{3,1},{4,6},{5,7},{6,4},{7,5},{8,10},{9,11},{10,... | collective-permute-start | bytes 196616 | tf_op jit(solution)/shard_map/ppermute | solution.py:274
  4.9 2.6 %collective-permute-start.1 = (bf16[256,128]{1,0:T(8,128)(2,1)S(1)}, bf16[256,128]{1,0:T(8,128)(2,1)S(1)}, u32[]{:S(2)}, u32[]{:S(2)}) collective-permute-start(bf16[256,128]{1,0:T(8,128)(2,1)S(1)} %convolution_convert_fusion.m_ref), channel_id=1, source_target_pairs={{0,4},{1,5},{2,6},{3,7},{4,0},{5,1},{6,2},{7,3},{8,12},{9,13},{10,... | collective-permute-start | bytes 196616 | tf_op jit(solution)/shard_map/ppermute | solution.py:274
  7.5 0.7 %copy-done.9 = s32[256]{0:T(256)S(1)} copy-done((s32[256]{0:T(256)S(1)}, s32[256]{0:T(256)}, u32[]{:S(2)}) %copy-start.9) | copy-done | bytes 1048
  8.2 1.0 %copy-done.2 = f32[3,256,128]{2,1,0:T(8,128)S(1)} copy-done((f32[3,256,128]{2,1,0:T(8,128)S(1)}, f32[3,256,128]{2,1,0:T(8,128)}, u32[]{:S(2)}) %copy-start.2) | copy-done | bytes 393240
  9.2 37.4 %near.1.refs_1_ = f32[256,128]{1,0:T(8,128)S(1)} custom-call(s32[4,256]{1,0:T(4,128)S(1)} %bitcast.23, s32[2,128]{1,0:T(2,128)S(1)} %bitcast.25, bf16[256,128]{1,0:T(8,128)(2,1)S(1)} %copy-done.3, f32[3,256,128]{2,1,0:T(8,128)S(1)} %copy-done.2), custom_call_target="tpu_custom_call" | custom-call | flops 15000000512 | bytes 1000000 | tf_op jit(solution)/shard_map/near/pallas_call | solution.py:278
  46.6 0.0 collective-permute-done.1
  46.7 0.1 collective-permute-start.3
  46.8 0.1 copy.14
  47.0 0.0 copy-start.6
  47.0 0.1 reshape.11.refs_0_
  47.1 0.0 copy-start.8
  47.1 0.5 copy-done.1
  47.6 0.0 copy-done.6
  47.7 0.1 copy-done.5
  47.8 0.0 copy-done.8
  47.8 1.6 %slots.1 = bf16[4,144,128]{2,1,0:T(8,128)(2,1)S(1)} custom-call(bf16[256,128]{1,0:T(8,128)(2,1)S(1)} %convolution_convert_fusion.m_ref, s32[4,4,64]{2,1,0:T(4,128)S(1)} %bitcast.21, s32[4,4,64]{2,1,0:T(4,128)S(1)} %bitcast.22, s32[4,64]{1,0:T(4,128)S(1)} %bitcast.24, bf16[2048,128]{1,0:T(8,128)(2,1)S(1)} %bitcast.19), custom_call_target="tpu_custom_call" | custom-call | flops 1000000000 | bytes 1000000 | tf_op jit(solution)/shard_map/slots/pallas_call | solution.py:300
  49.5 1.8 %collective-permute-start.4 = (bf16[144,128]{1,0:T(8,128)(2,1)S(1)}, bf16[144,128]{1,0:T(8,128)(2,1)S(1)}, u32[]{:S(2)}, u32[]{:S(2)}) collective-permute-start(bf16[144,128]{1,0:T(8,128)(2,1)S(1)} %get-tuple-element.19), channel_id=1, source_target_pairs={{0,8},{8,0},{16,24},{24,16},{1,9},{9,1},{17,25},{25,17},{2,10},{10... | collective-permute-start | bytes 110600 | tf_op jit(solution)/shard_map/ppermute | solution.py:323
  51.2 1.5 %collective-permute-start.5 = (bf16[144,128]{1,0:T(8,128)(2,1)S(1)}, bf16[144,128]{1,0:T(8,128)(2,1)S(1)}, u32[]{:S(2)}, u32[]{:S(2)}) collective-permute-start(bf16[144,128]{1,0:T(8,128)(2,1)S(1)} %get-tuple-element.18), channel_id=1, source_target_pairs={{0,16},{8,24},{16,0},{24,8},{1,17},{9,25},{17,1},{25,9},{2,18},{10... | collective-permute-start | bytes 110600 | tf_op jit(solution)/shard_map/ppermute | solution.py:323
  52.8 0.2 collective-permute-start.6
  53.0 2.4 %group.1.refs_2_ = f32[256,128]{1,0:T(8,128)S(1)} custom-call(s32[16,128]{1,0:T(8,128)S(1)} %reshape.11.refs_0_, bf16[2048,128]{1,0:T(8,128)(2,1)S(1)} %bitcast.20, bf16[1024,128]{1,0:T(8,128)(2,1)S(1)} %constant_dynamic-update-slice_fusion.refs_2_, bf16[1024,128]{1,0:T(8,128)(2,1)S(1)} %collective-permute-done.3.refs_3_), custom_call_target="tpu_custom_call" | custom-call | flops 3000000000 | bytes 2000000 | tf_op jit(solution)/shard_map/group/pallas_call | solution.py:329
  55.4 2.2 %collective-permute-done.6.refs_7_ = bf16[144,128]{1,0:T(8,128)(2,1)S(1)} collective-permute-done((bf16[144,128]{1,0:T(8,128)(2,1)S(1)}, bf16[144,128]{1,0:T(8,128)(2,1)S(1)}, u32[]{:S(2)}, u32[]{:S(2)}) %collective-permute-start.6) | collective-permute-done | bytes 36896 | tf_op jit(solution)/shard_map/ppermute | solution.py:323
  57.6 1.0 %final.1 = f32[256,128]{1,0:T(8,128)} custom-call(s32[2,128]{1,0:T(2,128)S(1)} %bitcast.26, f32[256,128]{1,0:T(8,128)S(1)} %near.1.refs_1_, f32[256,128]{1,0:T(8,128)S(1)} %group.1.refs_2_, bf16[128,128]{1,0:T(8,128)(2,1)S(1)} %copy-done.4, bf16[144,128]{1,0:T(8,128)(2,1)S(1)} %get-tuple-element.20.refs_4_, ...), custom_call_target="tpu_custom_call" | custom-call | flops 200000000 | bytes 600000 | tf_op jit(solution)/shard_map/final/pallas_call | solution.py:342
  (27 shorter events, 0.1 us)
Async XLA Ops:
  0.0 0.8 %copy-start = (bf16[128,128]{1,0:T(8,128)(2,1)S(1)}, bf16[128,128]{1,0:T(8,128)(2,1)}, u32[]{:S(2)}) copy-start(bf16[128,128]{1,0:T(8,128)(2,1)} %param.15) | copy-start | bytes 98308
  0.0 7.5 %copy-start.3 = (bf16[256,128]{1,0:T(8,128)(2,1)S(1)}, bf16[256,128]{1,0:T(8,128)(2,1)}, u32[]{:S(2)}) copy-start(bf16[256,128]{1,0:T(8,128)(2,1)} %chg_ref.1) | copy-start | bytes 196612
  0.0 7.5 %copy-start.7 = (s32[256,4]{0,1:T(4,128)S(1)}, s32[256,4]{0,1:T(4,128)}, u32[]{:S(2)}) copy-start(s32[256,4]{0,1:T(4,128)} %param.18) | copy-start | bytes 12292
  1.8 44.8 %collective-permute-start = (bf16[256,128]{1,0:T(8,128)(2,1)S(1)}, bf16[256,128]{1,0:T(8,128)(2,1)S(1)}, u32[]{:S(2)}, u32[]{:S(2)}) collective-permute-start(bf16[256,128]{1,0:T(8,128)(2,1)S(1)} %convolution_convert_fusion.m_ref), channel_id=1, source_target_pairs={{0,2},{1,3},{2,0},{3,1},{4,6},{5,7},{6,4},{7,5},{8,10},{9,11},{10,... | collective-permute-start | bytes 196616 | tf_op jit(solution)/shard_map/ppermute | solution.py:274
  4.9 41.7 %collective-permute-start.1 = (bf16[256,128]{1,0:T(8,128)(2,1)S(1)}, bf16[256,128]{1,0:T(8,128)(2,1)S(1)}, u32[]{:S(2)}, u32[]{:S(2)}) collective-permute-start(bf16[256,128]{1,0:T(8,128)(2,1)S(1)} %convolution_convert_fusion.m_ref), channel_id=1, source_target_pairs={{0,4},{1,5},{2,6},{3,7},{4,0},{5,1},{6,2},{7,3},{8,12},{9,13},{10,... | collective-permute-start | bytes 196616 | tf_op jit(solution)/shard_map/ppermute | solution.py:274
  7.5 39.1 %collective-permute-start.2 = (bf16[256,128]{1,0:T(8,128)(2,1)S(1)}, bf16[256,128]{1,0:T(8,128)(2,1)S(1)}, u32[]{:S(2)}, u32[]{:S(2)}) collective-permute-start(bf16[256,128]{1,0:T(8,128)(2,1)S(1)} %convolution_convert_fusion.m_ref), channel_id=1, source_target_pairs={{0,6},{1,7},{2,4},{3,5},{4,2},{5,3},{6,0},{7,1},{8,14},{9,15},{10,... | collective-permute-start | bytes 196616 | tf_op jit(solution)/shard_map/ppermute | solution.py:274
  7.5 0.7 %copy-start.9 = (s32[256]{0:T(256)S(1)}, s32[256]{0:T(256)}, u32[]{:S(2)}) copy-start(s32[256]{0:T(256)} %param.13) | copy-start | bytes 3076
  8.2 1.0 %copy-start.2 = (f32[3,256,128]{2,1,0:T(8,128)S(1)}, f32[3,256,128]{2,1,0:T(8,128)}, u32[]{:S(2)}) copy-start(f32[3,256,128]{2,1,0:T(8,128)} %pos_ref.1) | copy-start | bytes 1179652
  9.2 37.6 %copy-start.10 = (s32[256,8]{0,1:T(8,128)S(1)}, s32[256,8]{0,1:T(8,128)}, u32[]{:S(2)}) copy-start(s32[256,8]{0,1:T(8,128)} %param.20) | copy-start | bytes 24580
  9.2 37.6 %copy-start.11 = (s32[256,8]{0,1:T(8,128)S(1)}, s32[256,8]{0,1:T(8,128)}, u32[]{:S(2)}) copy-start(s32[256,8]{0,1:T(8,128)} %param.19) | copy-start | bytes 24580
  46.6 1.1 %copy-start.1 = (bf16[16,128,128]{2,1,0:T(8,128)(2,1)S(1)}, bf16[16,128,128]{2,1,0:T(8,128)(2,1)}, u32[]{:S(2)}) copy-start(bf16[16,128,128]{2,1,0:T(8,128)(2,1)} %param.16) | copy-start | bytes 1572868
  46.7 6.3 %collective-permute-start.3 = (bf16[1024,128]{1,0:T(8,128)(2,1)S(1)}, bf16[1024,128]{1,0:T(8,128)(2,1)S(1)}, u32[]{:S(2)}, u32[]{:S(2)}) collective-permute-start(bf16[1024,128]{1,0:T(8,128)(2,1)S(1)} %constant_dynamic-update-slice_fusion.refs_2_), channel_id=1, source_target_pairs={{0,1},{1,0},{2,3},{3,2},{4,5},{5,4},{6,7},{7,6},{8,9},{9,8},{10,11... | collective-permute-start | bytes 786440 | tf_op jit(solution)/shard_map/ppermute | solution.py:297
  47.0 0.7 %copy-start.6 = (s32[1,1,4,64,4]{3,4,2,1,0:T(4,128)S(1)}, s32[1,1,4,64,4]{3,4,2,1,0:T(4,128)}, u32[]{:S(2)}) copy-start(s32[1,1,4,64,4]{3,4,2,1,0:T(4,128)} %param.22) | copy-start | bytes 12292
  47.1 0.7 %copy-start.5 = (s32[1,1,4,64,4]{3,4,2,1,0:T(4,128)S(1)}, s32[1,1,4,64,4]{3,4,2,1,0:T(4,128)}, u32[]{:S(2)}) copy-start(s32[1,1,4,64,4]{3,4,2,1,0:T(4,128)} %param.21) | copy-start | bytes 12292
  47.1 0.7 %copy-start.8 = (s32[1,1,4,64]{3,2,1,0:T(4,128)S(1)}, s32[1,1,4,64]{3,2,1,0:T(4,128)}, u32[]{:S(2)}) copy-start(s32[1,1,4,64]{3,2,1,0:T(4,128)} %param.23) | copy-start | bytes 3076
  49.5 5.9 %collective-permute-start.4 = (bf16[144,128]{1,0:T(8,128)(2,1)S(1)}, bf16[144,128]{1,0:T(8,128)(2,1)S(1)}, u32[]{:S(2)}, u32[]{:S(2)}) collective-permute-start(bf16[144,128]{1,0:T(8,128)(2,1)S(1)} %get-tuple-element.19), channel_id=1, source_target_pairs={{0,8},{8,0},{16,24},{24,16},{1,9},{9,1},{17,25},{25,17},{2,10},{10... | collective-permute-start | bytes 110600 | tf_op jit(solution)/shard_map/ppermute | solution.py:323
  51.2 4.2 %collective-permute-start.5 = (bf16[144,128]{1,0:T(8,128)(2,1)S(1)}, bf16[144,128]{1,0:T(8,128)(2,1)S(1)}, u32[]{:S(2)}, u32[]{:S(2)}) collective-permute-start(bf16[144,128]{1,0:T(8,128)(2,1)S(1)} %get-tuple-element.18), channel_id=1, source_target_pairs={{0,16},{8,24},{16,0},{24,8},{1,17},{9,25},{17,1},{25,9},{2,18},{10... | collective-permute-start | bytes 110600 | tf_op jit(solution)/shard_map/ppermute | solution.py:323
  52.8 4.9 %copy-start.4 = (bf16[128,128]{1,0:T(8,128)(2,1)S(1)}, bf16[128,128]{1,0:T(8,128)(2,1)}, u32[]{:S(2)}) copy-start(bf16[128,128]{1,0:T(8,128)(2,1)} %refs_3_.1) | copy-start | bytes 98308
  52.8 4.9 %collective-permute-start.6 = (bf16[144,128]{1,0:T(8,128)(2,1)S(1)}, bf16[144,128]{1,0:T(8,128)(2,1)S(1)}, u32[]{:S(2)}, u32[]{:S(2)}) collective-permute-start(bf16[144,128]{1,0:T(8,128)(2,1)S(1)} %get-tuple-element.17), channel_id=1, source_target_pairs={{0,24},{8,16},{16,8},{24,0},{1,25},{9,17},{17,9},{25,1},{2,26},{10... | collective-permute-start | bytes 110600 | tf_op jit(solution)/shard_map/ppermute | solution.py:323

commit v6 on v2

--- a/solution.py
+++ b/solution.py
@@ -95,11 +95,10 @@
         ).astype(BF16)
 
 
-def near_kernel(nb_ref, cnt_ref, chg_ref, pos_ref, out_ref, feat, right, left):
+def table_kernel(cnt_ref, chg_ref, pos_ref, rows_ref, right_ref, left_ref, feat):
     boxes = chg_ref.shape[0]
-    knear = nb_ref.shape[0]
     live = iota((boxes, LANES), 1) < count_columns(cnt_ref, boxes)
-    feat[7] = jnp.where(live, chg_ref[...].astype(F32), 0.0)
+    rows_ref[1] = jnp.where(live, chg_ref[...].astype(F32), 0.0)
     norm = jnp.zeros((boxes, LANES), F32)
     for c in range(3):
         u = pos_ref[c] - 1.0
@@ -109,32 +108,35 @@
         feat[2 * c + 1] = m
         v = h + m
         norm = norm + v * v
-    feat[6] = norm
+    rows_ref[0] = norm
 
     def build(g, carry):
         rows = pl.ds(pl.multiple_of(g * 8, 8), 8)
-        tile = [feat[f, rows, :] for f in range(7)]
+        tile = [feat[f, rows, :] for f in range(6)]
         parts = []
         for c in range(3):
             h = -2.0 * tile[2 * c]
             m = -2.0 * tile[2 * c + 1]
             parts += [h, h, m, m]
-        n = tile[6] + EPS
+        n = rows_ref[0, rows, :] + EPS
         n1 = n.astype(BF16).astype(F32)
         n2 = (n - n1).astype(BF16).astype(F32)
         parts += [n1, n2, n - n1 - n2, jnp.zeros((8, LANES), F32)]
-        left[g] = jnp.concatenate(parts, axis=0).T.astype(BF16)
+        left_ref[g] = jnp.concatenate(parts, axis=0).T.astype(BF16)
         for r in range(8):
             for c in range(3):
                 h = jnp.broadcast_to(tile[2 * c][r : r + 1], (8, LANES))
                 m = jnp.broadcast_to(tile[2 * c + 1][r : r + 1], (8, LANES))
-                right[g * 8 + r, 16 * c : 16 * c + 16, :] = jnp.concatenate(
+                right_ref[g * 8 + r, 16 * c : 16 * c + 16, :] = jnp.concatenate(
                     [h, m], axis=0
                 ).astype(BF16)
         return carry
 
-    lax.fori_loop(0, boxes // 8, build, 0)
-
+    lax.fori_loop(0, boxes // 8, build, 0, unroll=4)
+
+
+def near_kernel(nb_ref, rows_ref, right_ref, left_ref, out_ref, *, start):
+    knear = nb_ref.shape[0]
     masks = [
         jnp.where((iota((LANES, LANES), 1) & 7) == j, 1.0, 0.0).astype(BF16) for j in range(8)
     ]
@@ -142,11 +144,12 @@
     ones = jnp.where(iota((32, LANES), 0) < 24, 1.0, 0.0).astype(BF16)
 
     def operand(box):
-        x, y, z = [right[box, 16 * c : 16 * c + 16, :] for c in range(3)]
+        x, y, z = [right_ref[box, 16 * c : 16 * c + 16, :] for c in range(3)]
         return jnp.concatenate([x, x, y, y, z, z, ones], axis=0)
 
-    def group(g, carry):
-        turned = left[g]
+    def group(i, carry):
+        g = i + start
+        turned = left_ref[g]
         outs = []
         for r in range(8):
             lhs = turned * masks[r]
@@ -155,20 +158,23 @@
                 pair = [nb_ref[k + i, g * 8 + r] for i in range(2)]
                 dist = dot(lhs, jnp.concatenate([operand(b) for b in pair], axis=1))
                 for i in range(2):
-                    shift = feat[6, pl.ds(pair[i], 1), :]
-                    q = feat[7, pl.ds(pair[i], 1), :]
+                    shift = rows_ref[0, pl.ds(pair[i], 1), :]
+                    q = rows_ref[1, pl.ds(pair[i], 1), :]
                     term = lax.rsqrt(dist[:, i * LANES : (i + 1) * LANES] + shift) * q
                     acc = term if acc is None else acc + term
             total = jnp.sum(acc, axis=1, keepdims=True)
             outs.append(jnp.sum(jnp.where(eye, total, 0.0), axis=0, keepdims=True))
-        out_ref[pl.ds(pl.multiple_of(g * 8, 8), 8), :] = jnp.concatenate(outs, axis=0)
+        out_ref[pl.ds(pl.multiple_of((g - start) * 8, 8), 8), :] = jnp.concatenate(outs, axis=0)
         return carry
 
-    lax.fori_loop(0, boxes // 8, group, 0, unroll=2)
-
-
-def group_kernel(*refs, blocks, fanin):
-    code_ref, ops_ref, mine_ref, other_ref, out_ref, sums = refs
+    lax.fori_loop(0, out_ref.shape[0] // 8, group, 0, unroll=2)
+
+
+def far_kernel(*refs, blocks, fanin, pieces):
+    code_ref, cnt_ref, ops_ref, eval_ref, mine_ref, other_ref = refs[:6]
+    near_refs = refs[6 : 6 + pieces]
+    pay_refs = refs[6 + pieces : -2]
+    out_ref, sums = refs[-2:]
     width = mine_ref.shape[1]
     boxes = mine_ref.shape[0] // (blocks // 2)
     patterns = ops_ref.shape[0] // width
@@ -207,14 +213,7 @@
                 sums[i * per : (i + 1) * per, p * width : (p + 1) * width] = s[
                     p * per : (p + 1) * per
                 ]
-    out_ref[...] = dot(sums[...], ops_ref[...])
-
-
-def final_kernel(*refs):
-    cnt_ref, near_ref, local_ref, eval_ref = refs[:4]
-    pay_refs = refs[4:-1]
-    out_ref = refs[-1]
-    boxes = local_ref.shape[0]
+    near_local = dot(sums[...], ops_ref[...])
     hits = []
     values = []
     for pay in pay_refs:
@@ -223,9 +222,10 @@
         box = iota((boxes, depth), 0).astype(F32)
         hits.append(jnp.where(box == target, 1.0, 0.0).astype(BF16))
         values.append(pay[0:depth, :])
-    local = local_ref[...] + dot(jnp.concatenate(hits, axis=1), jnp.concatenate(values, axis=0))
+    local = near_local + dot(jnp.concatenate(hits, axis=1), jnp.concatenate(values, axis=0))
     far = dot(local.astype(BF16), eval_ref[...])
-    total = near_ref[...] * (1.0 / (4.0 * math.pi)) + far
+    near = jnp.concatenate([ref[...] for ref in near_refs], axis=0)
+    total = near * (1.0 / (4.0 * math.pi)) + far
     live = iota((boxes, LANES), 1) < count_columns(cnt_ref, boxes)
     out_ref[...] = jnp.where(live, total, 0.0)
 
@@ -233,6 +233,7 @@
 VMEM = pl.BlockSpec(memory_space=pltpu.VMEM)
 SMEM = pl.BlockSpec(memory_space=pltpu.SMEM)
 MIB = 1024 * 1024
+PIECES = 4
 
 
 def body(
@@ -262,31 +263,60 @@
     multipole = jnp.dot(strength, moment_map, preferred_element_type=F32).astype(BF16)
 
     me = lax.axis_index("cube")
-    along = [multipole] + [
-        lax.ppermute(multipole, "cube", [(i, i ^ k) for i in range(n_cube)])
-        for k in range(2, n_cube, 2)
-    ]
-
-    near = pl.pallas_call(
-        near_kernel,
-        out_shape=jax.ShapeDtypeStruct((boxes, panels), F32),
-        in_specs=[SMEM, VMEM, VMEM, VMEM],
-        out_specs=VMEM,
-        scratch_shapes=[
-            pltpu.VMEM((8, boxes, panels), F32),
-            pltpu.VMEM((boxes, 48, panels), BF16),
-            pltpu.VMEM((boxes // 8, panels, LANES), BF16),
-        ],
+    octant = lax.axis_index("oct")
+
+    def over_cube(value, k):
+        return lax.ppermute(value, "cube", [(i, i ^ k) for i in range(n_cube)])
+
+    def over_oct(value, k):
+        return lax.ppermute(value, "oct", [(i, i ^ k) for i in range(n_oct)])
+
+    def after(value, *earlier):
+        return lax.optimization_barrier((value, *earlier))[0]
+
+    steps = list(range(2, n_cube, 2))
+    tables = pl.pallas_call(
+        table_kernel,
+        out_shape=(
+            jax.ShapeDtypeStruct((2, boxes, panels), F32),
+            jax.ShapeDtypeStruct((boxes, 48, panels), BF16),
+            jax.ShapeDtypeStruct((boxes // 8, panels, LANES), BF16),
+        ),
+        in_specs=[VMEM] * 3,
+        out_specs=(VMEM,) * 3,
+        scratch_shapes=[pltpu.VMEM((6, boxes, panels), F32)],
         compiler_params=pltpu.CompilerParams(vmem_limit_bytes=24 * MIB),
         cost_estimate=pl.CostEstimate(
-            flops=15_000_000_000, bytes_accessed=1_000_000, transcendentals=16_000_000
+            flops=1_000_000_000, bytes_accessed=1_000_000, transcendentals=0
         ),
-        name="near",
-    )(near_boxes.T, counts, charges, positions)
-
-    near, base, *along = lax.optimization_barrier((near, multipole, *along))
-    mine = jnp.concatenate(along, axis=0)
-    other = lax.ppermute(mine, "cube", [(i, i ^ 1) for i in range(n_cube)])
+        name="tables",
+    )(counts, charges, positions)
+
+    neighbours = near_boxes.T
+    size = boxes // PIECES
+
+    def near_piece(i, tables):
+        return pl.pallas_call(
+            functools.partial(near_kernel, start=i * size // 8),
+            out_shape=jax.ShapeDtypeStruct((size, panels), F32),
+            in_specs=[SMEM, VMEM, VMEM, VMEM],
+            out_specs=VMEM,
+            compiler_params=pltpu.CompilerParams(vmem_limit_bytes=16 * MIB),
+            cost_estimate=pl.CostEstimate(
+                flops=4_000_000_000, bytes_accessed=1_000_000, transcendentals=4_000_000
+            ),
+            name="near",
+        )(neighbours, *tables)
+
+    first, *rest = steps
+    along = {0: multipole, first: over_cube(multipole, first)}
+    held = after(multipole, *tables)
+    for k in rest[: (len(rest) + 1) // 2]:
+        along[k] = over_cube(held, k)
+    near = [near_piece(0, tables)]
+    held = after(multipole, near[0])
+    for k in rest[(len(rest) + 1) // 2 :]:
+        along[k] = over_cube(held, k)
 
     slots, fanin = remote_sources.shape[3:]
     sent = pl.pallas_call(
@@ -301,47 +331,53 @@
         ),
         name="slots",
     )(
-        base,
+        held,
         remote_sources[0, 0].transpose(0, 2, 1),
         remote_patterns[0, 0].transpose(0, 2, 1),
         remote_targets[0, 0],
         operators,
     )
-    octant = lax.axis_index("oct")
-    payloads = []
-    for k in range(n_oct):
-        part = lax.dynamic_index_in_dim(sent, octant ^ k, 0, keepdims=False)
-        if k > 0:
-            part = lax.ppermute(part, "oct", [(i, i ^ k) for i in range(n_oct)])
-        payloads.append(part)
+    parts = [
+        lax.dynamic_index_in_dim(sent, octant ^ k, 0, keepdims=False) for k in range(n_oct)
+    ]
+    third = -(-(n_oct - 1) // 3)
+    got = {0: parts[0]}
+    for k in range(1, min(1 + third, n_oct)):
+        got[k] = over_oct(parts[k], k)
+    tables = lax.optimization_barrier((*tables, sent, near[0]))[:3]
+    near.append(near_piece(1, tables))
+
+    held = lax.optimization_barrier((*[along[k] for k in sorted(along)], near[1]))[:-1]
+    mine = jnp.concatenate(held, axis=0)
+    other = over_cube(mine, 1)
+    for k in range(1 + third, min(1 + 2 * third, n_oct)):
+        got[k] = over_oct(after(parts[k], near[1]), k)
+    tables = lax.optimization_barrier((*tables, mine))[:3]
+    near.append(near_piece(2, tables))
+    for k in range(1 + 2 * third, n_oct):
+        got[k] = over_oct(after(parts[k], near[2]), k)
+    tables = lax.optimization_barrier((*tables, near[2]))[:3]
+    near.append(near_piece(3, tables))
+    other, *payloads, last = lax.optimization_barrier(
+        (other, *[got[k] for k in range(n_oct)], near[3])
+    )
+    near[3] = last
 
     klist = group_sources.shape[1]
     group = n_cube * boxes
     code = (group_sources ^ (me * boxes)) + group * group_patterns
-    near_local = pl.pallas_call(
-        functools.partial(group_kernel, blocks=n_cube, fanin=klist),
-        out_shape=jax.ShapeDtypeStruct((boxes, width), F32),
-        in_specs=[VMEM] * 4,
+    return pl.pallas_call(
+        functools.partial(far_kernel, blocks=n_cube, fanin=klist, pieces=PIECES),
+        out_shape=jax.ShapeDtypeStruct((boxes, panels), F32),
+        in_specs=[VMEM] * (6 + PIECES + n_oct),
         out_specs=VMEM,
         scratch_shapes=[pltpu.VMEM((boxes, patterns * width), BF16)],
         compiler_params=pltpu.CompilerParams(vmem_limit_bytes=24 * MIB),
         cost_estimate=pl.CostEstimate(
             flops=3_000_000_000, bytes_accessed=2_000_000, transcendentals=0
         ),
-        name="group",
-    )(code.reshape(-1, LANES), operators, mine, other)
-
-    return pl.pallas_call(
-        final_kernel,
-        out_shape=jax.ShapeDtypeStruct((boxes, panels), F32),
-        in_specs=[VMEM] * (4 + n_oct),
-        out_specs=VMEM,
-        compiler_params=pltpu.CompilerParams(vmem_limit_bytes=16 * MIB),
-        cost_estimate=pl.CostEstimate(
-            flops=200_000_000, bytes_accessed=600_000, transcendentals=0
-        ),
-        name="final",
-    )(counts, near, near_local, evaluation, *payloads)
+        name="far",
+    )(code.reshape(-1, LANES), counts, operators, evaluation, mine, other, *near, *payloads)
 
 
 def solution(mesh):

time: 40.2 us -> 41.8 us (1.040)
  local copies, waits for them, and re-layouts: 3.47 us -> 7.39 us
  waiting for transfers between devices: 2.19 us -> 0.12 us
  Pallas kernels: 23.6 us -> 23 us
    unnamed x27 -> x35, local copies, waits for them, and re-layouts: 3.2 us -> 7.12 us
    ppermute x7, waiting for transfers between devices: 2.19 us -> 0.12 us  [the longest x3 0.11 us: over_oct(): return lax.ppermute(value, 'oct', [(i, i ^ k) for i in range(n_oct)])]
    pallas_call x3 -> x6, Pallas kernels: 22 us -> 21.4 us  [the longest x4 16.9 us: near_piece(): pl.pallas_call(functools.partial(near_kernel, start=i * size // 8), out_s...]
  transfers between devices with their start and end apart: 7 -> 7, of which waited for: 1 -> 1; matrix products, arithmetic and copies ran while one was open for 1% -> 1% of each run, Pallas kernels for 57% -> 48%
where the time goes in v6:
time: 41.8 us; the launch traced here: 41.3 us
  Pallas kernels  23 us (55%)
  starting transfers between devices  9.51 us (23%)
  local copies, waits for them, and re-layouts  7.39 us (18%)
  matrix products  1.06 us (3%)
    pallas_call x4, Pallas kernels, near_piece(): pl.pallas_call(functools.partial(near_kernel, start=i * size // 8), out_s...  16.9 us
    unnamed x35, local copies, waits for them, and re-layouts  7.12 us
    ppermute x4, starting transfers between devices, over_cube(): return lax.ppermute(value, 'cube', [(i, i ^ k) for i in range(n_cube)])  5.86 us
    ppermute x3, starting transfers between devices, over_oct(): return lax.ppermute(value, 'oct', [(i, i ^ k) for i in range(n_oct)])  3.65 us
    pallas_call x1, Pallas kernels, body(): pl.pallas_call(functools.partial(far_kernel, blocks=n_cube, fanin=klist,...  3.19 us
    pallas_call x1, Pallas kernels, body(): pl.pallas_call(slot_kernel, out_shape=jax.ShapeDtypeStruct((n_oct, 2 * sl...  1.59 us
    pallas_call x1, Pallas kernels, body(): pl.pallas_call(table_kernel, out_shape=(jax.ShapeDtypeStruct((2, boxes, p...  1.35 us
    dot_general x1, matrix products, body(): jnp.dot(strength, moment_map, preferred_element_type=F32).astype(BF16)  1.06 us
  transfers between devices with their start and end apart: 7, of which 1 were waited for; matrix products, arithmetic and copies ran while one was open for 1% of the time, Pallas kernels for 48%

profile of v6, /device:TPU:0, one launch (start us, length us, event | category | flops | bytes accessed | tf_op | source)
XLA Modules:
  0.0 41.3 jit_solution(952417001334477729)
XLA Ops:
  0.0 0.8 %copy-done = bf16[128,128]{1,0:T(8,128)(2,1)S(1)} copy-done((bf16[128,128]{1,0:T(8,128)(2,1)S(1)}, bf16[128,128]{1,0:T(8,128)(2,1)}, u32[]{:S(2)}) %copy-start) | copy-done | bytes 32792
  0.8 1.1 %convolution_convert_fusion.m_ref = bf16[256,128]{1,0:T(8,128)(2,1)S(1)} fusion(bf16[128,128]{1,0:T(8,128)(2,1)S(1)} %copy-done, bf16[256,128]{1,0:T(8,128)(2,1)} %chg_ref.1, s32[256]{0:T(256)} %param.13), kind=kOutput, calls=%fused_computation | convolution fusion | flops 8486912 | bytes 164864 | tf_op jit(solution)/shard_map/dot_general | solution.py:263
  1.8 3.1 %collective-permute-start = (bf16[256,128]{1,0:T(8,128)(2,1)S(1)}, bf16[256,128]{1,0:T(8,128)(2,1)S(1)}, u32[]{:S(2)}, u32[]{:S(2)}) collective-permute-start(bf16[256,128]{1,0:T(8,128)(2,1)S(1)} %convolution_convert_fusion.m_ref), channel_id=1, source_target_pairs={{0,2},{1,3},{2,0},{3,1},{4,6},{5,7},{6,4},{7,5},{8,10},{9,11},{10,... | collective-permute-start | bytes 196616 | tf_op jit(solution)/shard_map/ppermute | solution.py:269
  4.9 1.0 %copy-done.2 = f32[3,256,128]{2,1,0:T(8,128)S(1)} copy-done((f32[3,256,128]{2,1,0:T(8,128)S(1)}, f32[3,256,128]{2,1,0:T(8,128)}, u32[]{:S(2)}) %copy-start.2) | copy-done | bytes 393240
  5.9 0.8 %copy-done.3 = bf16[256,128]{1,0:T(8,128)(2,1)S(1)} copy-done((bf16[256,128]{1,0:T(8,128)(2,1)S(1)}, bf16[256,128]{1,0:T(8,128)(2,1)}, u32[]{:S(2)}) %copy-start.3) | copy-done | bytes 65560
  6.8 0.7 %copy-done.9 = s32[256]{0:T(256)S(1)} copy-done((s32[256]{0:T(256)S(1)}, s32[256]{0:T(256)}, u32[]{:S(2)}) %copy-start.9) | copy-done | bytes 1048
  7.4 1.4 %tables.1 = (f32[2,256,128]{2,1,0:T(8,128)S(1)}, bf16[256,48,128]{2,1,0:T(8,128)(2,1)S(1)}, bf16[32,128,128]{2,1,0:T(8,128)(2,1)S(1)}) custom-call(s32[2,128]{1,0:T(2,128)S(1)} %bitcast.28, bf16[256,128]{1,0:T(8,128)(2,1)S(1)} %copy-done.3, f32[3,256,128]{2,1,0:T(8,128)S(1)} %copy-done.2), custom_call_target="tpu_custom_call" | custom-call | flops 1000000000 | bytes 1000000 | tf_op jit(solution)/shard_map/tables/pallas_call | solution.py:278
  8.9 4.2 %near.4.refs_6_ = f32[64,128]{1,0:T(8,128)S(1)} custom-call(s32[4,256]{1,0:T(4,128)S(1)} %bitcast.23, f32[2,256,128]{2,1,0:T(8,128)S(1)} %get-tuple-element.48.rows_ref, bf16[256,48,128]{2,1,0:T(8,128)(2,1)S(1)} %get-tuple-element.49.right_ref, bf16[32,128,128]{2,1,0:T(8,128)(2,1)S(1)} %get-tuple-element.50.left_ref), custom_call_target="tpu_custom_call" | custom-call | flops 4000000000 | bytes 1000000 | tf_op jit(solution)/shard_map/near/pallas_call | solution.py:299
  13.1 2.5 %collective-permute-start.2 = (bf16[256,128]{1,0:T(8,128)(2,1)S(1)}, bf16[256,128]{1,0:T(8,128)(2,1)S(1)}, u32[]{:S(2)}, u32[]{:S(2)}) collective-permute-start(bf16[256,128]{1,0:T(8,128)(2,1)S(1)} %convolution_convert_fusion.m_ref), channel_id=1, source_target_pairs={{0,6},{1,7},{2,4},{3,5},{4,2},{5,3},{6,0},{7,1},{8,14},{9,15},{10,... | collective-permute-start | bytes 196616 | tf_op jit(solution)/shard_map/ppermute | solution.py:269
  15.7 0.2 collective-permute-start.1
  15.8 1.6 %slots.1 = bf16[4,144,128]{2,1,0:T(8,128)(2,1)S(1)} custom-call(bf16[256,128]{1,0:T(8,128)(2,1)S(1)} %convolution_convert_fusion.m_ref, s32[4,4,64]{2,1,0:T(4,128)S(1)} %bitcast.21, s32[4,4,64]{2,1,0:T(4,128)S(1)} %bitcast.22, s32[4,64]{1,0:T(4,128)S(1)} %bitcast.27, bf16[2048,128]{1,0:T(8,128)(2,1)S(1)} %bitcast.19), custom_call_target="tpu_custom_call" | custom-call | flops 1000000000 | bytes 1000000 | tf_op jit(solution)/shard_map/slots/pallas_call | solution.py:322
  17.4 1.9 %copy-done.12 = bf16[256,48,128]{2,1,0:T(8,128)(2,1)S(1)} copy-done((bf16[256,48,128]{2,1,0:T(8,128)(2,1)S(1)}, bf16[256,48,128]{2,1,0:T(8,128)(2,1)}, u32[]{:S(2)}) %copy-start.12) | copy-done | bytes 3145752
  19.3 4.2 %near.5.refs_7_ = f32[64,128]{1,0:T(8,128)S(1)} custom-call(s32[4,256]{1,0:T(4,128)S(1)} %bitcast.24, f32[2,256,128]{2,1,0:T(8,128)S(1)} %get-tuple-element.48.rows_ref, bf16[256,48,128]{2,1,0:T(8,128)(2,1)S(1)} %copy-done.12, bf16[32,128,128]{2,1,0:T(8,128)(2,1)S(1)} %get-tuple-element.50.left_ref), custom_call_target="tpu_custom_call" | custom-call | flops 4000000000 | bytes 1000000 | tf_op jit(solution)/shard_map/near/pallas_call | solution.py:299
  23.6 1.6 %collective-permute-start.5 = (bf16[144,128]{1,0:T(8,128)(2,1)S(1)}, bf16[144,128]{1,0:T(8,128)(2,1)S(1)}, u32[]{:S(2)}, u32[]{:S(2)}) collective-permute-start(bf16[144,128]{1,0:T(8,128)(2,1)S(1)} %get-tuple-element.43), channel_id=1, source_target_pairs={{0,16},{8,24},{16,0},{24,8},{1,17},{9,25},{17,1},{25,9},{2,18},{10... | collective-permute-start | bytes 110600 | tf_op jit(solution)/shard_map/ppermute | solution.py:272
  25.2 1.5 %collective-permute-start.4 = (bf16[144,128]{1,0:T(8,128)(2,1)S(1)}, bf16[144,128]{1,0:T(8,128)(2,1)S(1)}, u32[]{:S(2)}, u32[]{:S(2)}) collective-permute-start(bf16[144,128]{1,0:T(8,128)(2,1)S(1)} %get-tuple-element.59), channel_id=1, source_target_pairs={{0,8},{8,0},{16,24},{24,16},{1,9},{9,1},{17,25},{25,17},{2,10},{10... | collective-permute-start | bytes 110600 | tf_op jit(solution)/shard_map/ppermute | solution.py:272
  26.7 0.1 copy.14
  26.8 0.1 reshape.10.refs_0_
  27.0 0.1 collective-permute-start.3
  27.1 1.9 %copy-done.13 = bf16[256,48,128]{2,1,0:T(8,128)(2,1)S(1)} copy-done((bf16[256,48,128]{2,1,0:T(8,128)(2,1)S(1)}, bf16[256,48,128]{2,1,0:T(8,128)(2,1)}, u32[]{:S(2)}) %copy-start.13) | copy-done | bytes 3145752
  29.0 4.2 %near.6.refs_8_ = f32[64,128]{1,0:T(8,128)S(1)} custom-call(s32[4,256]{1,0:T(4,128)S(1)} %bitcast.25, f32[2,256,128]{2,1,0:T(8,128)S(1)} %get-tuple-element.48.rows_ref, bf16[256,48,128]{2,1,0:T(8,128)(2,1)S(1)} %copy-done.13, bf16[32,128,128]{2,1,0:T(8,128)(2,1)S(1)} %get-tuple-element.50.left_ref), custom_call_target="tpu_custom_call" | custom-call | flops 4000000000 | bytes 1000000 | tf_op jit(solution)/shard_map/near/pallas_call | solution.py:299
  33.2 0.6 %collective-permute-start.6 = (bf16[144,128]{1,0:T(8,128)(2,1)S(1)}, bf16[144,128]{1,0:T(8,128)(2,1)S(1)}, u32[]{:S(2)}, u32[]{:S(2)}) collective-permute-start(bf16[144,128]{1,0:T(8,128)(2,1)S(1)} %get-tuple-element.47), channel_id=1, source_target_pairs={{0,24},{8,16},{16,8},{24,0},{1,25},{9,17},{17,9},{25,1},{2,26},{10... | collective-permute-start | bytes 110600 | tf_op jit(solution)/shard_map/ppermute | solution.py:272
  33.8 4.2 %near.7.refs_9_ = f32[64,128]{1,0:T(8,128)S(1)} custom-call(s32[4,256]{1,0:T(4,128)S(1)} %bitcast.26, f32[2,256,128]{2,1,0:T(8,128)S(1)} %get-tuple-element.48.rows_ref, bf16[256,48,128]{2,1,0:T(8,128)(2,1)S(1)} %copy-done.13, bf16[32,128,128]{2,1,0:T(8,128)(2,1)S(1)} %get-tuple-element.50.left_ref), custom_call_target="tpu_custom_call" | custom-call | flops 4000000000 | bytes 1000000 | tf_op jit(solution)/shard_map/near/pallas_call | solution.py:299
  38.0 0.1 collective-permute-done.6.refs_13_
  38.2 3.2 %far.1 = f32[256,128]{1,0:T(8,128)} custom-call(s32[16,128]{1,0:T(8,128)S(1)} %reshape.10.refs_0_, s32[2,128]{1,0:T(2,128)S(1)} %bitcast.29, bf16[2048,128]{1,0:T(8,128)(2,1)S(1)} %bitcast.20, bf16[128,128]{1,0:T(8,128)(2,1)S(1)} %copy-done.4, bf16[1024,128]{1,0:T(8,128)(2,1)S(1)} %constant_dynamic-update-slice_fusion.refs_4_, ...), custom_call_target="tpu_custom_call" | custom-call | flops 3000000000 | bytes 2000000 | tf_op jit(solution)/shard_map/far/pallas_call | solution.py:369
  (38 shorter events, 0.2 us)
Async XLA Ops:
  0.0 0.8 %copy-start = (bf16[128,128]{1,0:T(8,128)(2,1)S(1)}, bf16[128,128]{1,0:T(8,128)(2,1)}, u32[]{:S(2)}) copy-start(bf16[128,128]{1,0:T(8,128)(2,1)} %param.15) | copy-start | bytes 98308
  0.0 8.8 %copy-start.7 = (s32[256,4]{0,1:T(4,128)S(1)}, s32[256,4]{0,1:T(4,128)}, u32[]{:S(2)}) copy-start(s32[256,4]{0,1:T(4,128)} %param.18) | copy-start | bytes 12292
  1.8 25.1 %collective-permute-start = (bf16[256,128]{1,0:T(8,128)(2,1)S(1)}, bf16[256,128]{1,0:T(8,128)(2,1)S(1)}, u32[]{:S(2)}, u32[]{:S(2)}) collective-permute-start(bf16[256,128]{1,0:T(8,128)(2,1)S(1)} %convolution_convert_fusion.m_ref), channel_id=1, source_target_pairs={{0,2},{1,3},{2,0},{3,1},{4,6},{5,7},{6,4},{7,5},{8,10},{9,11},{10,... | collective-permute-start | bytes 196616 | tf_op jit(solution)/shard_map/ppermute | solution.py:269
  4.9 1.0 %copy-start.2 = (f32[3,256,128]{2,1,0:T(8,128)S(1)}, f32[3,256,128]{2,1,0:T(8,128)}, u32[]{:S(2)}) copy-start(f32[3,256,128]{2,1,0:T(8,128)} %pos_ref.1) | copy-start | bytes 1179652
  5.9 0.8 %copy-start.3 = (bf16[256,128]{1,0:T(8,128)(2,1)S(1)}, bf16[256,128]{1,0:T(8,128)(2,1)}, u32[]{:S(2)}) copy-start(bf16[256,128]{1,0:T(8,128)(2,1)} %chg_ref.1) | copy-start | bytes 196612
  6.7 0.7 %copy-start.9 = (s32[256]{0:T(256)S(1)}, s32[256]{0:T(256)}, u32[]{:S(2)}) copy-start(s32[256]{0:T(256)} %param.13) | copy-start | bytes 3076
  8.8 4.3 %copy-start.11 = (bf16[256,48,128]{2,1,0:T(8,128)(2,1)}, bf16[256,48,128]{2,1,0:T(8,128)(2,1)S(1)}, u32[]{:S(2)}) copy-start(bf16[256,48,128]{2,1,0:T(8,128)(2,1)S(1)} %get-tuple-element.49.right_ref) | copy-start | bytes 9437188
  8.8 7.0 %copy-start.1 = (bf16[16,128,128]{2,1,0:T(8,128)(2,1)S(1)}, bf16[16,128,128]{2,1,0:T(8,128)(2,1)}, u32[]{:S(2)}) copy-start(bf16[16,128,128]{2,1,0:T(8,128)(2,1)} %param.16) | copy-start | bytes 1572868
  8.8 7.0 %copy-start.5 = (s32[1,1,4,64,4]{3,4,2,1,0:T(4,128)S(1)}, s32[1,1,4,64,4]{3,4,2,1,0:T(4,128)}, u32[]{:S(2)}) copy-start(s32[1,1,4,64,4]{3,4,2,1,0:T(4,128)} %param.21) | copy-start | bytes 12292
  8.8 7.0 %copy-start.6 = (s32[1,1,4,64,4]{3,4,2,1,0:T(4,128)S(1)}, s32[1,1,4,64,4]{3,4,2,1,0:T(4,128)}, u32[]{:S(2)}) copy-start(s32[1,1,4,64,4]{3,4,2,1,0:T(4,128)} %param.22) | copy-start | bytes 12292
  8.8 7.0 %copy-start.8 = (s32[1,1,4,64]{3,2,1,0:T(4,128)S(1)}, s32[1,1,4,64]{3,2,1,0:T(4,128)}, u32[]{:S(2)}) copy-start(s32[1,1,4,64]{3,2,1,0:T(4,128)} %param.23) | copy-start | bytes 3076
  13.1 13.8 %collective-permute-start.2 = (bf16[256,128]{1,0:T(8,128)(2,1)S(1)}, bf16[256,128]{1,0:T(8,128)(2,1)S(1)}, u32[]{:S(2)}, u32[]{:S(2)}) collective-permute-start(bf16[256,128]{1,0:T(8,128)(2,1)S(1)} %convolution_convert_fusion.m_ref), channel_id=1, source_target_pairs={{0,6},{1,7},{2,4},{3,5},{4,2},{5,3},{6,0},{7,1},{8,14},{9,15},{10,... | collective-permute-start | bytes 196616 | tf_op jit(solution)/shard_map/ppermute | solution.py:269
  15.7 11.3 %collective-permute-start.1 = (bf16[256,128]{1,0:T(8,128)(2,1)S(1)}, bf16[256,128]{1,0:T(8,128)(2,1)S(1)}, u32[]{:S(2)}, u32[]{:S(2)}) collective-permute-start(bf16[256,128]{1,0:T(8,128)(2,1)S(1)} %convolution_convert_fusion.m_ref), channel_id=1, source_target_pairs={{0,4},{1,5},{2,6},{3,7},{4,0},{5,1},{6,2},{7,3},{8,12},{9,13},{10,... | collective-permute-start | bytes 196616 | tf_op jit(solution)/shard_map/ppermute | solution.py:269
  17.4 1.9 %copy-start.12 = (bf16[256,48,128]{2,1,0:T(8,128)(2,1)S(1)}, bf16[256,48,128]{2,1,0:T(8,128)(2,1)}, u32[]{:S(2)}) copy-start(bf16[256,48,128]{2,1,0:T(8,128)(2,1)} %copy-done.11) | copy-start | bytes 9437188
  19.3 7.3 %copy-start.14 = (s32[256,8]{0,1:T(8,128)S(1)}, s32[256,8]{0,1:T(8,128)}, u32[]{:S(2)}) copy-start(s32[256,8]{0,1:T(8,128)} %param.20) | copy-start | bytes 24580
  19.3 7.3 %copy-start.15 = (s32[256,8]{0,1:T(8,128)S(1)}, s32[256,8]{0,1:T(8,128)}, u32[]{:S(2)}) copy-start(s32[256,8]{0,1:T(8,128)} %param.19) | copy-start | bytes 24580
  23.6 14.4 %collective-permute-start.5 = (bf16[144,128]{1,0:T(8,128)(2,1)S(1)}, bf16[144,128]{1,0:T(8,128)(2,1)S(1)}, u32[]{:S(2)}, u32[]{:S(2)}) collective-permute-start(bf16[144,128]{1,0:T(8,128)(2,1)S(1)} %get-tuple-element.43), channel_id=1, source_target_pairs={{0,16},{8,24},{16,0},{24,8},{1,17},{9,25},{17,1},{25,9},{2,18},{10... | collective-permute-start | bytes 110600 | tf_op jit(solution)/shard_map/ppermute | solution.py:272
  25.2 12.8 %collective-permute-start.4 = (bf16[144,128]{1,0:T(8,128)(2,1)S(1)}, bf16[144,128]{1,0:T(8,128)(2,1)S(1)}, u32[]{:S(2)}, u32[]{:S(2)}) collective-permute-start(bf16[144,128]{1,0:T(8,128)(2,1)S(1)} %get-tuple-element.59), channel_id=1, source_target_pairs={{0,8},{8,0},{16,24},{24,16},{1,9},{9,1},{17,25},{25,17},{2,10},{10... | collective-permute-start | bytes 110600 | tf_op jit(solution)/shard_map/ppermute | solution.py:272
  27.0 11.1 %collective-permute-start.3 = (bf16[1024,128]{1,0:T(8,128)(2,1)S(1)}, bf16[1024,128]{1,0:T(8,128)(2,1)S(1)}, u32[]{:S(2)}, u32[]{:S(2)}) collective-permute-start(bf16[1024,128]{1,0:T(8,128)(2,1)S(1)} %constant_dynamic-update-slice_fusion.refs_4_), channel_id=1, source_target_pairs={{0,1},{1,0},{2,3},{3,2},{4,5},{5,4},{6,7},{7,6},{8,9},{9,8},{10,11... | collective-permute-start | bytes 786440 | tf_op jit(solution)/shard_map/ppermute | solution.py:269
  27.1 1.9 %copy-start.13 = (bf16[256,48,128]{2,1,0:T(8,128)(2,1)S(1)}, bf16[256,48,128]{2,1,0:T(8,128)(2,1)}, u32[]{:S(2)}) copy-start(bf16[256,48,128]{2,1,0:T(8,128)(2,1)} %copy-done.11) | copy-start | bytes 9437188
  33.2 5.0 %copy-start.4 = (bf16[128,128]{1,0:T(8,128)(2,1)S(1)}, bf16[128,128]{1,0:T(8,128)(2,1)}, u32[]{:S(2)}) copy-start(bf16[128,128]{1,0:T(8,128)(2,1)} %refs_3_.1) | copy-start | bytes 98308
  33.2 4.9 %copy-start.10 = (s32[256]{0:T(256)S(1)}, s32[256]{0:T(256)}, u32[]{:S(2)}) copy-start(s32[256]{0:T(256)} %param.13) | copy-start | bytes 3076
  33.2 4.9 %collective-permute-start.6 = (bf16[144,128]{1,0:T(8,128)(2,1)S(1)}, bf16[144,128]{1,0:T(8,128)(2,1)S(1)}, u32[]{:S(2)}, u32[]{:S(2)}) collective-permute-start(bf16[144,128]{1,0:T(8,128)(2,1)S(1)} %get-tuple-element.47), channel_id=1, source_target_pairs={{0,24},{8,16},{16,8},{24,0},{1,25},{9,17},{17,9},{25,1},{2,26},{10... | collective-permute-start | bytes 110600 | tf_op jit(solution)/shard_map/ppermute | solution.py:272

commit v7 on v6

--- a/solution.py
+++ b/solution.py
@@ -135,8 +135,7 @@
     lax.fori_loop(0, boxes // 8, build, 0, unroll=4)
 
 
-def near_kernel(nb_ref, rows_ref, right_ref, left_ref, out_ref, *, start):
-    knear = nb_ref.shape[0]
+def near_kernel(nb_ref, rows_ref, right_ref, left_ref, out_ref, *buffers, start):
     masks = [
         jnp.where((iota((LANES, LANES), 1) & 7) == j, 1.0, 0.0).astype(BF16) for j in range(8)
     ]
@@ -147,27 +146,46 @@
         x, y, z = [right_ref[box, 16 * c : 16 * c + 16, :] for c in range(3)]
         return jnp.concatenate([x, x, y, y, z, z, ones], axis=0)
 
+    count = out_ref.shape[0] // 8
+    last = start + count - 1
+
+    def product(g, r, half, buffer):
+        box = g * 8 + r
+        lhs = left_ref[g] * masks[r]
+        pair = [operand(nb_ref[2 * half + i, box]) for i in range(2)]
+        buffer[...] = dot(lhs, jnp.concatenate(pair, axis=1))
+
+    def terms(g, r, half, buffer):
+        acc = None
+        for i in range(2):
+            source = nb_ref[2 * half + i, g * 8 + r]
+            shift = rows_ref[0, pl.ds(source, 1), :]
+            q = rows_ref[1, pl.ds(source, 1), :]
+            term = lax.rsqrt(buffer[:, i * LANES : (i + 1) * LANES] + shift) * q
+            acc = term if acc is None else acc + term
+        return acc
+
+    halves = nb_ref.shape[0] // 2
+    for half in range(halves):
+        product(start, 0, half, buffers[half])
+
     def group(i, carry):
         g = i + start
-        turned = left_ref[g]
         outs = []
         for r in range(8):
-            lhs = turned * masks[r]
+            after_g, after_r = (g, r + 1) if r < 7 else (jnp.minimum(g + 1, last), 0)
+            here, there = (r % 2) * halves, ((r + 1) % 2) * halves
             acc = None
-            for k in range(0, knear, 2):
-                pair = [nb_ref[k + i, g * 8 + r] for i in range(2)]
-                dist = dot(lhs, jnp.concatenate([operand(b) for b in pair], axis=1))
-                for i in range(2):
-                    shift = rows_ref[0, pl.ds(pair[i], 1), :]
-                    q = rows_ref[1, pl.ds(pair[i], 1), :]
-                    term = lax.rsqrt(dist[:, i * LANES : (i + 1) * LANES] + shift) * q
-                    acc = term if acc is None else acc + term
+            for half in range(halves):
+                product(after_g, after_r, half, buffers[there + half])
+                part = terms(g, r, half, buffers[here + half])
+                acc = part if acc is None else acc + part
             total = jnp.sum(acc, axis=1, keepdims=True)
             outs.append(jnp.sum(jnp.where(eye, total, 0.0), axis=0, keepdims=True))
         out_ref[pl.ds(pl.multiple_of((g - start) * 8, 8), 8), :] = jnp.concatenate(outs, axis=0)
         return carry
 
-    lax.fori_loop(0, out_ref.shape[0] // 8, group, 0, unroll=2)
+    lax.fori_loop(0, count, group, 0)
 
 
 def far_kernel(*refs, blocks, fanin, pieces):
@@ -285,7 +303,7 @@
         in_specs=[VMEM] * 3,
         out_specs=(VMEM,) * 3,
         scratch_shapes=[pltpu.VMEM((6, boxes, panels), F32)],
-        compiler_params=pltpu.CompilerParams(vmem_limit_bytes=24 * MIB),
+        compiler_params=pltpu.CompilerParams(vmem_limit_bytes=10 * MIB),
         cost_estimate=pl.CostEstimate(
             flops=1_000_000_000, bytes_accessed=1_000_000, transcendentals=0
         ),
@@ -301,7 +319,8 @@
             out_shape=jax.ShapeDtypeStruct((size, panels), F32),
             in_specs=[SMEM, VMEM, VMEM, VMEM],
             out_specs=VMEM,
-            compiler_params=pltpu.CompilerParams(vmem_limit_bytes=16 * MIB),
+            scratch_shapes=[pltpu.VMEM((panels, 2 * LANES), F32)] * near_boxes.shape[1],
+            compiler_params=pltpu.CompilerParams(vmem_limit_bytes=8 * MIB),
             cost_estimate=pl.CostEstimate(
                 flops=4_000_000_000, bytes_accessed=1_000_000, transcendentals=4_000_000
             ),
@@ -325,7 +344,7 @@
         in_specs=[VMEM] * 5,
         out_specs=VMEM,
         scratch_shapes=[pltpu.VMEM((n_oct * slots, patterns * width), BF16)],
-        compiler_params=pltpu.CompilerParams(vmem_limit_bytes=16 * MIB),
+        compiler_params=pltpu.CompilerParams(vmem_limit_bytes=8 * MIB),
         cost_estimate=pl.CostEstimate(
             flops=1_000_000_000, bytes_accessed=1_000_000, transcendentals=0
         ),
@@ -372,7 +391,7 @@
         in_specs=[VMEM] * (6 + PIECES + n_oct),
         out_specs=VMEM,
         scratch_shapes=[pltpu.VMEM((boxes, patterns * width), BF16)],
-        compiler_params=pltpu.CompilerParams(vmem_limit_bytes=24 * MIB),
+        compiler_params=pltpu.CompilerParams(vmem_limit_bytes=10 * MIB),
         cost_estimate=pl.CostEstimate(
             flops=3_000_000_000, bytes_accessed=2_000_000, transcendentals=0
         ),

time: 41.8 us -> 45.8 us (1.096)
  Pallas kernels: 23 us -> 27.1 us
    pallas_call x4, Pallas kernels: 16.9 us -> 21 us  [near_piece(): pl.pallas_call(functools.partial(near_kernel, start=i * size // 8), out_s...]
  transfers between devices with their start and end apart: 7 -> 7, of which waited for: 1 -> 0; matrix products, arithmetic and copies ran while one was open for 1% -> 1% of each run, Pallas kernels for 48% -> 53%
where the time goes in v7:
time: 45.8 us; the launch traced here: 45.4 us
  Pallas kernels  27.1 us (59%)
  starting transfers between devices  9.52 us (21%)
  local copies, waits for them, and re-layouts  7.39 us (16%)
  matrix products  1.06 us (2%)
    pallas_call x4, Pallas kernels, near_piece(): pl.pallas_call(functools.partial(near_kernel, start=i * size // 8), out_s...  21 us
    unnamed x35, local copies, waits for them, and re-layouts  7.12 us
    ppermute x4, starting transfers between devices, over_cube(): return lax.ppermute(value, 'cube', [(i, i ^ k) for i in range(n_cube)])  5.9 us
    ppermute x3, starting transfers between devices, over_oct(): return lax.ppermute(value, 'oct', [(i, i ^ k) for i in range(n_oct)])  3.63 us
    pallas_call x1, Pallas kernels, body(): pl.pallas_call(functools.partial(far_kernel, blocks=n_cube, fanin=klist,...  3.18 us
    pallas_call x1, Pallas kernels, body(): pl.pallas_call(slot_kernel, out_shape=jax.ShapeDtypeStruct((n_oct, 2 * sl...  1.59 us
    pallas_call x1, Pallas kernels, body(): pl.pallas_call(table_kernel, out_shape=(jax.ShapeDtypeStruct((2, boxes, p...  1.35 us
    dot_general x1, matrix products, body(): jnp.dot(strength, moment_map, preferred_element_type=F32).astype(BF16)  1.06 us
  transfers between devices with their start and end apart: 7, of which 0 were waited for; matrix products, arithmetic and copies ran while one was open for 1% of the time, Pallas kernels for 53%

profile of v7, /device:TPU:0, one launch (start us, length us, event | category | flops | bytes accessed | tf_op | source)
XLA Modules:
  0.0 45.4 jit_solution(1275832825040175589)
XLA Ops:
  0.0 0.8 %copy-done = bf16[128,128]{1,0:T(8,128)(2,1)S(1)} copy-done((bf16[128,128]{1,0:T(8,128)(2,1)S(1)}, bf16[128,128]{1,0:T(8,128)(2,1)}, u32[]{:S(2)}) %copy-start) | copy-done | bytes 32792
  0.8 1.1 %convolution_convert_fusion.m_ref = bf16[256,128]{1,0:T(8,128)(2,1)S(1)} fusion(bf16[128,128]{1,0:T(8,128)(2,1)S(1)} %copy-done, bf16[256,128]{1,0:T(8,128)(2,1)} %chg_ref.1, s32[256]{0:T(256)} %param.13), kind=kOutput, calls=%fused_computation | convolution fusion | flops 8486912 | bytes 164864 | tf_op jit(solution)/shard_map/dot_general | solution.py:281
  1.8 3.1 %collective-permute-start = (bf16[256,128]{1,0:T(8,128)(2,1)S(1)}, bf16[256,128]{1,0:T(8,128)(2,1)S(1)}, u32[]{:S(2)}, u32[]{:S(2)}) collective-permute-start(bf16[256,128]{1,0:T(8,128)(2,1)S(1)} %convolution_convert_fusion.m_ref), channel_id=1, source_target_pairs={{0,2},{1,3},{2,0},{3,1},{4,6},{5,7},{6,4},{7,5},{8,10},{9,11},{10,... | collective-permute-start | bytes 196616 | tf_op jit(solution)/shard_map/ppermute | solution.py:287
  4.9 1.0 %copy-done.2 = f32[3,256,128]{2,1,0:T(8,128)S(1)} copy-done((f32[3,256,128]{2,1,0:T(8,128)S(1)}, f32[3,256,128]{2,1,0:T(8,128)}, u32[]{:S(2)}) %copy-start.2) | copy-done | bytes 393240
  5.9 0.8 %copy-done.3 = bf16[256,128]{1,0:T(8,128)(2,1)S(1)} copy-done((bf16[256,128]{1,0:T(8,128)(2,1)S(1)}, bf16[256,128]{1,0:T(8,128)(2,1)}, u32[]{:S(2)}) %copy-start.3) | copy-done | bytes 65560
  6.8 0.7 %copy-done.9 = s32[256]{0:T(256)S(1)} copy-done((s32[256]{0:T(256)S(1)}, s32[256]{0:T(256)}, u32[]{:S(2)}) %copy-start.9) | copy-done | bytes 1048
  7.4 1.4 %tables.1 = (f32[2,256,128]{2,1,0:T(8,128)S(1)}, bf16[256,48,128]{2,1,0:T(8,128)(2,1)S(1)}, bf16[32,128,128]{2,1,0:T(8,128)(2,1)S(1)}) custom-call(s32[2,128]{1,0:T(2,128)S(1)} %bitcast.28, bf16[256,128]{1,0:T(8,128)(2,1)S(1)} %copy-done.3, f32[3,256,128]{2,1,0:T(8,128)S(1)} %copy-done.2), custom_call_target="tpu_custom_call" | custom-call | flops 1000000000 | bytes 1000000 | tf_op jit(solution)/shard_map/tables/pallas_call | solution.py:296
  8.8 0.0 copy-start.6
  8.9 5.2 %near.4.refs_6_ = f32[64,128]{1,0:T(8,128)S(1)} custom-call(s32[4,256]{1,0:T(4,128)S(1)} %bitcast.23, f32[2,256,128]{2,1,0:T(8,128)S(1)} %get-tuple-element.48.rows_ref, bf16[256,48,128]{2,1,0:T(8,128)(2,1)S(1)} %get-tuple-element.49.right_ref, bf16[32,128,128]{2,1,0:T(8,128)(2,1)S(1)} %get-tuple-element.50.left_ref), custom_call_target="tpu_custom_call" | custom-call | flops 4000000000 | bytes 1000000 | tf_op jit(solution)/shard_map/near/pallas_call | solution.py:317
  14.1 2.5 %collective-permute-start.2 = (bf16[256,128]{1,0:T(8,128)(2,1)S(1)}, bf16[256,128]{1,0:T(8,128)(2,1)S(1)}, u32[]{:S(2)}, u32[]{:S(2)}) collective-permute-start(bf16[256,128]{1,0:T(8,128)(2,1)S(1)} %convolution_convert_fusion.m_ref), channel_id=1, source_target_pairs={{0,6},{1,7},{2,4},{3,5},{4,2},{5,3},{6,0},{7,1},{8,14},{9,15},{10,... | collective-permute-start | bytes 196616 | tf_op jit(solution)/shard_map/ppermute | solution.py:287
  16.7 0.2 collective-permute-start.1
  16.9 1.6 %slots.1 = bf16[4,144,128]{2,1,0:T(8,128)(2,1)S(1)} custom-call(bf16[256,128]{1,0:T(8,128)(2,1)S(1)} %convolution_convert_fusion.m_ref, s32[4,4,64]{2,1,0:T(4,128)S(1)} %bitcast.21, s32[4,4,64]{2,1,0:T(4,128)S(1)} %bitcast.22, s32[4,64]{1,0:T(4,128)S(1)} %bitcast.27, bf16[2048,128]{1,0:T(8,128)(2,1)S(1)} %bitcast.19), custom_call_target="tpu_custom_call" | custom-call | flops 1000000000 | bytes 1000000 | tf_op jit(solution)/shard_map/slots/pallas_call | solution.py:341
  18.5 1.9 %copy-done.12 = bf16[256,48,128]{2,1,0:T(8,128)(2,1)S(1)} copy-done((bf16[256,48,128]{2,1,0:T(8,128)(2,1)S(1)}, bf16[256,48,128]{2,1,0:T(8,128)(2,1)}, u32[]{:S(2)}) %copy-start.12) | copy-done | bytes 3145752
  20.4 5.3 %near.5.refs_7_ = f32[64,128]{1,0:T(8,128)S(1)} custom-call(s32[4,256]{1,0:T(4,128)S(1)} %bitcast.24, f32[2,256,128]{2,1,0:T(8,128)S(1)} %get-tuple-element.48.rows_ref, bf16[256,48,128]{2,1,0:T(8,128)(2,1)S(1)} %copy-done.12, bf16[32,128,128]{2,1,0:T(8,128)(2,1)S(1)} %get-tuple-element.50.left_ref), custom_call_target="tpu_custom_call" | custom-call | flops 4000000000 | bytes 1000000 | tf_op jit(solution)/shard_map/near/pallas_call | solution.py:317
  25.7 1.6 %collective-permute-start.5 = (bf16[144,128]{1,0:T(8,128)(2,1)S(1)}, bf16[144,128]{1,0:T(8,128)(2,1)S(1)}, u32[]{:S(2)}, u32[]{:S(2)}) collective-permute-start(bf16[144,128]{1,0:T(8,128)(2,1)S(1)} %get-tuple-element.43), channel_id=1, source_target_pairs={{0,16},{8,24},{16,0},{24,8},{1,17},{9,25},{17,1},{25,9},{2,18},{10... | collective-permute-start | bytes 110600 | tf_op jit(solution)/shard_map/ppermute | solution.py:290
  27.3 1.5 %collective-permute-start.4 = (bf16[144,128]{1,0:T(8,128)(2,1)S(1)}, bf16[144,128]{1,0:T(8,128)(2,1)S(1)}, u32[]{:S(2)}, u32[]{:S(2)}) collective-permute-start(bf16[144,128]{1,0:T(8,128)(2,1)S(1)} %get-tuple-element.59), channel_id=1, source_target_pairs={{0,8},{8,0},{16,24},{24,16},{1,9},{9,1},{17,25},{25,17},{2,10},{10... | collective-permute-start | bytes 110600 | tf_op jit(solution)/shard_map/ppermute | solution.py:290
  28.8 0.1 copy.14
  28.9 0.1 reshape.10.refs_0_
  29.1 0.1 collective-permute-start.3
  29.2 1.9 %copy-done.13 = bf16[256,48,128]{2,1,0:T(8,128)(2,1)S(1)} copy-done((bf16[256,48,128]{2,1,0:T(8,128)(2,1)S(1)}, bf16[256,48,128]{2,1,0:T(8,128)(2,1)}, u32[]{:S(2)}) %copy-start.13) | copy-done | bytes 3145752
  31.1 5.3 %near.6.refs_8_ = f32[64,128]{1,0:T(8,128)S(1)} custom-call(s32[4,256]{1,0:T(4,128)S(1)} %bitcast.25, f32[2,256,128]{2,1,0:T(8,128)S(1)} %get-tuple-element.48.rows_ref, bf16[256,48,128]{2,1,0:T(8,128)(2,1)S(1)} %copy-done.13, bf16[32,128,128]{2,1,0:T(8,128)(2,1)S(1)} %get-tuple-element.50.left_ref), custom_call_target="tpu_custom_call" | custom-call | flops 4000000000 | bytes 1000000 | tf_op jit(solution)/shard_map/near/pallas_call | solution.py:317
  36.4 0.5 %collective-permute-start.6 = (bf16[144,128]{1,0:T(8,128)(2,1)S(1)}, bf16[144,128]{1,0:T(8,128)(2,1)S(1)}, u32[]{:S(2)}, u32[]{:S(2)}) collective-permute-start(bf16[144,128]{1,0:T(8,128)(2,1)S(1)} %get-tuple-element.47), channel_id=1, source_target_pairs={{0,24},{8,16},{16,8},{24,0},{1,25},{9,17},{17,9},{25,1},{2,26},{10... | collective-permute-start | bytes 110600 | tf_op jit(solution)/shard_map/ppermute | solution.py:290
  36.9 5.3 %near.7.refs_9_ = f32[64,128]{1,0:T(8,128)S(1)} custom-call(s32[4,256]{1,0:T(4,128)S(1)} %bitcast.26, f32[2,256,128]{2,1,0:T(8,128)S(1)} %get-tuple-element.48.rows_ref, bf16[256,48,128]{2,1,0:T(8,128)(2,1)S(1)} %copy-done.13, bf16[32,128,128]{2,1,0:T(8,128)(2,1)S(1)} %get-tuple-element.50.left_ref), custom_call_target="tpu_custom_call" | custom-call | flops 4000000000 | bytes 1000000 | tf_op jit(solution)/shard_map/near/pallas_call | solution.py:317
  42.2 3.2 %far.1 = f32[256,128]{1,0:T(8,128)} custom-call(s32[16,128]{1,0:T(8,128)S(1)} %reshape.10.refs_0_, s32[2,128]{1,0:T(2,128)S(1)} %bitcast.29, bf16[2048,128]{1,0:T(8,128)(2,1)S(1)} %bitcast.20, bf16[128,128]{1,0:T(8,128)(2,1)S(1)} %copy-done.4, bf16[1024,128]{1,0:T(8,128)(2,1)S(1)} %constant_dynamic-update-slice_fusion.refs_4_, ...), custom_call_target="tpu_custom_call" | custom-call | flops 3000000000 | bytes 2000000 | tf_op jit(solution)/shard_map/far/pallas_call | solution.py:388
  (38 shorter events, 0.2 us)
Async XLA Ops:
  0.0 0.8 %copy-start = (bf16[128,128]{1,0:T(8,128)(2,1)S(1)}, bf16[128,128]{1,0:T(8,128)(2,1)}, u32[]{:S(2)}) copy-start(bf16[128,128]{1,0:T(8,128)(2,1)} %param.15) | copy-start | bytes 98308
  0.0 8.8 %copy-start.7 = (s32[256,4]{0,1:T(4,128)S(1)}, s32[256,4]{0,1:T(4,128)}, u32[]{:S(2)}) copy-start(s32[256,4]{0,1:T(4,128)} %param.18) | copy-start | bytes 12292
  1.8 27.2 %collective-permute-start = (bf16[256,128]{1,0:T(8,128)(2,1)S(1)}, bf16[256,128]{1,0:T(8,128)(2,1)S(1)}, u32[]{:S(2)}, u32[]{:S(2)}) collective-permute-start(bf16[256,128]{1,0:T(8,128)(2,1)S(1)} %convolution_convert_fusion.m_ref), channel_id=1, source_target_pairs={{0,2},{1,3},{2,0},{3,1},{4,6},{5,7},{6,4},{7,5},{8,10},{9,11},{10,... | collective-permute-start | bytes 196616 | tf_op jit(solution)/shard_map/ppermute | solution.py:287
  4.9 1.0 %copy-start.2 = (f32[3,256,128]{2,1,0:T(8,128)S(1)}, f32[3,256,128]{2,1,0:T(8,128)}, u32[]{:S(2)}) copy-start(f32[3,256,128]{2,1,0:T(8,128)} %pos_ref.1) | copy-start | bytes 1179652
  5.9 0.8 %copy-start.3 = (bf16[256,128]{1,0:T(8,128)(2,1)S(1)}, bf16[256,128]{1,0:T(8,128)(2,1)}, u32[]{:S(2)}) copy-start(bf16[256,128]{1,0:T(8,128)(2,1)} %chg_ref.1) | copy-start | bytes 196612
  6.7 0.7 %copy-start.9 = (s32[256]{0:T(256)S(1)}, s32[256]{0:T(256)}, u32[]{:S(2)}) copy-start(s32[256]{0:T(256)} %param.13) | copy-start | bytes 3076
  8.8 5.3 %copy-start.11 = (bf16[256,48,128]{2,1,0:T(8,128)(2,1)}, bf16[256,48,128]{2,1,0:T(8,128)(2,1)S(1)}, u32[]{:S(2)}) copy-start(bf16[256,48,128]{2,1,0:T(8,128)(2,1)S(1)} %get-tuple-element.49.right_ref) | copy-start | bytes 9437188
  8.8 8.1 %copy-start.1 = (bf16[16,128,128]{2,1,0:T(8,128)(2,1)S(1)}, bf16[16,128,128]{2,1,0:T(8,128)(2,1)}, u32[]{:S(2)}) copy-start(bf16[16,128,128]{2,1,0:T(8,128)(2,1)} %param.16) | copy-start | bytes 1572868
  8.8 8.0 %copy-start.5 = (s32[1,1,4,64,4]{3,4,2,1,0:T(4,128)S(1)}, s32[1,1,4,64,4]{3,4,2,1,0:T(4,128)}, u32[]{:S(2)}) copy-start(s32[1,1,4,64,4]{3,4,2,1,0:T(4,128)} %param.21) | copy-start | bytes 12292
  8.8 8.0 %copy-start.6 = (s32[1,1,4,64,4]{3,4,2,1,0:T(4,128)S(1)}, s32[1,1,4,64,4]{3,4,2,1,0:T(4,128)}, u32[]{:S(2)}) copy-start(s32[1,1,4,64,4]{3,4,2,1,0:T(4,128)} %param.22) | copy-start | bytes 12292
  8.8 8.0 %copy-start.8 = (s32[1,1,4,64]{3,2,1,0:T(4,128)S(1)}, s32[1,1,4,64]{3,2,1,0:T(4,128)}, u32[]{:S(2)}) copy-start(s32[1,1,4,64]{3,2,1,0:T(4,128)} %param.23) | copy-start | bytes 3076
  14.1 14.9 %collective-permute-start.2 = (bf16[256,128]{1,0:T(8,128)(2,1)S(1)}, bf16[256,128]{1,0:T(8,128)(2,1)S(1)}, u32[]{:S(2)}, u32[]{:S(2)}) collective-permute-start(bf16[256,128]{1,0:T(8,128)(2,1)S(1)} %convolution_convert_fusion.m_ref), channel_id=1, source_target_pairs={{0,6},{1,7},{2,4},{3,5},{4,2},{5,3},{6,0},{7,1},{8,14},{9,15},{10,... | collective-permute-start | bytes 196616 | tf_op jit(solution)/shard_map/ppermute | solution.py:287
  16.7 12.4 %collective-permute-start.1 = (bf16[256,128]{1,0:T(8,128)(2,1)S(1)}, bf16[256,128]{1,0:T(8,128)(2,1)S(1)}, u32[]{:S(2)}, u32[]{:S(2)}) collective-permute-start(bf16[256,128]{1,0:T(8,128)(2,1)S(1)} %convolution_convert_fusion.m_ref), channel_id=1, source_target_pairs={{0,4},{1,5},{2,6},{3,7},{4,0},{5,1},{6,2},{7,3},{8,12},{9,13},{10,... | collective-permute-start | bytes 196616 | tf_op jit(solution)/shard_map/ppermute | solution.py:287
  18.5 1.9 %copy-start.12 = (bf16[256,48,128]{2,1,0:T(8,128)(2,1)S(1)}, bf16[256,48,128]{2,1,0:T(8,128)(2,1)}, u32[]{:S(2)}) copy-start(bf16[256,48,128]{2,1,0:T(8,128)(2,1)} %copy-done.11) | copy-start | bytes 9437188
  20.4 8.4 %copy-start.14 = (s32[256,8]{0,1:T(8,128)S(1)}, s32[256,8]{0,1:T(8,128)}, u32[]{:S(2)}) copy-start(s32[256,8]{0,1:T(8,128)} %param.20) | copy-start | bytes 24580
  20.4 8.4 %copy-start.15 = (s32[256,8]{0,1:T(8,128)S(1)}, s32[256,8]{0,1:T(8,128)}, u32[]{:S(2)}) copy-start(s32[256,8]{0,1:T(8,128)} %param.19) | copy-start | bytes 24580
  25.7 16.5 %collective-permute-start.5 = (bf16[144,128]{1,0:T(8,128)(2,1)S(1)}, bf16[144,128]{1,0:T(8,128)(2,1)S(1)}, u32[]{:S(2)}, u32[]{:S(2)}) collective-permute-start(bf16[144,128]{1,0:T(8,128)(2,1)S(1)} %get-tuple-element.43), channel_id=1, source_target_pairs={{0,16},{8,24},{16,0},{24,8},{1,17},{9,25},{17,1},{25,9},{2,18},{10... | collective-permute-start | bytes 110600 | tf_op jit(solution)/shard_map/ppermute | solution.py:290
  27.3 14.9 %collective-permute-start.4 = (bf16[144,128]{1,0:T(8,128)(2,1)S(1)}, bf16[144,128]{1,0:T(8,128)(2,1)S(1)}, u32[]{:S(2)}, u32[]{:S(2)}) collective-permute-start(bf16[144,128]{1,0:T(8,128)(2,1)S(1)} %get-tuple-element.59), channel_id=1, source_target_pairs={{0,8},{8,0},{16,24},{24,16},{1,9},{9,1},{17,25},{25,17},{2,10},{10... | collective-permute-start | bytes 110600 | tf_op jit(solution)/shard_map/ppermute | solution.py:290
  29.1 13.1 %collective-permute-start.3 = (bf16[1024,128]{1,0:T(8,128)(2,1)S(1)}, bf16[1024,128]{1,0:T(8,128)(2,1)S(1)}, u32[]{:S(2)}, u32[]{:S(2)}) collective-permute-start(bf16[1024,128]{1,0:T(8,128)(2,1)S(1)} %constant_dynamic-update-slice_fusion.refs_4_), channel_id=1, source_target_pairs={{0,1},{1,0},{2,3},{3,2},{4,5},{5,4},{6,7},{7,6},{8,9},{9,8},{10,11... | collective-permute-start | bytes 786440 | tf_op jit(solution)/shard_map/ppermute | solution.py:287
  29.2 1.9 %copy-start.13 = (bf16[256,48,128]{2,1,0:T(8,128)(2,1)S(1)}, bf16[256,48,128]{2,1,0:T(8,128)(2,1)}, u32[]{:S(2)}) copy-start(bf16[256,48,128]{2,1,0:T(8,128)(2,1)} %copy-done.11) | copy-start | bytes 9437188
  36.3 5.9 %copy-start.4 = (bf16[128,128]{1,0:T(8,128)(2,1)S(1)}, bf16[128,128]{1,0:T(8,128)(2,1)}, u32[]{:S(2)}) copy-start(bf16[128,128]{1,0:T(8,128)(2,1)} %refs_3_.1) | copy-start | bytes 98308
  36.4 5.9 %copy-start.10 = (s32[256]{0:T(256)S(1)}, s32[256]{0:T(256)}, u32[]{:S(2)}) copy-start(s32[256]{0:T(256)} %param.13) | copy-start | bytes 3076
  36.4 5.8 %collective-permute-start.6 = (bf16[144,128]{1,0:T(8,128)(2,1)S(1)}, bf16[144,128]{1,0:T(8,128)(2,1)S(1)}, u32[]{:S(2)}, u32[]{:S(2)}) collective-permute-start(bf16[144,128]{1,0:T(8,128)(2,1)S(1)} %get-tuple-element.47), channel_id=1, source_target_pairs={{0,24},{8,16},{16,8},{24,0},{1,25},{9,17},{17,9},{25,1},{2,26},{10... | collective-permute-start | bytes 110600 | tf_op jit(solution)/shard_map/ppermute | solution.py:290

commit v8 on v6

--- a/solution.py
+++ b/solution.py
@@ -95,79 +95,122 @@
         ).astype(BF16)
 
 
-def table_kernel(cnt_ref, chg_ref, pos_ref, rows_ref, right_ref, left_ref, feat):
+def plan_kernel(
+    nb_ref, cnt_ref, chg_ref, pos_ref, plan_ref, rows_ref, coords_ref, left_ref, ranked
+):
     boxes = chg_ref.shape[0]
-    live = iota((boxes, LANES), 1) < count_columns(cnt_ref, boxes)
-    rows_ref[1] = jnp.where(live, chg_ref[...].astype(F32), 0.0)
+    column = count_columns(cnt_ref, boxes)
+    row = jnp.concatenate([cnt_ref[i : i + 1, :] for i in range(boxes // LANES)], axis=1)
+    rows_ref[1] = jnp.where(iota((boxes, LANES), 1) < column, chg_ref[...].astype(F32), 0.0)
+
+    down, across = iota((boxes, boxes), 0), iota((boxes, boxes), 1)
+    ahead = (column < row) | ((column == row) & (down < across))
+    rank_row = jnp.sum(jnp.where(ahead, 1.0, 0.0), axis=0, keepdims=True)
+    behind = (row < column) | ((row == column) & (across < down))
+    rank_column = jnp.sum(jnp.where(behind, 1.0, 0.0), axis=1, keepdims=True)
+    to_rank = jnp.where(rank_row == down.astype(F32), 1.0, 0.0).astype(BF16)
+    from_rank = jnp.where(rank_column == across.astype(F32), 1.0, 0.0).astype(BF16)
+
+    lists = jnp.concatenate(
+        [
+            nb_ref[...].astype(F32),
+            row.astype(F32),
+            across[0:1].astype(F32),
+            jnp.zeros((16 - 2 - nb_ref.shape[0], boxes), F32),
+        ],
+        axis=0,
+    )
+    plan = dot(lists.astype(BF16), from_rank)[0:8].astype(jnp.int32)
+    within = jnp.where(column <= STEP * across, 1.0, 0.0)
+    ends = jnp.sum(within, axis=0, keepdims=True).astype(jnp.int32) >> log2(TEAM)
+    plan_ref[...] = jnp.where(iota((8, boxes), 0) == nb_ref.shape[0] + 2, ends, plan)
+
     norm = jnp.zeros((boxes, LANES), F32)
+    parts = []
     for c in range(3):
         u = pos_ref[c] - 1.0
         h = u.astype(BF16).astype(F32)
         m = (u - h).astype(BF16).astype(F32)
-        feat[2 * c] = h
-        feat[2 * c + 1] = m
+        coords_ref[2 * c] = h
+        coords_ref[2 * c + 1] = m
+        parts += [-2.0 * h, -2.0 * m]
         v = h + m
         norm = norm + v * v
     rows_ref[0] = norm
+    n = norm + EPS
+    n1 = n.astype(BF16).astype(F32)
+    n2 = (n - n1).astype(BF16).astype(F32)
+    parts += [n1, n2, n - n1 - n2]
+    ranked[...] = dot(to_rank, jnp.concatenate([p.astype(BF16) for p in parts], axis=1))
 
     def build(g, carry):
         rows = pl.ds(pl.multiple_of(g * 8, 8), 8)
-        tile = [feat[f, rows, :] for f in range(6)]
-        parts = []
+        f = [ranked[rows, i * LANES : (i + 1) * LANES] for i in range(9)]
+        stack = []
         for c in range(3):
-            h = -2.0 * tile[2 * c]
-            m = -2.0 * tile[2 * c + 1]
-            parts += [h, h, m, m]
-        n = rows_ref[0, rows, :] + EPS
-        n1 = n.astype(BF16).astype(F32)
-        n2 = (n - n1).astype(BF16).astype(F32)
-        parts += [n1, n2, n - n1 - n2, jnp.zeros((8, LANES), F32)]
-        left_ref[g] = jnp.concatenate(parts, axis=0).T.astype(BF16)
+            stack += [f[2 * c], f[2 * c], f[2 * c + 1], f[2 * c + 1]]
+        stack += f[6:9] + [jnp.zeros((8, LANES), F32)]
+        left_ref[g] = jnp.concatenate(stack, axis=0).T.astype(BF16)
+        return carry
+
+    lax.fori_loop(0, boxes // 8, build, 0, unroll=4)
+
+
+def near_kernel(plan_ref, rows_ref, coords_ref, left_ref, out_ref, right, *, start, stop):
+    boxes = out_ref.shape[0]
+    knear = 4
+    out_ref[...] = jnp.zeros_like(out_ref)
+
+    def build(g, carry):
+        rows = pl.ds(pl.multiple_of(g * 8, 8), 8)
+        tile = [coords_ref[f, rows, :] for f in range(6)]
         for r in range(8):
             for c in range(3):
                 h = jnp.broadcast_to(tile[2 * c][r : r + 1], (8, LANES))
                 m = jnp.broadcast_to(tile[2 * c + 1][r : r + 1], (8, LANES))
-                right_ref[g * 8 + r, 16 * c : 16 * c + 16, :] = jnp.concatenate(
+                right[g * 8 + r, 16 * c : 16 * c + 16, :] = jnp.concatenate(
                     [h, m], axis=0
                 ).astype(BF16)
         return carry
 
     lax.fori_loop(0, boxes // 8, build, 0, unroll=4)
 
-
-def near_kernel(nb_ref, rows_ref, right_ref, left_ref, out_ref, *, start):
-    knear = nb_ref.shape[0]
-    masks = [
-        jnp.where((iota((LANES, LANES), 1) & 7) == j, 1.0, 0.0).astype(BF16) for j in range(8)
-    ]
-    eye = iota((LANES, LANES), 0) == iota((LANES, LANES), 1)
     ones = jnp.where(iota((32, LANES), 0) < 24, 1.0, 0.0).astype(BF16)
 
     def operand(box):
-        x, y, z = [right_ref[box, 16 * c : 16 * c + 16, :] for c in range(3)]
+        x, y, z = [right[box, 16 * c : 16 * c + 16, :] for c in range(3)]
         return jnp.concatenate([x, x, y, y, z, z, ones], axis=0)
 
-    def group(i, carry):
-        g = i + start
-        turned = left_ref[g]
-        outs = []
-        for r in range(8):
-            lhs = turned * masks[r]
-            acc = None
-            for k in range(0, knear, 2):
-                pair = [nb_ref[k + i, g * 8 + r] for i in range(2)]
-                dist = dot(lhs, jnp.concatenate([operand(b) for b in pair], axis=1))
-                for i in range(2):
-                    shift = rows_ref[0, pl.ds(pair[i], 1), :]
-                    q = rows_ref[1, pl.ds(pair[i], 1), :]
-                    term = lax.rsqrt(dist[:, i * LANES : (i + 1) * LANES] + shift) * q
-                    acc = term if acc is None else acc + term
-            total = jnp.sum(acc, axis=1, keepdims=True)
-            outs.append(jnp.sum(jnp.where(eye, total, 0.0), axis=0, keepdims=True))
-        out_ref[pl.ds(pl.multiple_of((g - start) * 8, 8), 8), :] = jnp.concatenate(outs, axis=0)
+    def team(depth, g, carry):
+        masks = [
+            jnp.where((iota((depth, LANES), 1) & 7) == j, 1.0, 0.0).astype(BF16) for j in range(8)
+        ]
+        eye = iota((depth, LANES), 0) == iota((depth, LANES), 1)
+        for e in range(TEAM // 8):
+            turned = left_ref[g * (TEAM // 8) + e, 0:depth, :]
+            for r in range(8):
+                place = g * TEAM + e * 8 + r
+                lhs = turned * masks[r]
+                acc = None
+                for k in range(0, knear, 2):
+                    pair = [plan_ref[k + i, place] for i in range(2)]
+                    dist = dot(lhs, jnp.concatenate([operand(b) for b in pair], axis=1))
+                    for i in range(2):
+                        shift = rows_ref[0, pl.ds(pair[i], 1), :]
+                        q = rows_ref[1, pl.ds(pair[i], 1), :]
+                        term = lax.rsqrt(dist[:, i * LANES : (i + 1) * LANES] + shift) * q
+                        acc = term if acc is None else acc + term
+                total = jnp.sum(acc, axis=1, keepdims=True)
+                out_ref[pl.ds(plan_ref[knear + 1, place], 1), :] = jnp.sum(
+                    jnp.where(eye, total, 0.0), axis=0, keepdims=True
+                )
         return carry
 
-    lax.fori_loop(0, out_ref.shape[0] // 8, group, 0, unroll=2)
+    done = start
+    for step in range(1, LANES // STEP + 1):
+        until = jnp.clip(plan_ref[knear + 2, step], done, stop)
+        lax.fori_loop(done, until, functools.partial(team, step * STEP), 0)
+        done = until
 
 
 def far_kernel(*refs, blocks, fanin, pieces):
@@ -224,7 +267,9 @@
         values.append(pay[0:depth, :])
     local = near_local + dot(jnp.concatenate(hits, axis=1), jnp.concatenate(values, axis=0))
     far = dot(local.astype(BF16), eval_ref[...])
-    near = jnp.concatenate([ref[...] for ref in near_refs], axis=0)
+    near = near_refs[0][...]
+    for ref in near_refs[1:]:
+        near = near + ref[...]
     total = near * (1.0 / (4.0 * math.pi)) + far
     live = iota((boxes, LANES), 1) < count_columns(cnt_ref, boxes)
     out_ref[...] = jnp.where(live, total, 0.0)
@@ -233,7 +278,9 @@
 VMEM = pl.BlockSpec(memory_space=pltpu.VMEM)
 SMEM = pl.BlockSpec(memory_space=pltpu.SMEM)
 MIB = 1024 * 1024
-PIECES = 4
+PIECES = 2
+TEAM = 16
+STEP = 16
 
 
 def body(
@@ -274,49 +321,40 @@
     def after(value, *earlier):
         return lax.optimization_barrier((value, *earlier))[0]
 
-    steps = list(range(2, n_cube, 2))
-    tables = pl.pallas_call(
-        table_kernel,
+    plan, *tables = pl.pallas_call(
+        plan_kernel,
         out_shape=(
+            jax.ShapeDtypeStruct((8, boxes), jnp.int32),
             jax.ShapeDtypeStruct((2, boxes, panels), F32),
-            jax.ShapeDtypeStruct((boxes, 48, panels), BF16),
+            jax.ShapeDtypeStruct((6, boxes, panels), F32),
             jax.ShapeDtypeStruct((boxes // 8, panels, LANES), BF16),
         ),
-        in_specs=[VMEM] * 3,
-        out_specs=(VMEM,) * 3,
-        scratch_shapes=[pltpu.VMEM((6, boxes, panels), F32)],
-        compiler_params=pltpu.CompilerParams(vmem_limit_bytes=24 * MIB),
+        in_specs=[VMEM] * 4,
+        out_specs=(VMEM,) * 4,
+        scratch_shapes=[pltpu.VMEM((boxes, 9 * LANES), F32)],
+        compiler_params=pltpu.CompilerParams(vmem_limit_bytes=12 * MIB),
         cost_estimate=pl.CostEstimate(
             flops=1_000_000_000, bytes_accessed=1_000_000, transcendentals=0
         ),
-        name="tables",
-    )(counts, charges, positions)
-
-    neighbours = near_boxes.T
-    size = boxes // PIECES
-
-    def near_piece(i, tables):
+        name="plan",
+    )(near_boxes.T, counts, charges, positions)
+
+    teams = boxes // TEAM
+    cut = teams * 5 // 8
+
+    def near_piece(start, stop, tables):
         return pl.pallas_call(
-            functools.partial(near_kernel, start=i * size // 8),
-            out_shape=jax.ShapeDtypeStruct((size, panels), F32),
+            functools.partial(near_kernel, start=start, stop=stop),
+            out_shape=jax.ShapeDtypeStruct((boxes, panels), F32),
             in_specs=[SMEM, VMEM, VMEM, VMEM],
             out_specs=VMEM,
-            compiler_params=pltpu.CompilerParams(vmem_limit_bytes=16 * MIB),
+            scratch_shapes=[pltpu.VMEM((boxes, 48, panels), BF16)],
+            compiler_params=pltpu.CompilerParams(vmem_limit_bytes=12 * MIB),
             cost_estimate=pl.CostEstimate(
-                flops=4_000_000_000, bytes_accessed=1_000_000, transcendentals=4_000_000
+                flops=200_000_000, bytes_accessed=1_000_000, transcendentals=0
             ),
             name="near",
-        )(neighbours, *tables)
-
-    first, *rest = steps
-    along = {0: multipole, first: over_cube(multipole, first)}
-    held = after(multipole, *tables)
-    for k in rest[: (len(rest) + 1) // 2]:
-        along[k] = over_cube(held, k)
-    near = [near_piece(0, tables)]
-    held = after(multipole, near[0])
-    for k in rest[(len(rest) + 1) // 2 :]:
-        along[k] = over_cube(held, k)
+        )(plan, *tables)
 
     slots, fanin = remote_sources.shape[3:]
     sent = pl.pallas_call(
@@ -325,43 +363,59 @@
         in_specs=[VMEM] * 5,
         out_specs=VMEM,
         scratch_shapes=[pltpu.VMEM((n_oct * slots, patterns * width), BF16)],
-        compiler_params=pltpu.CompilerParams(vmem_limit_bytes=16 * MIB),
+        compiler_params=pltpu.CompilerParams(vmem_limit_bytes=8 * MIB),
         cost_estimate=pl.CostEstimate(
             flops=1_000_000_000, bytes_accessed=1_000_000, transcendentals=0
         ),
         name="slots",
     )(
-        held,
+        multipole,
         remote_sources[0, 0].transpose(0, 2, 1),
         remote_patterns[0, 0].transpose(0, 2, 1),
         remote_targets[0, 0],
         operators,
     )
-    parts = [
-        lax.dynamic_index_in_dim(sent, octant ^ k, 0, keepdims=False) for k in range(n_oct)
-    ]
-    third = -(-(n_oct - 1) // 3)
-    got = {0: parts[0]}
-    for k in range(1, min(1 + third, n_oct)):
-        got[k] = over_oct(parts[k], k)
-    tables = lax.optimization_barrier((*tables, sent, near[0]))[:3]
-    near.append(near_piece(1, tables))
-
-    held = lax.optimization_barrier((*[along[k] for k in sorted(along)], near[1]))[:-1]
-    mine = jnp.concatenate(held, axis=0)
+    box = {k: lax.dynamic_index_in_dim(sent, octant ^ k, 0, keepdims=False) for k in range(n_oct)}
+
+    def oct_step(bit):
+        moving = [k for k in range(n_oct) if k & bit]
+        load = jnp.concatenate([box[k] for k in moving], axis=0)
+        return load, over_oct(load, bit)
+
+    def unpack(bit, came):
+        moving = [k for k in range(n_oct) if k & bit]
+        rows = came.shape[0] // len(moving)
+        for i, k in enumerate(moving):
+            box[k] = came[i * rows : (i + 1) * rows]
+
+    def cube_step(bit, mine):
+        return jnp.concatenate([mine, over_cube(mine, bit)], axis=0)
+
+    oct_bits = [1 << i for i in range(log2(n_oct))]
+    cube_bits = [1 << i for i in range(1, log2(n_cube))]
+    mine = cube_step(cube_bits[0], multipole)
+    mine = after(mine, plan, sent)
+    anchor = [mine]
+    for bit in oct_bits[:-1]:
+        load, came = oct_step(bit)
+        unpack(bit, came)
+        anchor.append(load)
+    for bit in cube_bits[1:]:
+        mine = cube_step(bit, mine)
+    tables = lax.optimization_barrier((*tables, *anchor))[: len(tables)]
+    first = near_piece(0, cut, tables)
+
+    mine = after(mine, first)
     other = over_cube(mine, 1)
-    for k in range(1 + third, min(1 + 2 * third, n_oct)):
-        got[k] = over_oct(after(parts[k], near[1]), k)
-    tables = lax.optimization_barrier((*tables, mine))[:3]
-    near.append(near_piece(2, tables))
-    for k in range(1 + 2 * third, n_oct):
-        got[k] = over_oct(after(parts[k], near[2]), k)
-    tables = lax.optimization_barrier((*tables, near[2]))[:3]
-    near.append(near_piece(3, tables))
-    other, *payloads, last = lax.optimization_barrier(
-        (other, *[got[k] for k in range(n_oct)], near[3])
-    )
-    near[3] = last
+    for k in range(n_oct):
+        box[k] = after(box[k], first) if k > 0 else box[k]
+    load, came = oct_step(oct_bits[-1])
+    tables = lax.optimization_barrier((*tables, mine, load))[: len(tables)]
+    second = near_piece(cut, teams, tables)
+    other, second, came = lax.optimization_barrier((other, second, came))
+    unpack(oct_bits[-1], came)
+    payloads = [box[k] for k in range(n_oct)]
+    near = [first, second]
 
     klist = group_sources.shape[1]
     group = n_cube * boxes

time: 41.8 us -> 35 us (0.84)
  local copies, waits for them, and re-layouts: 7.39 us -> 4.23 us
  Pallas kernels: 23 us -> 20 us
    unnamed x35 -> x27, local copies, waits for them, and re-layouts: 7.12 us -> 3.95 us
    pallas_call x5 -> x3, Pallas kernels: 18.2 us -> 15.2 us  [the longest x2 13.7 us: near_piece(): pl.pallas_call(functools.partial(near_kernel, start=start, stop=stop), ou...]
    ppermute x3 -> x2, starting transfers between devices: 3.65 us -> 3.36 us  [over_oct(): return lax.ppermute(value, 'oct', [(i, i ^ k) for i in range(n_oct)])]
    ppermute x4 -> x3, starting transfers between devices: 5.86 us -> 5.82 us  [over_cube(): return lax.ppermute(value, 'cube', [(i, i ^ k) for i in range(n_cube)])]
  transfers between devices with their start and end apart: 7 -> 5, of which waited for: 1 -> 0; matrix products, arithmetic and copies ran while one was open for 1% -> 1% of each run, Pallas kernels for 48% -> 48%
where the time goes in v8:
time: 35 us; the launch traced here: 34.8 us
  Pallas kernels  20 us (57%)
  starting transfers between devices  9.18 us (26%)
  local copies, waits for them, and re-layouts  4.23 us (12%)
  matrix products  1.06 us (3%)
    pallas_call x2, Pallas kernels, near_piece(): pl.pallas_call(functools.partial(near_kernel, start=start, stop=stop), ou...  13.7 us
    ppermute x3, starting transfers between devices, over_cube(): return lax.ppermute(value, 'cube', [(i, i ^ k) for i in range(n_cube)])  5.82 us
    unnamed x27, local copies, waits for them, and re-layouts  3.95 us
    ppermute x2, starting transfers between devices, over_oct(): return lax.ppermute(value, 'oct', [(i, i ^ k) for i in range(n_oct)])  3.36 us
    pallas_call x1, Pallas kernels, body(): pl.pallas_call(functools.partial(far_kernel, blocks=n_cube, fanin=klist,...  3.19 us
    pallas_call x1, Pallas kernels, body(): pl.pallas_call(slot_kernel, out_shape=jax.ShapeDtypeStruct((n_oct, 2 * sl...  1.59 us
    pallas_call x1, Pallas kernels, body(): pl.pallas_call(plan_kernel, out_shape=(jax.ShapeDtypeStruct((8, boxes), j...  1.55 us
    dot_general x1, matrix products, body(): jnp.dot(strength, moment_map, preferred_element_type=F32).astype(BF16)  1.06 us
  transfers between devices with their start and end apart: 5, of which 0 were waited for; matrix products, arithmetic and copies ran while one was open for 1% of the time, Pallas kernels for 48%

profile of v8, /device:TPU:0, one launch (start us, length us, event | category | flops | bytes accessed | tf_op | source)
XLA Modules:
  0.0 34.8 jit_solution(7882430773114683863)
XLA Ops:
  0.0 0.8 %copy-done = bf16[128,128]{1,0:T(8,128)(2,1)S(1)} copy-done((bf16[128,128]{1,0:T(8,128)(2,1)S(1)}, bf16[128,128]{1,0:T(8,128)(2,1)}, u32[]{:S(2)}) %copy-start) | copy-done | bytes 32792
  0.8 1.1 %convolution_convert_fusion.m_ref = bf16[256,128]{1,0:T(8,128)(2,1)S(1)} fusion(bf16[128,128]{1,0:T(8,128)(2,1)S(1)} %copy-done, bf16[256,128]{1,0:T(8,128)(2,1)} %chg_ref.1, s32[256]{0:T(256)} %param.13), kind=kOutput, calls=%fused_computation | convolution fusion | flops 8486912 | bytes 164864 | tf_op jit(solution)/shard_map/dot_general | solution.py:310
  1.8 3.1 %collective-permute-start = (bf16[256,128]{1,0:T(8,128)(2,1)S(1)}, bf16[256,128]{1,0:T(8,128)(2,1)S(1)}, u32[]{:S(2)}, u32[]{:S(2)}) collective-permute-start(bf16[256,128]{1,0:T(8,128)(2,1)S(1)} %convolution_convert_fusion.m_ref), channel_id=1, source_target_pairs={{0,2},{1,3},{2,0},{3,1},{4,6},{5,7},{6,4},{7,5},{8,10},{9,11},{10,... | collective-permute-start | bytes 196616 | tf_op jit(solution)/shard_map/ppermute | solution.py:316
  4.9 0.7 %copy-done.9 = s32[1,1,4,64]{3,2,1,0:T(4,128)S(1)} copy-done((s32[1,1,4,64]{3,2,1,0:T(4,128)S(1)}, s32[1,1,4,64]{3,2,1,0:T(4,128)}, u32[]{:S(2)}) %copy-start.9) | copy-done | bytes 1048
  5.6 0.0 copy-done.7
  5.6 0.0 copy-done.6
  5.6 1.0 %copy-done.1 = bf16[16,128,128]{2,1,0:T(8,128)(2,1)S(1)} copy-done((bf16[16,128,128]{2,1,0:T(8,128)(2,1)S(1)}, bf16[16,128,128]{2,1,0:T(8,128)(2,1)}, u32[]{:S(2)}) %copy-start.1) | copy-done | bytes 524312
  6.7 1.6 %slots.1 = bf16[4,144,128]{2,1,0:T(8,128)(2,1)S(1)} custom-call(bf16[256,128]{1,0:T(8,128)(2,1)S(1)} %convolution_convert_fusion.m_ref, s32[4,4,64]{2,1,0:T(4,128)S(1)} %bitcast.21, s32[4,4,64]{2,1,0:T(4,128)S(1)} %bitcast.22, s32[4,64]{1,0:T(4,128)S(1)} %bitcast.24, bf16[2048,128]{1,0:T(8,128)(2,1)S(1)} %bitcast.19), custom_call_target="tpu_custom_call" | custom-call | flops 1000000000 | bytes 1000000 | tf_op jit(solution)/shard_map/slots/pallas_call | solution.py:360
  8.3 0.0 copy-start.3
  8.3 1.6 %collective-permute-start.3 = (bf16[288,128]{1,0:T(8,128)(2,1)S(1)}, bf16[288,128]{1,0:T(8,128)(2,1)S(1)}, u32[]{:S(2)}, u32[]{:S(2)}) collective-permute-start(bf16[288,128]{1,0:T(8,128)(2,1)S(1)} %pad_maximum_fusion.2), channel_id=1, source_target_pairs={{0,8},{8,0},{16,24},{24,16},{1,9},{9,1},{17,25},{25,17},{2,10},{10... | collective-permute-start | bytes 221192 | tf_op jit(solution)/shard_map/ppermute | solution.py:319
  9.9 0.7 %copy-done.8 = s32[256,4]{0,1:T(4,128)S(1)} copy-done((s32[256,4]{0,1:T(4,128)S(1)}, s32[256,4]{0,1:T(4,128)}, u32[]{:S(2)}) %copy-start.8) | copy-done | bytes 4120
  10.6 0.0 copy-done.10
  10.6 1.6 %plan.1 = (s32[8,256]{1,0:T(8,128)S(1)}, f32[2,256,128]{2,1,0:T(8,128)S(1)}, f32[6,256,128]{2,1,0:T(8,128)S(1)}, bf16[32,128,128]{2,1,0:T(8,128)(2,1)S(1)}) custom-call(s32[4,256]{1,0:T(4,128)S(1)} %bitcast.23, s32[2,128]{1,0:T(2,128)S(1)} %bitcast.25, bf16[256,128]{1,0:T(8,128)(2,1)S(1)} %copy-done.4, f32[3,256,128]{2,1,0:T(8,128)S(1)} %copy-done.3), custom_call_target="tpu_custom_call" | custom-call | flops 1000000000 | bytes 1000000 | tf_op jit(solution)/shard_map/plan/pallas_call | solution.py:324
  12.2 2.7 %collective-permute-start.1 = (bf16[512,128]{1,0:T(8,128)(2,1)S(1)}, bf16[512,128]{1,0:T(8,128)(2,1)S(1)}, u32[]{:S(2)}, u32[]{:S(2)}) collective-permute-start(bf16[512,128]{1,0:T(8,128)(2,1)S(1)} %pad_maximum_fusion.1), channel_id=1, source_target_pairs={{0,4},{1,5},{2,6},{3,7},{4,0},{5,1},{6,2},{7,3},{8,12},{9,13},{10,... | collective-permute-start | bytes 393224 | tf_op jit(solution)/shard_map/ppermute | solution.py:316
  14.8 7.2 %near.2.refs_6_ = f32[256,128]{1,0:T(8,128)S(1)} custom-call(s32[8,256]{1,0:T(8,128)S(1)} %get-tuple-element.23.plan_ref, f32[2,256,128]{2,1,0:T(8,128)S(1)} %get-tuple-element.34.rows_ref, f32[6,256,128]{2,1,0:T(8,128)S(1)} %get-tuple-element.35.coords_ref, bf16[32,128,128]{2,1,0:T(8,128)(2,1)S(1)} %get-tuple-element.36.left_ref), custom_call_target="tpu_custom_call" | custom-call | flops 200000000 | bytes 1000000 | tf_op jit(solution)/shard_map/near/pallas_call | solution.py:346
  22.1 0.0 copy-start.11
  22.2 0.0 copy-start.12
  22.2 0.1 collective-permute-start.2
  22.3 1.8 %collective-permute-start.4 = (bf16[288,128]{1,0:T(8,128)(2,1)S(1)}, bf16[288,128]{1,0:T(8,128)(2,1)S(1)}, u32[]{:S(2)}, u32[]{:S(2)}) collective-permute-start(bf16[288,128]{1,0:T(8,128)(2,1)S(1)} %constant_dynamic-update-slice_fusion), channel_id=1, source_target_pairs={{0,16},{8,24},{16,0},{24,8},{1,17},{9,25},{17,1},{25,9},{2,18},{10... | collective-permute-start | bytes 221192 | tf_op jit(solution)/shard_map/ppermute | solution.py:319
  24.1 0.1 copy.14
  24.2 0.1 reshape.10.refs_0_
  24.3 6.5 %near.3.refs_7_ = f32[256,128]{1,0:T(8,128)S(1)} custom-call(s32[8,256]{1,0:T(8,128)S(1)} %get-tuple-element.23.plan_ref, f32[2,256,128]{2,1,0:T(8,128)S(1)} %get-tuple-element.34.rows_ref, f32[6,256,128]{2,1,0:T(8,128)S(1)} %get-tuple-element.35.coords_ref, bf16[32,128,128]{2,1,0:T(8,128)(2,1)S(1)} %get-tuple-element.36.left_ref), custom_call_target="tpu_custom_call" | custom-call | flops 200000000 | bytes 1000000 | tf_op jit(solution)/shard_map/near/pallas_call | solution.py:346
  30.9 0.7 %copy-done.5 = bf16[128,128]{1,0:T(8,128)(2,1)S(1)} copy-done((bf16[128,128]{1,0:T(8,128)(2,1)S(1)}, bf16[128,128]{1,0:T(8,128)(2,1)}, u32[]{:S(2)}) %copy-start.5) | copy-done | bytes 32792
  31.6 3.2 %far.1 = f32[256,128]{1,0:T(8,128)} custom-call(s32[16,128]{1,0:T(8,128)S(1)} %reshape.10.refs_0_, s32[2,128]{1,0:T(2,128)S(1)} %bitcast.26, bf16[2048,128]{1,0:T(8,128)(2,1)S(1)} %bitcast.20, bf16[128,128]{1,0:T(8,128)(2,1)S(1)} %copy-done.5, bf16[1024,128]{1,0:T(8,128)(2,1)S(1)} %pad_maximum_fusion.refs_4_, ...), custom_call_target="tpu_custom_call" | custom-call | flops 3000000000 | bytes 2000000 | tf_op jit(solution)/shard_map/far/pallas_call | solution.py:423
  (29 shorter events, 0.1 us)
Async XLA Ops:
  0.0 0.8 %copy-start = (bf16[128,128]{1,0:T(8,128)(2,1)S(1)}, bf16[128,128]{1,0:T(8,128)(2,1)}, u32[]{:S(2)}) copy-start(bf16[128,128]{1,0:T(8,128)(2,1)} %param.15) | copy-start | bytes 98308
  1.8 10.3 %collective-permute-start = (bf16[256,128]{1,0:T(8,128)(2,1)S(1)}, bf16[256,128]{1,0:T(8,128)(2,1)S(1)}, u32[]{:S(2)}, u32[]{:S(2)}) collective-permute-start(bf16[256,128]{1,0:T(8,128)(2,1)S(1)} %convolution_convert_fusion.m_ref), channel_id=1, source_target_pairs={{0,2},{1,3},{2,0},{3,1},{4,6},{5,7},{6,4},{7,5},{8,10},{9,11},{10,... | collective-permute-start | bytes 196616 | tf_op jit(solution)/shard_map/ppermute | solution.py:316
  4.9 0.7 %copy-start.9 = (s32[1,1,4,64]{3,2,1,0:T(4,128)S(1)}, s32[1,1,4,64]{3,2,1,0:T(4,128)}, u32[]{:S(2)}) copy-start(s32[1,1,4,64]{3,2,1,0:T(4,128)} %param.23) | copy-start | bytes 3076
  4.9 0.7 %copy-start.7 = (s32[1,1,4,64,4]{3,4,2,1,0:T(4,128)S(1)}, s32[1,1,4,64,4]{3,4,2,1,0:T(4,128)}, u32[]{:S(2)}) copy-start(s32[1,1,4,64,4]{3,4,2,1,0:T(4,128)} %param.22) | copy-start | bytes 12292
  4.9 0.7 %copy-start.6 = (s32[1,1,4,64,4]{3,4,2,1,0:T(4,128)S(1)}, s32[1,1,4,64,4]{3,4,2,1,0:T(4,128)}, u32[]{:S(2)}) copy-start(s32[1,1,4,64,4]{3,4,2,1,0:T(4,128)} %param.21) | copy-start | bytes 12292
  5.6 1.0 %copy-start.1 = (bf16[16,128,128]{2,1,0:T(8,128)(2,1)S(1)}, bf16[16,128,128]{2,1,0:T(8,128)(2,1)}, u32[]{:S(2)}) copy-start(bf16[16,128,128]{2,1,0:T(8,128)(2,1)} %param.16) | copy-start | bytes 1572868
  6.7 3.2 %copy-start.4 = (bf16[256,128]{1,0:T(8,128)(2,1)S(1)}, bf16[256,128]{1,0:T(8,128)(2,1)}, u32[]{:S(2)}) copy-start(bf16[256,128]{1,0:T(8,128)(2,1)} %chg_ref.1) | copy-start | bytes 196612
  8.3 1.6 %copy-start.3 = (f32[3,256,128]{2,1,0:T(8,128)S(1)}, f32[3,256,128]{2,1,0:T(8,128)}, u32[]{:S(2)}) copy-start(f32[3,256,128]{2,1,0:T(8,128)} %pos_ref.1) | copy-start | bytes 1179652
  8.3 13.7 %collective-permute-start.3 = (bf16[288,128]{1,0:T(8,128)(2,1)S(1)}, bf16[288,128]{1,0:T(8,128)(2,1)S(1)}, u32[]{:S(2)}, u32[]{:S(2)}) collective-permute-start(bf16[288,128]{1,0:T(8,128)(2,1)S(1)} %pad_maximum_fusion.2), channel_id=1, source_target_pairs={{0,8},{8,0},{16,24},{24,16},{1,9},{9,1},{17,25},{25,17},{2,10},{10... | collective-permute-start | bytes 221192 | tf_op jit(solution)/shard_map/ppermute | solution.py:319
  9.9 0.7 %copy-start.8 = (s32[256,4]{0,1:T(4,128)S(1)}, s32[256,4]{0,1:T(4,128)}, u32[]{:S(2)}) copy-start(s32[256,4]{0,1:T(4,128)} %param.18) | copy-start | bytes 12292
  9.9 0.7 %copy-start.10 = (s32[256]{0:T(256)S(1)}, s32[256]{0:T(256)}, u32[]{:S(2)}) copy-start(s32[256]{0:T(256)} %param.13) | copy-start | bytes 3076
  12.2 9.9 %collective-permute-start.1 = (bf16[512,128]{1,0:T(8,128)(2,1)S(1)}, bf16[512,128]{1,0:T(8,128)(2,1)S(1)}, u32[]{:S(2)}, u32[]{:S(2)}) collective-permute-start(bf16[512,128]{1,0:T(8,128)(2,1)S(1)} %pad_maximum_fusion.1), channel_id=1, source_target_pairs={{0,4},{1,5},{2,6},{3,7},{4,0},{5,1},{6,2},{7,3},{8,12},{9,13},{10,... | collective-permute-start | bytes 393224 | tf_op jit(solution)/shard_map/ppermute | solution.py:316
  22.1 1.9 %copy-start.11 = (s32[256,8]{0,1:T(8,128)S(1)}, s32[256,8]{0,1:T(8,128)}, u32[]{:S(2)}) copy-start(s32[256,8]{0,1:T(8,128)} %param.20) | copy-start | bytes 24580
  22.2 1.9 %copy-start.12 = (s32[256,8]{0,1:T(8,128)S(1)}, s32[256,8]{0,1:T(8,128)}, u32[]{:S(2)}) copy-start(s32[256,8]{0,1:T(8,128)} %param.19) | copy-start | bytes 24580
  22.2 8.7 %collective-permute-start.2 = (bf16[1024,128]{1,0:T(8,128)(2,1)S(1)}, bf16[1024,128]{1,0:T(8,128)(2,1)S(1)}, u32[]{:S(2)}, u32[]{:S(2)}) collective-permute-start(bf16[1024,128]{1,0:T(8,128)(2,1)S(1)} %pad_maximum_fusion.refs_4_), channel_id=1, source_target_pairs={{0,1},{1,0},{2,3},{3,2},{4,5},{5,4},{6,7},{7,6},{8,9},{9,8},{10,11... | collective-permute-start | bytes 786440 | tf_op jit(solution)/shard_map/ppermute | solution.py:316
  22.3 8.6 %collective-permute-start.4 = (bf16[288,128]{1,0:T(8,128)(2,1)S(1)}, bf16[288,128]{1,0:T(8,128)(2,1)S(1)}, u32[]{:S(2)}, u32[]{:S(2)}) collective-permute-start(bf16[288,128]{1,0:T(8,128)(2,1)S(1)} %constant_dynamic-update-slice_fusion), channel_id=1, source_target_pairs={{0,16},{8,24},{16,0},{24,8},{1,17},{9,25},{17,1},{25,9},{2,18},{10... | collective-permute-start | bytes 221192 | tf_op jit(solution)/shard_map/ppermute | solution.py:319
  24.3 6.5 %copy-start.2 = (bf16[16,128,128]{2,1,0:T(8,128)(2,1)S(1)}, bf16[16,128,128]{2,1,0:T(8,128)(2,1)}, u32[]{:S(2)}) copy-start(bf16[16,128,128]{2,1,0:T(8,128)(2,1)} %param.16) | copy-start | bytes 1572868
  30.8 0.8 %copy-start.5 = (bf16[128,128]{1,0:T(8,128)(2,1)S(1)}, bf16[128,128]{1,0:T(8,128)(2,1)}, u32[]{:S(2)}) copy-start(bf16[128,128]{1,0:T(8,128)(2,1)} %refs_3_.1) | copy-start | bytes 98308

commit v9 on v8

--- a/solution.py
+++ b/solution.py
@@ -55,7 +55,29 @@
     return jnp.dot(a, b, preferred_element_type=F32)
 
 
-def slot_kernel(m_ref, src_ref, pat_ref, tgt_ref, ops_ref, out_ref, sums):
+def front_kernel(*refs):
+    strength_ref, count_ref, out_ref = refs[3:6]
+    chg_ref, cnt_ref, map_ref = refs[6:9]
+    for copy in fetch(refs[:3], refs[6:9], refs[9]):
+        copy.wait()
+    boxes = chg_ref.shape[0]
+    live = iota((boxes, LANES), 1) < count_columns(cnt_ref, boxes)
+    strength = jnp.where(live, chg_ref[...].astype(F32), 0.0)
+    strength_ref[...] = strength
+    count_ref[...] = cnt_ref[...]
+    out_ref[...] = dot(strength.astype(BF16), map_ref[...]).astype(BF16)
+
+
+def fetch(sources, targets, sems):
+    copies = [
+        pltpu.make_async_copy(s, t, sems.at[i]) for i, (s, t) in enumerate(zip(sources, targets))
+    ]
+    for copy in copies:
+        copy.start()
+    return copies
+
+
+def slot_stage(m_ref, src_ref, pat_ref, tgt_ref, ops_ref, out_ref, sums, operators_here):
     boxes, width = m_ref.shape
     patterns = ops_ref.shape[0] // width
     groups, fanin, slots = src_ref.shape
@@ -83,6 +105,7 @@
             sums[d * slots : (d + 1) * slots, p * width : (p + 1) * width] = s[
                 p * slots : (p + 1) * slots
             ]
+    operators_here.wait()
     result = dot(sums[...], ops_ref[...])
     hi = result.astype(BF16)
     lo = (result - hi.astype(F32)).astype(BF16)
@@ -95,13 +118,17 @@
         ).astype(BF16)
 
 
-def plan_kernel(
-    nb_ref, cnt_ref, chg_ref, pos_ref, plan_ref, rows_ref, coords_ref, left_ref, ranked
-):
-    boxes = chg_ref.shape[0]
+def plan_kernel(*refs):
+    cnt_ref, strength_ref, m_ref = refs[:3]
+    plan_ref, rows_ref, coords_ref, left_ref, sent_ref = refs[9:14]
+    ranked, sums = refs[14:16]
+    here = refs[16:22]
+    nb_ref, pos_ref, src_ref, pat_ref, tgt_ref, ops_ref = here
+    copies = fetch(refs[3:9], here, refs[22])
+    boxes = strength_ref.shape[0]
     column = count_columns(cnt_ref, boxes)
     row = jnp.concatenate([cnt_ref[i : i + 1, :] for i in range(boxes // LANES)], axis=1)
-    rows_ref[1] = jnp.where(iota((boxes, LANES), 1) < column, chg_ref[...].astype(F32), 0.0)
+    rows_ref[1] = strength_ref[...]
 
     down, across = iota((boxes, boxes), 0), iota((boxes, boxes), 1)
     ahead = (column < row) | ((column == row) & (down < across))
@@ -111,6 +138,7 @@
     to_rank = jnp.where(rank_row == down.astype(F32), 1.0, 0.0).astype(BF16)
     from_rank = jnp.where(rank_column == across.astype(F32), 1.0, 0.0).astype(BF16)
 
+    copies[0].wait()
     lists = jnp.concatenate(
         [
             nb_ref[...].astype(F32),
@@ -125,6 +153,7 @@
     ends = jnp.sum(within, axis=0, keepdims=True).astype(jnp.int32) >> log2(TEAM)
     plan_ref[...] = jnp.where(iota((8, boxes), 0) == nb_ref.shape[0] + 2, ends, plan)
 
+    copies[1].wait()
     norm = jnp.zeros((boxes, LANES), F32)
     parts = []
     for c in range(3):
@@ -154,6 +183,9 @@
         return carry
 
     lax.fori_loop(0, boxes // 8, build, 0, unroll=4)
+    for copy in copies[2:5]:
+        copy.wait()
+    slot_stage(m_ref, src_ref, pat_ref, tgt_ref, ops_ref, sent_ref, sums, copies[5])
 
 
 def near_kernel(plan_ref, rows_ref, coords_ref, left_ref, out_ref, right, *, start, stop):
@@ -214,10 +246,11 @@
 
 
 def far_kernel(*refs, blocks, fanin, pieces):
-    code_ref, cnt_ref, ops_ref, eval_ref, mine_ref, other_ref = refs[:6]
+    code_ref, cnt_ref, ops_hbm, eval_hbm, mine_ref, other_ref = refs[:6]
     near_refs = refs[6 : 6 + pieces]
-    pay_refs = refs[6 + pieces : -2]
-    out_ref, sums = refs[-2:]
+    pay_refs = refs[6 + pieces : -5]
+    out_ref, sums, ops_ref, eval_ref, sems = refs[-5:]
+    copies = fetch((ops_hbm, eval_hbm), (ops_ref, eval_ref), sems)
     width = mine_ref.shape[1]
     boxes = mine_ref.shape[0] // (blocks // 2)
     patterns = ops_ref.shape[0] // width
@@ -256,6 +289,8 @@
                 sums[i * per : (i + 1) * per, p * width : (p + 1) * width] = s[
                     p * per : (p + 1) * per
                 ]
+    for copy in copies:
+        copy.wait()
     near_local = dot(sums[...], ops_ref[...])
     hits = []
     values = []
@@ -276,8 +311,15 @@
 
 
 VMEM = pl.BlockSpec(memory_space=pltpu.VMEM)
+HBM = pl.BlockSpec(memory_space=pltpu.HBM)
 SMEM = pl.BlockSpec(memory_space=pltpu.SMEM)
 MIB = 1024 * 1024
+
+
+def in_hbm(value):
+    return pltpu.with_memory_space_constraint(value, pltpu.HBM)
+
+
 PIECES = 2
 TEAM = 16
 STEP = 16
@@ -304,10 +346,23 @@
     patterns = translations.shape[0]
     operators = translations.reshape(patterns * width, width)
     counts = panel_counts.reshape(boxes // LANES, LANES)
-    slot_index = jnp.arange(panels, dtype=jnp.int32)
-    live = slot_index[None, :] < panel_counts[:, None]
-    strength = jnp.where(live, charges, jnp.zeros_like(charges))
-    multipole = jnp.dot(strength, moment_map, preferred_element_type=F32).astype(BF16)
+    strength, counts, multipole = pl.pallas_call(
+        front_kernel,
+        out_shape=(
+            jax.ShapeDtypeStruct((boxes, panels), F32),
+            jax.ShapeDtypeStruct(counts.shape, jnp.int32),
+            jax.ShapeDtypeStruct((boxes, width), BF16),
+        ),
+        in_specs=[HBM] * 3,
+        out_specs=(VMEM,) * 3,
+        scratch_shapes=[pltpu.VMEM(v.shape, v.dtype) for v in (charges, counts, moment_map)]
+        + [pltpu.SemaphoreType.DMA((3,))],
+        compiler_params=pltpu.CompilerParams(vmem_limit_bytes=8 * MIB),
+        cost_estimate=pl.CostEstimate(
+            flops=10_000_000, bytes_accessed=300_000, transcendentals=0
+        ),
+        name="front",
+    )(in_hbm(charges), in_hbm(counts), in_hbm(moment_map))
 
     me = lax.axis_index("cube")
     octant = lax.axis_index("oct")
@@ -321,23 +376,38 @@
     def after(value, *earlier):
         return lax.optimization_barrier((value, *earlier))[0]
 
-    plan, *tables = pl.pallas_call(
+    slots, fanin = remote_sources.shape[3:]
+    fetched = (
+        near_boxes.T,
+        positions,
+        remote_sources[0, 0].transpose(0, 2, 1),
+        remote_patterns[0, 0].transpose(0, 2, 1),
+        remote_targets[0, 0],
+        operators,
+    )
+    plan, *tables, sent = pl.pallas_call(
         plan_kernel,
         out_shape=(
             jax.ShapeDtypeStruct((8, boxes), jnp.int32),
             jax.ShapeDtypeStruct((2, boxes, panels), F32),
             jax.ShapeDtypeStruct((6, boxes, panels), F32),
             jax.ShapeDtypeStruct((boxes // 8, panels, LANES), BF16),
+            jax.ShapeDtypeStruct((n_oct, 2 * slots + 16, width), BF16),
         ),
-        in_specs=[VMEM] * 4,
-        out_specs=(VMEM,) * 4,
-        scratch_shapes=[pltpu.VMEM((boxes, 9 * LANES), F32)],
-        compiler_params=pltpu.CompilerParams(vmem_limit_bytes=12 * MIB),
+        in_specs=[VMEM] * 3 + [HBM] * len(fetched),
+        out_specs=(VMEM,) * 5,
+        scratch_shapes=[
+            pltpu.VMEM((boxes, 9 * LANES), F32),
+            pltpu.VMEM((n_oct * slots, patterns * width), BF16),
+        ]
+        + [pltpu.VMEM(v.shape, v.dtype) for v in fetched]
+        + [pltpu.SemaphoreType.DMA((len(fetched),))],
+        compiler_params=pltpu.CompilerParams(vmem_limit_bytes=16 * MIB),
         cost_estimate=pl.CostEstimate(
-            flops=1_000_000_000, bytes_accessed=1_000_000, transcendentals=0
+            flops=1_000_000_000, bytes_accessed=2_000_000, transcendentals=0
         ),
         name="plan",
-    )(near_boxes.T, counts, charges, positions)
+    )(counts, strength, multipole, *map(in_hbm, fetched))
 
     teams = boxes // TEAM
     cut = teams * 5 // 8
@@ -356,25 +426,6 @@
             name="near",
         )(plan, *tables)
 
-    slots, fanin = remote_sources.shape[3:]
-    sent = pl.pallas_call(
-        slot_kernel,
-        out_shape=jax.ShapeDtypeStruct((n_oct, 2 * slots + 16, width), BF16),
-        in_specs=[VMEM] * 5,
-        out_specs=VMEM,
-        scratch_shapes=[pltpu.VMEM((n_oct * slots, patterns * width), BF16)],
-        compiler_params=pltpu.CompilerParams(vmem_limit_bytes=8 * MIB),
-        cost_estimate=pl.CostEstimate(
-            flops=1_000_000_000, bytes_accessed=1_000_000, transcendentals=0
-        ),
-        name="slots",
-    )(
-        multipole,
-        remote_sources[0, 0].transpose(0, 2, 1),
-        remote_patterns[0, 0].transpose(0, 2, 1),
-        remote_targets[0, 0],
-        operators,
-    )
     box = {k: lax.dynamic_index_in_dim(sent, octant ^ k, 0, keepdims=False) for k in range(n_oct)}
 
     def oct_step(bit):
@@ -423,15 +474,29 @@
     return pl.pallas_call(
         functools.partial(far_kernel, blocks=n_cube, fanin=klist, pieces=PIECES),
         out_shape=jax.ShapeDtypeStruct((boxes, panels), F32),
-        in_specs=[VMEM] * (6 + PIECES + n_oct),
+        in_specs=[VMEM] * 2 + [HBM] * 2 + [VMEM] * (2 + PIECES + n_oct),
         out_specs=VMEM,
-        scratch_shapes=[pltpu.VMEM((boxes, patterns * width), BF16)],
+        scratch_shapes=[
+            pltpu.VMEM((boxes, patterns * width), BF16),
+            pltpu.VMEM(operators.shape, BF16),
+            pltpu.VMEM(evaluation.shape, BF16),
+            pltpu.SemaphoreType.DMA((2,)),
+        ],
         compiler_params=pltpu.CompilerParams(vmem_limit_bytes=24 * MIB),
         cost_estimate=pl.CostEstimate(
             flops=3_000_000_000, bytes_accessed=2_000_000, transcendentals=0
         ),
         name="far",
-    )(code.reshape(-1, LANES), counts, operators, evaluation, mine, other, *near, *payloads)
+    )(
+        code.reshape(-1, LANES),
+        counts,
+        in_hbm(operators),
+        in_hbm(evaluation),
+        mine,
+        other,
+        *near,
+        *payloads,
+    )
 
 
 def solution(mesh):

time: 35 us -> 33.2 us (0.949)
  local copies, waits for them, and re-layouts: 4.23 us -> 0.3 us
  Pallas kernels: 20 us -> 23 us
  matrix products: 1.06 us -> 0 us
    unnamed x27 -> x5, local copies, waits for them, and re-layouts: 3.95 us -> 0.02 us
    pallas_call x1, Pallas kernels: 1.55 us -> 4.36 us  [body(): pl.pallas_call(plan_kernel, out_shape=(jax.ShapeDtypeStruct((8, boxes), j...]
    dot_general x1 -> x0, matrix products: 1.06 us -> none  [body(): jnp.dot(strength, moment_map, preferred_element_type=F32).astype(BF16)]
    pallas_call x1, Pallas kernels: 3.19 us -> 3.9 us  [body(): pl.pallas_call(functools.partial(far_kernel, blocks=n_cube, fanin=klist,...]
    pallas_call x1, Pallas kernels: 1.59 us -> 1.23 us  [body(): pl.pallas_call(front_kernel, out_shape=(jax.ShapeDtypeStruct((boxes, pane...]
  transfers between devices with their start and end apart: 5 -> 5, of which waited for: 0 -> 0; matrix products, arithmetic and copies ran while one was open for 1% -> 1% of each run, Pallas kernels for 48% -> 54%
where the time goes in v9:
time: 33.2 us; the launch traced here: 32.8 us
  Pallas kernels  23 us (69%)
  starting transfers between devices  9.18 us (28%)
    pallas_call x2, Pallas kernels, near_piece(): pl.pallas_call(functools.partial(near_kernel, start=start, stop=stop), ou...  13.5 us
    ppermute x3, starting transfers between devices, over_cube(): return lax.ppermute(value, 'cube', [(i, i ^ k) for i in range(n_cube)])  5.81 us
    pallas_call x1, Pallas kernels, body(): pl.pallas_call(plan_kernel, out_shape=(jax.ShapeDtypeStruct((8, boxes), j...  4.36 us
    pallas_call x1, Pallas kernels, body(): pl.pallas_call(functools.partial(far_kernel, blocks=n_cube, fanin=klist,...  3.9 us
    ppermute x2, starting transfers between devices, over_oct(): return lax.ppermute(value, 'oct', [(i, i ^ k) for i in range(n_oct)])  3.37 us
    pallas_call x1, Pallas kernels, body(): pl.pallas_call(front_kernel, out_shape=(jax.ShapeDtypeStruct((boxes, pane...  1.23 us
  transfers between devices with their start and end apart: 5, of which 0 were waited for; matrix products, arithmetic and copies ran while one was open for 1% of the time, Pallas kernels for 54%

profile of v9, /device:TPU:0, one launch (start us, length us, event | category | flops | bytes accessed | tf_op | source)
XLA Modules:
  0.0 32.8 jit_solution(11897508309564894256)
XLA Ops:
  0.0 1.2 %front.1 = (f32[256,128]{1,0:T(8,128)S(1)}, s32[2,128]{1,0:T(2,128)S(1)}, bf16[256,128]{1,0:T(8,128)(2,1)S(1)}) custom-call(bf16[256,128]{1,0:T(8,128)(2,1)} %refs_0_.1, s32[2,128]{1,0:T(2,128)} %bitcast.18, bf16[128,128]{1,0:T(8,128)(2,1)} %refs_2_.1), custom_call_target="tpu_custom_call" | custom-call | flops 10000000 | bytes 300000 | tf_op jit(solution)/shard_map/front/pallas_call | solution.py:349
  1.2 3.1 %collective-permute-start = (bf16[256,128]{1,0:T(8,128)(2,1)S(1)}, bf16[256,128]{1,0:T(8,128)(2,1)S(1)}, u32[]{:S(2)}, u32[]{:S(2)}) collective-permute-start(bf16[256,128]{1,0:T(8,128)(2,1)S(1)} %get-tuple-element.28.refs_2_), channel_id=1, source_target_pairs={{0,2},{1,3},{2,0},{3,1},{4,6},{5,7},{6,4},{7,5},{8,10},{9,11},{10,... | collective-permute-start | bytes 196616 | tf_op jit(solution)/shard_map/ppermute | solution.py:371
  4.3 4.4 %plan.1 = (s32[8,256]{1,0:T(8,128)S(1)}, f32[2,256,128]{2,1,0:T(8,128)S(1)}, f32[6,256,128]{2,1,0:T(8,128)S(1)}, bf16[32,128,128]{2,1,0:T(8,128)(2,1)S(1)}, bf16[4,144,128]{2,1,0:T(8,128)(2,1)S(1)}) custom-call(s32[2,128]{1,0:T(2,128)S(1)} %get-tuple-element.27.refs_0_.refs_1_, f32[256,128]{1,0:T(8,128)S(1)} %get-tuple-element.29.refs_1_, ...), custom_call_target="tpu_custom_call" | custom-call | flops 1000000000 | bytes 2000000 | tf_op jit(solution)/shard_map/plan/pallas_call | solution.py:388
  8.7 1.6 %collective-permute-start.3 = (bf16[288,128]{1,0:T(8,128)(2,1)S(1)}, bf16[288,128]{1,0:T(8,128)(2,1)S(1)}, u32[]{:S(2)}, u32[]{:S(2)}) collective-permute-start(bf16[288,128]{1,0:T(8,128)(2,1)S(1)} %pad_maximum_fusion.2), channel_id=1, source_target_pairs={{0,8},{8,0},{16,24},{24,16},{1,9},{9,1},{17,25},{25,17},{2,10},{10... | collective-permute-start | bytes 221192 | tf_op jit(solution)/shard_map/ppermute | solution.py:374
  10.3 0.0 collective-permute-done
  10.3 2.7 %collective-permute-start.1 = (bf16[512,128]{1,0:T(8,128)(2,1)S(1)}, bf16[512,128]{1,0:T(8,128)(2,1)S(1)}, u32[]{:S(2)}, u32[]{:S(2)}) collective-permute-start(bf16[512,128]{1,0:T(8,128)(2,1)S(1)} %pad_maximum_fusion.1), channel_id=1, source_target_pairs={{0,4},{1,5},{2,6},{3,7},{4,0},{5,1},{6,2},{7,3},{8,12},{9,13},{10,... | collective-permute-start | bytes 393224 | tf_op jit(solution)/shard_map/ppermute | solution.py:371
  13.0 7.1 %near.2.refs_6_ = f32[256,128]{1,0:T(8,128)S(1)} custom-call(s32[8,256]{1,0:T(8,128)S(1)} %get-tuple-element.30.plan_ref, f32[2,256,128]{2,1,0:T(8,128)S(1)} %get-tuple-element.42.rows_ref, f32[6,256,128]{2,1,0:T(8,128)S(1)} %get-tuple-element.43.coords_ref, bf16[32,128,128]{2,1,0:T(8,128)(2,1)S(1)} %get-tuple-element.44.left_ref), custom_call_target="tpu_custom_call" | custom-call | flops 200000000 | bytes 1000000 | tf_op jit(solution)/shard_map/near/pallas_call | solution.py:416
  20.1 0.0 collective-permute-done.3
  20.1 0.0 collective-permute-done.1
  20.2 0.0 copy-start
  20.2 0.0 copy-start.1
  20.2 0.1 collective-permute-start.2
  20.3 1.8 %collective-permute-start.4 = (bf16[288,128]{1,0:T(8,128)(2,1)S(1)}, bf16[288,128]{1,0:T(8,128)(2,1)S(1)}, u32[]{:S(2)}, u32[]{:S(2)}) collective-permute-start(bf16[288,128]{1,0:T(8,128)(2,1)S(1)} %constant_dynamic-update-slice_fusion), channel_id=1, source_target_pairs={{0,16},{8,24},{16,0},{24,8},{1,17},{9,25},{17,1},{25,9},{2,18},{10... | collective-permute-start | bytes 221192 | tf_op jit(solution)/shard_map/ppermute | solution.py:374
  22.1 0.0 copy-done
  22.1 0.0 copy-done.1
  22.1 0.1 copy.14
  22.3 0.1 reshape.9.refs_0_
  22.4 6.4 %near.3.refs_7_ = f32[256,128]{1,0:T(8,128)S(1)} custom-call(s32[8,256]{1,0:T(8,128)S(1)} %get-tuple-element.30.plan_ref, f32[2,256,128]{2,1,0:T(8,128)S(1)} %get-tuple-element.42.rows_ref, f32[6,256,128]{2,1,0:T(8,128)S(1)} %get-tuple-element.43.coords_ref, bf16[32,128,128]{2,1,0:T(8,128)(2,1)S(1)} %get-tuple-element.44.left_ref), custom_call_target="tpu_custom_call" | custom-call | flops 200000000 | bytes 1000000 | tf_op jit(solution)/shard_map/near/pallas_call | solution.py:416
  28.7 0.0 collective-permute-done.4
  28.7 0.0 collective-permute-done.2.refs_5_
  28.8 3.9 %far.1 = f32[256,128]{1,0:T(8,128)} custom-call(s32[16,128]{1,0:T(8,128)S(1)} %reshape.9.refs_0_, s32[2,128]{1,0:T(2,128)S(1)} %get-tuple-element.27.refs_0_.refs_1_, bf16[2048,128]{1,0:T(8,128)(2,1)} %bitcast.20, bf16[128,128]{1,0:T(8,128)(2,1)} %refs_3_.1, bf16[1024,128]{1,0:T(8,128)(2,1)S(1)} %pad_maximum_fusion.refs_4_, ...), custom_call_target="tpu_custom_call" | custom-call | flops 3000000000 | bytes 2000000 | tf_op jit(solution)/shard_map/far/pallas_call | solution.py:474
  (9 shorter events, 0.1 us)
Async XLA Ops:
  1.2 9.1 %collective-permute-start = (bf16[256,128]{1,0:T(8,128)(2,1)S(1)}, bf16[256,128]{1,0:T(8,128)(2,1)S(1)}, u32[]{:S(2)}, u32[]{:S(2)}) collective-permute-start(bf16[256,128]{1,0:T(8,128)(2,1)S(1)} %get-tuple-element.28.refs_2_), channel_id=1, source_target_pairs={{0,2},{1,3},{2,0},{3,1},{4,6},{5,7},{6,4},{7,5},{8,10},{9,11},{10,... | collective-permute-start | bytes 196616 | tf_op jit(solution)/shard_map/ppermute | solution.py:371
  8.7 11.4 %collective-permute-start.3 = (bf16[288,128]{1,0:T(8,128)(2,1)S(1)}, bf16[288,128]{1,0:T(8,128)(2,1)S(1)}, u32[]{:S(2)}, u32[]{:S(2)}) collective-permute-start(bf16[288,128]{1,0:T(8,128)(2,1)S(1)} %pad_maximum_fusion.2), channel_id=1, source_target_pairs={{0,8},{8,0},{16,24},{24,16},{1,9},{9,1},{17,25},{25,17},{2,10},{10... | collective-permute-start | bytes 221192 | tf_op jit(solution)/shard_map/ppermute | solution.py:374
  10.3 9.8 %collective-permute-start.1 = (bf16[512,128]{1,0:T(8,128)(2,1)S(1)}, bf16[512,128]{1,0:T(8,128)(2,1)S(1)}, u32[]{:S(2)}, u32[]{:S(2)}) collective-permute-start(bf16[512,128]{1,0:T(8,128)(2,1)S(1)} %pad_maximum_fusion.1), channel_id=1, source_target_pairs={{0,4},{1,5},{2,6},{3,7},{4,0},{5,1},{6,2},{7,3},{8,12},{9,13},{10,... | collective-permute-start | bytes 393224 | tf_op jit(solution)/shard_map/ppermute | solution.py:371
  20.2 1.9 %copy-start = (s32[256,8]{0,1:T(8,128)S(1)}, s32[256,8]{0,1:T(8,128)}, u32[]{:S(2)}) copy-start(s32[256,8]{0,1:T(8,128)} %param.20) | copy-start | bytes 24580
  20.2 1.9 %copy-start.1 = (s32[256,8]{0,1:T(8,128)S(1)}, s32[256,8]{0,1:T(8,128)}, u32[]{:S(2)}) copy-start(s32[256,8]{0,1:T(8,128)} %param.19) | copy-start | bytes 24580
  20.2 8.5 %collective-permute-start.2 = (bf16[1024,128]{1,0:T(8,128)(2,1)S(1)}, bf16[1024,128]{1,0:T(8,128)(2,1)S(1)}, u32[]{:S(2)}, u32[]{:S(2)}) collective-permute-start(bf16[1024,128]{1,0:T(8,128)(2,1)S(1)} %pad_maximum_fusion.refs_4_), channel_id=1, source_target_pairs={{0,1},{1,0},{2,3},{3,2},{4,5},{5,4},{6,7},{7,6},{8,9},{9,8},{10,11... | collective-permute-start | bytes 786440 | tf_op jit(solution)/shard_map/ppermute | solution.py:371
  20.3 8.4 %collective-permute-start.4 = (bf16[288,128]{1,0:T(8,128)(2,1)S(1)}, bf16[288,128]{1,0:T(8,128)(2,1)S(1)}, u32[]{:S(2)}, u32[]{:S(2)}) collective-permute-start(bf16[288,128]{1,0:T(8,128)(2,1)S(1)} %constant_dynamic-update-slice_fusion), channel_id=1, source_target_pairs={{0,16},{8,24},{16,0},{24,8},{1,17},{9,25},{17,1},{25,9},{2,18},{10... | collective-permute-start | bytes 221192 | tf_op jit(solution)/shard_map/ppermute | solution.py:374

commit v10 on v9

--- a/solution.py
+++ b/solution.py
@@ -55,10 +55,15 @@
     return jnp.dot(a, b, preferred_element_type=F32)
 
 
-def front_kernel(*refs):
-    strength_ref, count_ref, out_ref = refs[3:6]
-    chg_ref, cnt_ref, map_ref = refs[6:9]
-    for copy in fetch(refs[:3], refs[6:9], refs[9]):
+def front_kernel(*refs, extra):
+    strength_ref, count_ref, out_ref = refs[3 + extra : 6 + extra]
+    chg_ref, cnt_ref, map_ref = refs[6 + 2 * extra : 9 + 2 * extra]
+    copies = fetch(
+        refs[: 3 + extra],
+        (chg_ref, cnt_ref, map_ref, *refs[6 + extra : 6 + 2 * extra]),
+        refs[-1],
+    )
+    for copy in copies[:3]:
         copy.wait()
     boxes = chg_ref.shape[0]
     live = iota((boxes, LANES), 1) < count_columns(cnt_ref, boxes)
@@ -66,6 +71,8 @@
     strength_ref[...] = strength
     count_ref[...] = cnt_ref[...]
     out_ref[...] = dot(strength.astype(BF16), map_ref[...]).astype(BF16)
+    for copy in copies[3:]:
+        copy.wait()
 
 
 def fetch(sources, targets, sems):
@@ -119,12 +126,11 @@
 
 
 def plan_kernel(*refs):
-    cnt_ref, strength_ref, m_ref = refs[:3]
+    cnt_ref, strength_ref, m_ref, nb_ref, pos_ref, src_ref, pat_ref, tgt_ref, ops_hbm = refs[:9]
     plan_ref, rows_ref, coords_ref, left_ref, sent_ref = refs[9:14]
-    ranked, sums = refs[14:16]
-    here = refs[16:22]
-    nb_ref, pos_ref, src_ref, pat_ref, tgt_ref, ops_ref = here
-    copies = fetch(refs[3:9], here, refs[22])
+    ranked, sums, ops_ref, sem = refs[14:]
+    operators_here = pltpu.make_async_copy(ops_hbm, ops_ref, sem)
+    operators_here.start()
     boxes = strength_ref.shape[0]
     column = count_columns(cnt_ref, boxes)
     row = jnp.concatenate([cnt_ref[i : i + 1, :] for i in range(boxes // LANES)], axis=1)
@@ -138,7 +144,6 @@
     to_rank = jnp.where(rank_row == down.astype(F32), 1.0, 0.0).astype(BF16)
     from_rank = jnp.where(rank_column == across.astype(F32), 1.0, 0.0).astype(BF16)
 
-    copies[0].wait()
     lists = jnp.concatenate(
         [
             nb_ref[...].astype(F32),
@@ -153,7 +158,6 @@
     ends = jnp.sum(within, axis=0, keepdims=True).astype(jnp.int32) >> log2(TEAM)
     plan_ref[...] = jnp.where(iota((8, boxes), 0) == nb_ref.shape[0] + 2, ends, plan)
 
-    copies[1].wait()
     norm = jnp.zeros((boxes, LANES), F32)
     parts = []
     for c in range(3):
@@ -183,9 +187,7 @@
         return carry
 
     lax.fori_loop(0, boxes // 8, build, 0, unroll=4)
-    for copy in copies[2:5]:
-        copy.wait()
-    slot_stage(m_ref, src_ref, pat_ref, tgt_ref, ops_ref, sent_ref, sums, copies[5])
+    slot_stage(m_ref, src_ref, pat_ref, tgt_ref, ops_ref, sent_ref, sums, operators_here)
 
 
 def near_kernel(plan_ref, rows_ref, coords_ref, left_ref, out_ref, right, *, start, stop):
@@ -289,9 +291,6 @@
                 sums[i * per : (i + 1) * per, p * width : (p + 1) * width] = s[
                     p * per : (p + 1) * per
                 ]
-    for copy in copies:
-        copy.wait()
-    near_local = dot(sums[...], ops_ref[...])
     hits = []
     values = []
     for pay in pay_refs:
@@ -300,13 +299,16 @@
         box = iota((boxes, depth), 0).astype(F32)
         hits.append(jnp.where(box == target, 1.0, 0.0).astype(BF16))
         values.append(pay[0:depth, :])
-    local = near_local + dot(jnp.concatenate(hits, axis=1), jnp.concatenate(values, axis=0))
-    far = dot(local.astype(BF16), eval_ref[...])
+    remote_local = dot(jnp.concatenate(hits, axis=1), jnp.concatenate(values, axis=0))
     near = near_refs[0][...]
     for ref in near_refs[1:]:
         near = near + ref[...]
+    live = iota((boxes, LANES), 1) < count_columns(cnt_ref, boxes)
+    for copy in copies:
+        copy.wait()
+    local = dot(sums[...], ops_ref[...]) + remote_local
+    far = dot(local.astype(BF16), eval_ref[...])
     total = near * (1.0 / (4.0 * math.pi)) + far
-    live = iota((boxes, LANES), 1) < count_columns(cnt_ref, boxes)
     out_ref[...] = jnp.where(live, total, 0.0)
 
 
@@ -346,23 +348,31 @@
     patterns = translations.shape[0]
     operators = translations.reshape(patterns * width, width)
     counts = panel_counts.reshape(boxes // LANES, LANES)
-    strength, counts, multipole = pl.pallas_call(
-        front_kernel,
+    handed = (
+        near_boxes.T,
+        positions,
+        remote_sources[0, 0].transpose(0, 2, 1),
+        remote_patterns[0, 0].transpose(0, 2, 1),
+        remote_targets[0, 0],
+    )
+    strength, counts, multipole, *handed = pl.pallas_call(
+        functools.partial(front_kernel, extra=len(handed)),
         out_shape=(
             jax.ShapeDtypeStruct((boxes, panels), F32),
             jax.ShapeDtypeStruct(counts.shape, jnp.int32),
             jax.ShapeDtypeStruct((boxes, width), BF16),
+            *[jax.ShapeDtypeStruct(v.shape, v.dtype) for v in handed],
         ),
-        in_specs=[HBM] * 3,
-        out_specs=(VMEM,) * 3,
+        in_specs=[HBM] * (3 + len(handed)),
+        out_specs=(VMEM,) * (3 + len(handed)),
         scratch_shapes=[pltpu.VMEM(v.shape, v.dtype) for v in (charges, counts, moment_map)]
-        + [pltpu.SemaphoreType.DMA((3,))],
+        + [pltpu.SemaphoreType.DMA((3 + len(handed),))],
         compiler_params=pltpu.CompilerParams(vmem_limit_bytes=8 * MIB),
         cost_estimate=pl.CostEstimate(
             flops=10_000_000, bytes_accessed=300_000, transcendentals=0
         ),
         name="front",
-    )(in_hbm(charges), in_hbm(counts), in_hbm(moment_map))
+    )(in_hbm(charges), in_hbm(counts), in_hbm(moment_map), *map(in_hbm, handed))
 
     me = lax.axis_index("cube")
     octant = lax.axis_index("oct")
@@ -376,15 +386,7 @@
     def after(value, *earlier):
         return lax.optimization_barrier((value, *earlier))[0]
 
-    slots, fanin = remote_sources.shape[3:]
-    fetched = (
-        near_boxes.T,
-        positions,
-        remote_sources[0, 0].transpose(0, 2, 1),
-        remote_patterns[0, 0].transpose(0, 2, 1),
-        remote_targets[0, 0],
-        operators,
-    )
+    slots = remote_sources.shape[3]
     plan, *tables, sent = pl.pallas_call(
         plan_kernel,
         out_shape=(
@@ -394,23 +396,23 @@
             jax.ShapeDtypeStruct((boxes // 8, panels, LANES), BF16),
             jax.ShapeDtypeStruct((n_oct, 2 * slots + 16, width), BF16),
         ),
-        in_specs=[VMEM] * 3 + [HBM] * len(fetched),
+        in_specs=[VMEM] * (3 + len(handed)) + [HBM],
         out_specs=(VMEM,) * 5,
         scratch_shapes=[
             pltpu.VMEM((boxes, 9 * LANES), F32),
             pltpu.VMEM((n_oct * slots, patterns * width), BF16),
-        ]
-        + [pltpu.VMEM(v.shape, v.dtype) for v in fetched]
-        + [pltpu.SemaphoreType.DMA((len(fetched),))],
+            pltpu.VMEM(operators.shape, BF16),
+            pltpu.SemaphoreType.DMA,
+        ],
         compiler_params=pltpu.CompilerParams(vmem_limit_bytes=16 * MIB),
         cost_estimate=pl.CostEstimate(
             flops=1_000_000_000, bytes_accessed=2_000_000, transcendentals=0
         ),
         name="plan",
-    )(counts, strength, multipole, *map(in_hbm, fetched))
+    )(counts, strength, multipole, *handed, in_hbm(operators))
 
     teams = boxes // TEAM
-    cut = teams * 5 // 8
+    cut = teams * 11 // 16
 
     def near_piece(start, stop, tables):
         return pl.pallas_call(
@@ -443,7 +445,7 @@
         return jnp.concatenate([mine, over_cube(mine, bit)], axis=0)
 
     oct_bits = [1 << i for i in range(log2(n_oct))]
-    cube_bits = [1 << i for i in range(1, log2(n_cube))]
+    cube_bits = [1 << i for i in range(log2(n_cube) - 1, 0, -1)]
     mine = cube_step(cube_bits[0], multipole)
     mine = after(mine, plan, sent)
     anchor = [mine]
@@ -470,7 +472,10 @@
 
     klist = group_sources.shape[1]
     group = n_cube * boxes
-    code = (group_sources ^ (me * boxes)) + group * group_patterns
+    away = group_sources ^ (me * boxes)
+    code = (away & (2 * boxes - 1)) + group * group_patterns
+    for i in range(1, log2(n_cube)):
+        code = code + (((away // boxes) >> i) & 1) * ((n_cube >> i) * boxes)
     return pl.pallas_call(
         functools.partial(far_kernel, blocks=n_cube, fanin=klist, pieces=PIECES),
         out_shape=jax.ShapeDtypeStruct((boxes, panels), F32),

time: 33.2 us -> 32.6 us (0.982)
  starting transfers between devices: 9.18 us -> 8.84 us
    pallas_call x1, Pallas kernels: 4.36 us -> 3.36 us  [body(): pl.pallas_call(plan_kernel, out_shape=(jax.ShapeDtypeStruct((8, boxes), j...]
    pallas_call x2, Pallas kernels: 13.5 us -> 13.9 us  [near_piece(): pl.pallas_call(functools.partial(near_kernel, start=start, stop=stop), ou...]
    ppermute x2, starting transfers between devices: 3.37 us -> 3.02 us  [over_oct(): return lax.ppermute(value, 'oct', [(i, i ^ k) for i in range(n_oct)])]
  transfers between devices with their start and end apart: 5 -> 5, of which waited for: 0 -> 0; matrix products, arithmetic and copies ran while one was open for 1% -> 1% of each run, Pallas kernels for 54% -> 53%
where the time goes in v10:
time: 32.6 us; the launch traced here: 32.3 us
  Pallas kernels  22.7 us (70%)
  starting transfers between devices  8.84 us (27%)
    pallas_call x2, Pallas kernels, near_piece(): pl.pallas_call(functools.partial(near_kernel, start=start, stop=stop), ou...  13.9 us
    ppermute x3, starting transfers between devices, over_cube(): return lax.ppermute(value, 'cube', [(i, i ^ k) for i in range(n_cube)])  5.82 us
    pallas_call x1, Pallas kernels, body(): pl.pallas_call(functools.partial(far_kernel, blocks=n_cube, fanin=klist,...  4.22 us
    pallas_call x1, Pallas kernels, body(): pl.pallas_call(plan_kernel, out_shape=(jax.ShapeDtypeStruct((8, boxes), j...  3.36 us
    ppermute x2, starting transfers between devices, over_oct(): return lax.ppermute(value, 'oct', [(i, i ^ k) for i in range(n_oct)])  3.02 us
    pallas_call x1, Pallas kernels, body(): pl.pallas_call(functools.partial(front_kernel, extra=len(handed)), out_sh...  1.29 us
  transfers between devices with their start and end apart: 5, of which 0 were waited for; matrix products, arithmetic and copies ran while one was open for 1% of the time, Pallas kernels for 53%

profile of v10, /device:TPU:0, one launch (start us, length us, event | category | flops | bytes accessed | tf_op | source)
XLA Modules:
  0.0 32.3 jit_solution(16888592552759508656)
XLA Ops:
  0.0 1.3 %front.1 = (f32[256,128]{1,0:T(8,128)S(1)}, s32[2,128]{1,0:T(2,128)S(1)}, bf16[256,128]{1,0:T(8,128)(2,1)S(1)}, s32[4,256]{1,0:T(4,128)S(1)}, f32[3,256,128]{2,1...) custom-call(bf16[256,128]{1,0:T(8,128)(2,1)} %refs_0_.1, ...), custom_call_target="tpu_custom_call" | custom-call | flops 10000000 | bytes 300000 | tf_op jit(solution)/shard_map/front/pallas_call | solution.py:358
  1.3 4.1 %collective-permute-start = (bf16[256,128]{1,0:T(8,128)(2,1)S(1)}, bf16[256,128]{1,0:T(8,128)(2,1)S(1)}, u32[]{:S(2)}, u32[]{:S(2)}) collective-permute-start(bf16[256,128]{1,0:T(8,128)(2,1)S(1)} %get-tuple-element.33.refs_2_), channel_id=1, source_target_pairs={{0,4},{1,5},{2,6},{3,7},{4,0},{5,1},{6,2},{7,3},{8,12},{9,13},{10,... | collective-permute-start | bytes 196616 | tf_op jit(solution)/shard_map/ppermute | solution.py:381
  5.4 3.4 %plan.1 = (s32[8,256]{1,0:T(8,128)S(1)}, f32[2,256,128]{2,1,0:T(8,128)S(1)}, f32[6,256,128]{2,1,0:T(8,128)S(1)}, bf16[32,128,128]{2,1,0:T(8,128)(2,1)S(1)}, bf16[4,144,128]{2,1,0:T(8,128)(2,1)S(1)}) custom-call(s32[2,128]{1,0:T(2,128)S(1)} %get-tuple-element.32.refs_0_.refs_1_, f32[256,128]{1,0:T(8,128)S(1)} %get-tuple-element.34.refs_1_, ...), custom_call_target="tpu_custom_call" | custom-call | flops 1000000000 | bytes 2000000 | tf_op jit(solution)/shard_map/plan/pallas_call | solution.py:390
  8.8 1.6 %collective-permute-start.3 = (bf16[288,128]{1,0:T(8,128)(2,1)S(1)}, bf16[288,128]{1,0:T(8,128)(2,1)S(1)}, u32[]{:S(2)}, u32[]{:S(2)}) collective-permute-start(bf16[288,128]{1,0:T(8,128)(2,1)S(1)} %pad_maximum_fusion.2), channel_id=1, source_target_pairs={{0,8},{8,0},{16,24},{24,16},{1,9},{9,1},{17,25},{25,17},{2,10},{10... | collective-permute-start | bytes 221192 | tf_op jit(solution)/shard_map/ppermute | solution.py:384
  10.4 0.0 collective-permute-done
  10.4 1.6 %collective-permute-start.1 = (bf16[512,128]{1,0:T(8,128)(2,1)S(1)}, bf16[512,128]{1,0:T(8,128)(2,1)S(1)}, u32[]{:S(2)}, u32[]{:S(2)}) collective-permute-start(bf16[512,128]{1,0:T(8,128)(2,1)S(1)} %pad_maximum_fusion.1), channel_id=1, source_target_pairs={{0,2},{1,3},{2,0},{3,1},{4,6},{5,7},{6,4},{7,5},{8,10},{9,11},{10,... | collective-permute-start | bytes 393224 | tf_op jit(solution)/shard_map/ppermute | solution.py:381
  12.0 8.2 %near.2.refs_6_ = f32[256,128]{1,0:T(8,128)S(1)} custom-call(s32[8,256]{1,0:T(8,128)S(1)} %get-tuple-element.40.plan_ref, f32[2,256,128]{2,1,0:T(8,128)S(1)} %get-tuple-element.52.rows_ref, f32[6,256,128]{2,1,0:T(8,128)S(1)} %get-tuple-element.53.coords_ref, bf16[32,128,128]{2,1,0:T(8,128)(2,1)S(1)} %get-tuple-element.54.left_ref), custom_call_target="tpu_custom_call" | custom-call | flops 200000000 | bytes 1000000 | tf_op jit(solution)/shard_map/near/pallas_call | solution.py:418
  20.2 0.0 collective-permute-done.3
  20.2 0.0 collective-permute-done.1
  20.3 0.0 copy-start
  20.3 0.0 copy-start.1
  20.3 0.1 collective-permute-start.2
  20.4 1.5 %collective-permute-start.4 = (bf16[288,128]{1,0:T(8,128)(2,1)S(1)}, bf16[288,128]{1,0:T(8,128)(2,1)S(1)}, u32[]{:S(2)}, u32[]{:S(2)}) collective-permute-start(bf16[288,128]{1,0:T(8,128)(2,1)S(1)} %constant_dynamic-update-slice_fusion), channel_id=1, source_target_pairs={{0,16},{8,24},{16,0},{24,8},{1,17},{9,25},{17,1},{25,9},{2,18},{10... | collective-permute-start | bytes 221192 | tf_op jit(solution)/shard_map/ppermute | solution.py:384
  21.9 0.0 copy-done
  21.9 0.0 copy-done.1
  21.9 0.1 copy.14
  22.0 0.1 reshape.9.refs_0_
  22.1 5.7 %near.3.refs_7_ = f32[256,128]{1,0:T(8,128)S(1)} custom-call(s32[8,256]{1,0:T(8,128)S(1)} %get-tuple-element.40.plan_ref, f32[2,256,128]{2,1,0:T(8,128)S(1)} %get-tuple-element.52.rows_ref, f32[6,256,128]{2,1,0:T(8,128)S(1)} %get-tuple-element.53.coords_ref, bf16[32,128,128]{2,1,0:T(8,128)(2,1)S(1)} %get-tuple-element.54.left_ref), custom_call_target="tpu_custom_call" | custom-call | flops 200000000 | bytes 1000000 | tf_op jit(solution)/shard_map/near/pallas_call | solution.py:418
  27.9 0.0 collective-permute-done.4
  27.9 0.0 collective-permute-done.2.refs_5_
  27.9 4.2 %far.1 = f32[256,128]{1,0:T(8,128)} custom-call(s32[16,128]{1,0:T(8,128)S(1)} %reshape.9.refs_0_, s32[2,128]{1,0:T(2,128)S(1)} %get-tuple-element.32.refs_0_.refs_1_, bf16[2048,128]{1,0:T(8,128)(2,1)} %bitcast.24, bf16[128,128]{1,0:T(8,128)(2,1)} %refs_3_.1, bf16[1024,128]{1,0:T(8,128)(2,1)S(1)} %pad_maximum_fusion.refs_4_, ...), custom_call_target="tpu_custom_call" | custom-call | flops 3000000000 | bytes 2000000 | tf_op jit(solution)/shard_map/far/pallas_call | solution.py:479
  (9 shorter events, 0.1 us)
Async XLA Ops:
  1.3 9.1 %collective-permute-start = (bf16[256,128]{1,0:T(8,128)(2,1)S(1)}, bf16[256,128]{1,0:T(8,128)(2,1)S(1)}, u32[]{:S(2)}, u32[]{:S(2)}) collective-permute-start(bf16[256,128]{1,0:T(8,128)(2,1)S(1)} %get-tuple-element.33.refs_2_), channel_id=1, source_target_pairs={{0,4},{1,5},{2,6},{3,7},{4,0},{5,1},{6,2},{7,3},{8,12},{9,13},{10,... | collective-permute-start | bytes 196616 | tf_op jit(solution)/shard_map/ppermute | solution.py:381
  8.8 11.4 %collective-permute-start.3 = (bf16[288,128]{1,0:T(8,128)(2,1)S(1)}, bf16[288,128]{1,0:T(8,128)(2,1)S(1)}, u32[]{:S(2)}, u32[]{:S(2)}) collective-permute-start(bf16[288,128]{1,0:T(8,128)(2,1)S(1)} %pad_maximum_fusion.2), channel_id=1, source_target_pairs={{0,8},{8,0},{16,24},{24,16},{1,9},{9,1},{17,25},{25,17},{2,10},{10... | collective-permute-start | bytes 221192 | tf_op jit(solution)/shard_map/ppermute | solution.py:384
  10.4 9.9 %collective-permute-start.1 = (bf16[512,128]{1,0:T(8,128)(2,1)S(1)}, bf16[512,128]{1,0:T(8,128)(2,1)S(1)}, u32[]{:S(2)}, u32[]{:S(2)}) collective-permute-start(bf16[512,128]{1,0:T(8,128)(2,1)S(1)} %pad_maximum_fusion.1), channel_id=1, source_target_pairs={{0,2},{1,3},{2,0},{3,1},{4,6},{5,7},{6,4},{7,5},{8,10},{9,11},{10,... | collective-permute-start | bytes 393224 | tf_op jit(solution)/shard_map/ppermute | solution.py:381
  20.3 1.6 %copy-start = (s32[256,8]{0,1:T(8,128)S(1)}, s32[256,8]{0,1:T(8,128)}, u32[]{:S(2)}) copy-start(s32[256,8]{0,1:T(8,128)} %param.20) | copy-start | bytes 24580
  20.3 1.6 %copy-start.1 = (s32[256,8]{0,1:T(8,128)S(1)}, s32[256,8]{0,1:T(8,128)}, u32[]{:S(2)}) copy-start(s32[256,8]{0,1:T(8,128)} %param.19) | copy-start | bytes 24580
  20.3 7.6 %collective-permute-start.2 = (bf16[1024,128]{1,0:T(8,128)(2,1)S(1)}, bf16[1024,128]{1,0:T(8,128)(2,1)S(1)}, u32[]{:S(2)}, u32[]{:S(2)}) collective-permute-start(bf16[1024,128]{1,0:T(8,128)(2,1)S(1)} %pad_maximum_fusion.refs_4_), channel_id=1, source_target_pairs={{0,1},{1,0},{2,3},{3,2},{4,5},{5,4},{6,7},{7,6},{8,9},{9,8},{10,11... | collective-permute-start | bytes 786440 | tf_op jit(solution)/shard_map/ppermute | solution.py:381
  20.4 7.5 %collective-permute-start.4 = (bf16[288,128]{1,0:T(8,128)(2,1)S(1)}, bf16[288,128]{1,0:T(8,128)(2,1)S(1)}, u32[]{:S(2)}, u32[]{:S(2)}) collective-permute-start(bf16[288,128]{1,0:T(8,128)(2,1)S(1)} %constant_dynamic-update-slice_fusion), channel_id=1, source_target_pairs={{0,16},{8,24},{16,0},{24,8},{1,17},{9,25},{17,1},{25,9},{2,18},{10... | collective-permute-start | bytes 221192 | tf_op jit(solution)/shard_map/ppermute | solution.py:384

commit v11 on v10

--- a/solution.py
+++ b/solution.py
@@ -248,11 +248,10 @@
 
 
 def far_kernel(*refs, blocks, fanin, pieces):
-    code_ref, cnt_ref, ops_hbm, eval_hbm, mine_ref, other_ref = refs[:6]
+    code_ref, cnt_ref, ops_ref, eval_ref, mine_ref, other_ref = refs[:6]
     near_refs = refs[6 : 6 + pieces]
-    pay_refs = refs[6 + pieces : -5]
-    out_ref, sums, ops_ref, eval_ref, sems = refs[-5:]
-    copies = fetch((ops_hbm, eval_hbm), (ops_ref, eval_ref), sems)
+    pay_refs = refs[6 + pieces : -2]
+    out_ref, sums = refs[-2:]
     width = mine_ref.shape[1]
     boxes = mine_ref.shape[0] // (blocks // 2)
     patterns = ops_ref.shape[0] // width
@@ -304,8 +303,6 @@
     for ref in near_refs[1:]:
         near = near + ref[...]
     live = iota((boxes, LANES), 1) < count_columns(cnt_ref, boxes)
-    for copy in copies:
-        copy.wait()
     local = dot(sums[...], ops_ref[...]) + remote_local
     far = dot(local.astype(BF16), eval_ref[...])
     total = near * (1.0 / (4.0 * math.pi)) + far
@@ -354,8 +351,9 @@
         remote_sources[0, 0].transpose(0, 2, 1),
         remote_patterns[0, 0].transpose(0, 2, 1),
         remote_targets[0, 0],
+        evaluation,
     )
-    strength, counts, multipole, *handed = pl.pallas_call(
+    strength, counts, multipole, *handed, evaluation = pl.pallas_call(
         functools.partial(front_kernel, extra=len(handed)),
         out_shape=(
             jax.ShapeDtypeStruct((boxes, panels), F32),
@@ -445,7 +443,7 @@
         return jnp.concatenate([mine, over_cube(mine, bit)], axis=0)
 
     oct_bits = [1 << i for i in range(log2(n_oct))]
-    cube_bits = [1 << i for i in range(log2(n_cube) - 1, 0, -1)]
+    cube_bits = [1 << i for i in range(1, log2(n_cube))]
     mine = cube_step(cube_bits[0], multipole)
     mine = after(mine, plan, sent)
     anchor = [mine]
@@ -472,21 +470,13 @@
 
     klist = group_sources.shape[1]
     group = n_cube * boxes
-    away = group_sources ^ (me * boxes)
-    code = (away & (2 * boxes - 1)) + group * group_patterns
-    for i in range(1, log2(n_cube)):
-        code = code + (((away // boxes) >> i) & 1) * ((n_cube >> i) * boxes)
+    code = (group_sources ^ (me * boxes)) + group * group_patterns
     return pl.pallas_call(
         functools.partial(far_kernel, blocks=n_cube, fanin=klist, pieces=PIECES),
         out_shape=jax.ShapeDtypeStruct((boxes, panels), F32),
-        in_specs=[VMEM] * 2 + [HBM] * 2 + [VMEM] * (2 + PIECES + n_oct),
+        in_specs=[VMEM] * (6 + PIECES + n_oct),
         out_specs=VMEM,
-        scratch_shapes=[
-            pltpu.VMEM((boxes, patterns * width), BF16),
-            pltpu.VMEM(operators.shape, BF16),
-            pltpu.VMEM(evaluation.shape, BF16),
-            pltpu.SemaphoreType.DMA((2,)),
-        ],
+        scratch_shapes=[pltpu.VMEM((boxes, patterns * width), BF16)],
         compiler_params=pltpu.CompilerParams(vmem_limit_bytes=24 * MIB),
         cost_estimate=pl.CostEstimate(
             flops=3_000_000_000, bytes_accessed=2_000_000, transcendentals=0
@@ -495,8 +485,8 @@
     )(
         code.reshape(-1, LANES),
         counts,
-        in_hbm(operators),
-        in_hbm(evaluation),
+        operators,
+        evaluation,
         mine,
         other,
         *near,

time: 32.6 us -> 31.2 us (0.957)
  Pallas kernels: 22.7 us -> 21.7 us
    pallas_call x1, Pallas kernels: 4.22 us -> 3.19 us  [body(): pl.pallas_call(functools.partial(far_kernel, blocks=n_cube, fanin=klist,...]
  transfers between devices with their start and end apart: 5 -> 5, of which waited for: 0 -> 0; matrix products, arithmetic and copies ran while one was open for 1% -> 1% of each run, Pallas kernels for 53% -> 55%
where the time goes in v11:
time: 31.2 us; the launch traced here: 31.1 us
  Pallas kernels  21.7 us (70%)
  starting transfers between devices  8.8 us (28%)
    pallas_call x2, Pallas kernels, near_piece(): pl.pallas_call(functools.partial(near_kernel, start=start, stop=stop), ou...  13.9 us
    ppermute x3, starting transfers between devices, over_cube(): return lax.ppermute(value, 'cube', [(i, i ^ k) for i in range(n_cube)])  5.82 us
    pallas_call x1, Pallas kernels, body(): pl.pallas_call(plan_kernel, out_shape=(jax.ShapeDtypeStruct((8, boxes), j...  3.36 us
    pallas_call x1, Pallas kernels, body(): pl.pallas_call(functools.partial(far_kernel, blocks=n_cube, fanin=klist,...  3.19 us
    ppermute x2, starting transfers between devices, over_oct(): return lax.ppermute(value, 'oct', [(i, i ^ k) for i in range(n_oct)])  2.98 us
    pallas_call x1, Pallas kernels, body(): pl.pallas_call(functools.partial(front_kernel, extra=len(handed)), out_sh...  1.3 us
  transfers between devices with their start and end apart: 5, of which 0 were waited for; matrix products, arithmetic and copies ran while one was open for 1% of the time, Pallas kernels for 55%

profile of v11, /device:TPU:0, one launch (start us, length us, event | category | flops | bytes accessed | tf_op | source)
XLA Modules:
  0.0 31.1 jit_solution(4661186808021449194)
XLA Ops:
  0.0 1.3 %front.1 = (f32[256,128]{1,0:T(8,128)S(1)}, s32[2,128]{1,0:T(2,128)S(1)}, bf16[256,128]{1,0:T(8,128)(2,1)S(1)}, s32[4,256]{1,0:T(4,128)S(1)}, f32[3,256,128]{2,1...) custom-call(bf16[256,128]{1,0:T(8,128)(2,1)} %refs_0_.1, ...), custom_call_target="tpu_custom_call" | custom-call | flops 10000000 | bytes 300000 | tf_op jit(solution)/shard_map/front/pallas_call | solution.py:356
  1.3 3.1 %collective-permute-start = (bf16[256,128]{1,0:T(8,128)(2,1)S(1)}, bf16[256,128]{1,0:T(8,128)(2,1)S(1)}, u32[]{:S(2)}, u32[]{:S(2)}) collective-permute-start(bf16[256,128]{1,0:T(8,128)(2,1)S(1)} %get-tuple-element.35.refs_2_), channel_id=1, source_target_pairs={{0,2},{1,3},{2,0},{3,1},{4,6},{5,7},{6,4},{7,5},{8,10},{9,11},{10,... | collective-permute-start | bytes 196616 | tf_op jit(solution)/shard_map/ppermute | solution.py:379
  4.4 3.4 %plan.1 = (s32[8,256]{1,0:T(8,128)S(1)}, f32[2,256,128]{2,1,0:T(8,128)S(1)}, f32[6,256,128]{2,1,0:T(8,128)S(1)}, bf16[32,128,128]{2,1,0:T(8,128)(2,1)S(1)}, bf16[4,144,128]{2,1,0:T(8,128)(2,1)S(1)}) custom-call(s32[2,128]{1,0:T(2,128)S(1)} %get-tuple-element.33.refs_0_.refs_1_, f32[256,128]{1,0:T(8,128)S(1)} %get-tuple-element.36.refs_1_, ...), custom_call_target="tpu_custom_call" | custom-call | flops 1000000000 | bytes 2000000 | tf_op jit(solution)/shard_map/plan/pallas_call | solution.py:388
  7.8 1.6 %collective-permute-start.3 = (bf16[288,128]{1,0:T(8,128)(2,1)S(1)}, bf16[288,128]{1,0:T(8,128)(2,1)S(1)}, u32[]{:S(2)}, u32[]{:S(2)}) collective-permute-start(bf16[288,128]{1,0:T(8,128)(2,1)S(1)} %pad_maximum_fusion.2), channel_id=1, source_target_pairs={{0,8},{8,0},{16,24},{24,16},{1,9},{9,1},{17,25},{25,17},{2,10},{10... | collective-permute-start | bytes 221192 | tf_op jit(solution)/shard_map/ppermute | solution.py:382
  9.4 0.0 collective-permute-done
  9.4 2.7 %collective-permute-start.1 = (bf16[512,128]{1,0:T(8,128)(2,1)S(1)}, bf16[512,128]{1,0:T(8,128)(2,1)S(1)}, u32[]{:S(2)}, u32[]{:S(2)}) collective-permute-start(bf16[512,128]{1,0:T(8,128)(2,1)S(1)} %pad_maximum_fusion.1), channel_id=1, source_target_pairs={{0,4},{1,5},{2,6},{3,7},{4,0},{5,1},{6,2},{7,3},{8,12},{9,13},{10,... | collective-permute-start | bytes 393224 | tf_op jit(solution)/shard_map/ppermute | solution.py:379
  12.0 8.2 %near.2.refs_6_ = f32[256,128]{1,0:T(8,128)S(1)} custom-call(s32[8,256]{1,0:T(8,128)S(1)} %get-tuple-element.42.plan_ref, f32[2,256,128]{2,1,0:T(8,128)S(1)} %get-tuple-element.54.rows_ref, f32[6,256,128]{2,1,0:T(8,128)S(1)} %get-tuple-element.55.coords_ref, bf16[32,128,128]{2,1,0:T(8,128)(2,1)S(1)} %get-tuple-element.56.left_ref), custom_call_target="tpu_custom_call" | custom-call | flops 200000000 | bytes 1000000 | tf_op jit(solution)/shard_map/near/pallas_call | solution.py:416
  20.3 0.0 collective-permute-done.3
  20.3 0.0 collective-permute-done.1
  20.4 0.0 copy-start.1
  20.4 0.0 copy-start.2
  20.4 0.1 collective-permute-start.2
  20.5 1.4 %collective-permute-start.4 = (bf16[288,128]{1,0:T(8,128)(2,1)S(1)}, bf16[288,128]{1,0:T(8,128)(2,1)S(1)}, u32[]{:S(2)}, u32[]{:S(2)}) collective-permute-start(bf16[288,128]{1,0:T(8,128)(2,1)S(1)} %constant_dynamic-update-slice_fusion), channel_id=1, source_target_pairs={{0,16},{8,24},{16,0},{24,8},{1,17},{9,25},{17,1},{25,9},{2,18},{10... | collective-permute-start | bytes 221192 | tf_op jit(solution)/shard_map/ppermute | solution.py:382
  21.9 0.0 copy-done.1
  21.9 0.0 copy-done.2
  21.9 0.1 copy.14
  22.1 0.1 reshape.9.refs_0_
  22.2 0.0 copy-start
  22.2 5.7 %near.3.refs_7_ = f32[256,128]{1,0:T(8,128)S(1)} custom-call(s32[8,256]{1,0:T(8,128)S(1)} %get-tuple-element.42.plan_ref, f32[2,256,128]{2,1,0:T(8,128)S(1)} %get-tuple-element.54.rows_ref, f32[6,256,128]{2,1,0:T(8,128)S(1)} %get-tuple-element.55.coords_ref, bf16[32,128,128]{2,1,0:T(8,128)(2,1)S(1)} %get-tuple-element.56.left_ref), custom_call_target="tpu_custom_call" | custom-call | flops 200000000 | bytes 1000000 | tf_op jit(solution)/shard_map/near/pallas_call | solution.py:416
  27.8 0.0 collective-permute-done.4
  27.8 0.0 collective-permute-done.2.refs_5_
  27.9 0.0 copy-done
  27.9 3.2 %far.1 = f32[256,128]{1,0:T(8,128)} custom-call(s32[16,128]{1,0:T(8,128)S(1)} %reshape.9.refs_0_, s32[2,128]{1,0:T(2,128)S(1)} %get-tuple-element.33.refs_0_.refs_1_, bf16[2048,128]{1,0:T(8,128)(2,1)S(1)} %bitcast.19, bf16[128,128]{1,0:T(8,128)(2,1)S(1)} %get-tuple-element.34.refs_3_, bf16[1024,128]{1,0:T(8,128)(2,1)S(1)} %pad_maximum_fusion.refs_4_, ...), custom_call_target="tpu_custom_call" | custom-call | flops 3000000000 | bytes 2000000 | tf_op jit(solution)/shard_map/far/pallas_call | solution.py:474
  (9 shorter events, 0.1 us)
Async XLA Ops:
  1.3 8.1 %collective-permute-start = (bf16[256,128]{1,0:T(8,128)(2,1)S(1)}, bf16[256,128]{1,0:T(8,128)(2,1)S(1)}, u32[]{:S(2)}, u32[]{:S(2)}) collective-permute-start(bf16[256,128]{1,0:T(8,128)(2,1)S(1)} %get-tuple-element.35.refs_2_), channel_id=1, source_target_pairs={{0,2},{1,3},{2,0},{3,1},{4,6},{5,7},{6,4},{7,5},{8,10},{9,11},{10,... | collective-permute-start | bytes 196616 | tf_op jit(solution)/shard_map/ppermute | solution.py:379
  7.8 12.5 %collective-permute-start.3 = (bf16[288,128]{1,0:T(8,128)(2,1)S(1)}, bf16[288,128]{1,0:T(8,128)(2,1)S(1)}, u32[]{:S(2)}, u32[]{:S(2)}) collective-permute-start(bf16[288,128]{1,0:T(8,128)(2,1)S(1)} %pad_maximum_fusion.2), channel_id=1, source_target_pairs={{0,8},{8,0},{16,24},{24,16},{1,9},{9,1},{17,25},{25,17},{2,10},{10... | collective-permute-start | bytes 221192 | tf_op jit(solution)/shard_map/ppermute | solution.py:382
  9.4 10.9 %collective-permute-start.1 = (bf16[512,128]{1,0:T(8,128)(2,1)S(1)}, bf16[512,128]{1,0:T(8,128)(2,1)S(1)}, u32[]{:S(2)}, u32[]{:S(2)}) collective-permute-start(bf16[512,128]{1,0:T(8,128)(2,1)S(1)} %pad_maximum_fusion.1), channel_id=1, source_target_pairs={{0,4},{1,5},{2,6},{3,7},{4,0},{5,1},{6,2},{7,3},{8,12},{9,13},{10,... | collective-permute-start | bytes 393224 | tf_op jit(solution)/shard_map/ppermute | solution.py:379
  20.4 1.6 %copy-start.1 = (s32[256,8]{0,1:T(8,128)S(1)}, s32[256,8]{0,1:T(8,128)}, u32[]{:S(2)}) copy-start(s32[256,8]{0,1:T(8,128)} %param.20) | copy-start | bytes 24580
  20.4 1.5 %copy-start.2 = (s32[256,8]{0,1:T(8,128)S(1)}, s32[256,8]{0,1:T(8,128)}, u32[]{:S(2)}) copy-start(s32[256,8]{0,1:T(8,128)} %param.19) | copy-start | bytes 24580
  20.4 7.5 %collective-permute-start.2 = (bf16[1024,128]{1,0:T(8,128)(2,1)S(1)}, bf16[1024,128]{1,0:T(8,128)(2,1)S(1)}, u32[]{:S(2)}, u32[]{:S(2)}) collective-permute-start(bf16[1024,128]{1,0:T(8,128)(2,1)S(1)} %pad_maximum_fusion.refs_4_), channel_id=1, source_target_pairs={{0,1},{1,0},{2,3},{3,2},{4,5},{5,4},{6,7},{7,6},{8,9},{9,8},{10,11... | collective-permute-start | bytes 786440 | tf_op jit(solution)/shard_map/ppermute | solution.py:379
  20.5 7.4 %collective-permute-start.4 = (bf16[288,128]{1,0:T(8,128)(2,1)S(1)}, bf16[288,128]{1,0:T(8,128)(2,1)S(1)}, u32[]{:S(2)}, u32[]{:S(2)}) collective-permute-start(bf16[288,128]{1,0:T(8,128)(2,1)S(1)} %constant_dynamic-update-slice_fusion), channel_id=1, source_target_pairs={{0,16},{8,24},{16,0},{24,8},{1,17},{9,25},{17,1},{25,9},{2,18},{10... | collective-permute-start | bytes 221192 | tf_op jit(solution)/shard_map/ppermute | solution.py:382
  22.2 5.7 %copy-start = (bf16[16,128,128]{2,1,0:T(8,128)(2,1)S(1)}, bf16[16,128,128]{2,1,0:T(8,128)(2,1)}, u32[]{:S(2)}) copy-start(bf16[16,128,128]{2,1,0:T(8,128)(2,1)} %param.16) | copy-start | bytes 1572868

commit v12 on v11

--- a/solution.py
+++ b/solution.py
@@ -232,7 +232,8 @@
                     for i in range(2):
                         shift = rows_ref[0, pl.ds(pair[i], 1), :]
                         q = rows_ref[1, pl.ds(pair[i], 1), :]
-                        term = lax.rsqrt(dist[:, i * LANES : (i + 1) * LANES] + shift) * q
+                        square = dist[:, i * LANES : (i + 1) * LANES] + shift
+                        term = lax.rsqrt(square.astype(BF16)).astype(F32) * q
                         acc = term if acc is None else acc + term
                 total = jnp.sum(acc, axis=1, keepdims=True)
                 out_ref[pl.ds(plan_ref[knear + 1, place], 1), :] = jnp.sum(

time: 31.2 us -> 32.9 us (1.054)
  Pallas kernels: 21.7 us -> 23 us
  starting transfers between devices: 8.8 us -> 9.37 us
    pallas_call x2, Pallas kernels: 13.9 us -> 15.2 us  [near_piece(): pl.pallas_call(functools.partial(near_kernel, start=start, stop=stop), ou...]
    ppermute x2, starting transfers between devices: 2.98 us -> 3.55 us  [over_oct(): return lax.ppermute(value, 'oct', [(i, i ^ k) for i in range(n_oct)])]
  transfers between devices with their start and end apart: 5 -> 5, of which waited for: 0 -> 0; matrix products, arithmetic and copies ran while one was open for 1% -> 1% of each run, Pallas kernels for 55% -> 56%
where the time goes in v12:
time: 32.9 us
  Pallas kernels  23 us (70%)
  starting transfers between devices  9.37 us (28%)
    pallas_call x2, Pallas kernels, near_piece(): pl.pallas_call(functools.partial(near_kernel, start=start, stop=stop), ou...  15.2 us
    ppermute x3, starting transfers between devices, over_cube(): return lax.ppermute(value, 'cube', [(i, i ^ k) for i in range(n_cube)])  5.82 us
    ppermute x2, starting transfers between devices, over_oct(): return lax.ppermute(value, 'oct', [(i, i ^ k) for i in range(n_oct)])  3.55 us
    pallas_call x1, Pallas kernels, body(): pl.pallas_call(plan_kernel, out_shape=(jax.ShapeDtypeStruct((8, boxes), j...  3.36 us
    pallas_call x1, Pallas kernels, body(): pl.pallas_call(functools.partial(far_kernel, blocks=n_cube, fanin=klist,...  3.18 us
    pallas_call x1, Pallas kernels, body(): pl.pallas_call(functools.partial(front_kernel, extra=len(handed)), out_sh...  1.3 us
  transfers between devices with their start and end apart: 5, of which 0 were waited for; matrix products, arithmetic and copies ran while one was open for 1% of the time, Pallas kernels for 56%

profile of v12, /device:TPU:0, one launch (start us, length us, event | category | flops | bytes accessed | tf_op | source)
XLA Modules:
  0.0 32.9 jit_solution(6726543647298797331)
XLA Ops:
  0.0 1.3 %front.1 = (f32[256,128]{1,0:T(8,128)S(1)}, s32[2,128]{1,0:T(2,128)S(1)}, bf16[256,128]{1,0:T(8,128)(2,1)S(1)}, s32[4,256]{1,0:T(4,128)S(1)}, f32[3,256,128]{2,1...) custom-call(bf16[256,128]{1,0:T(8,128)(2,1)} %refs_0_.1, ...), custom_call_target="tpu_custom_call" | custom-call | flops 10000000 | bytes 300000 | tf_op jit(solution)/shard_map/front/pallas_call | solution.py:357
  1.3 3.1 %collective-permute-start = (bf16[256,128]{1,0:T(8,128)(2,1)S(1)}, bf16[256,128]{1,0:T(8,128)(2,1)S(1)}, u32[]{:S(2)}, u32[]{:S(2)}) collective-permute-start(bf16[256,128]{1,0:T(8,128)(2,1)S(1)} %get-tuple-element.35.refs_2_), channel_id=1, source_target_pairs={{0,2},{1,3},{2,0},{3,1},{4,6},{5,7},{6,4},{7,5},{8,10},{9,11},{10,... | collective-permute-start | bytes 196616 | tf_op jit(solution)/shard_map/ppermute | solution.py:380
  4.4 3.4 %plan.1 = (s32[8,256]{1,0:T(8,128)S(1)}, f32[2,256,128]{2,1,0:T(8,128)S(1)}, f32[6,256,128]{2,1,0:T(8,128)S(1)}, bf16[32,128,128]{2,1,0:T(8,128)(2,1)S(1)}, bf16[4,144,128]{2,1,0:T(8,128)(2,1)S(1)}) custom-call(s32[2,128]{1,0:T(2,128)S(1)} %get-tuple-element.33.refs_0_.refs_1_, f32[256,128]{1,0:T(8,128)S(1)} %get-tuple-element.36.refs_1_, ...), custom_call_target="tpu_custom_call" | custom-call | flops 1000000000 | bytes 2000000 | tf_op jit(solution)/shard_map/plan/pallas_call | solution.py:389
  7.8 1.6 %collective-permute-start.3 = (bf16[288,128]{1,0:T(8,128)(2,1)S(1)}, bf16[288,128]{1,0:T(8,128)(2,1)S(1)}, u32[]{:S(2)}, u32[]{:S(2)}) collective-permute-start(bf16[288,128]{1,0:T(8,128)(2,1)S(1)} %pad_maximum_fusion.2), channel_id=1, source_target_pairs={{0,8},{8,0},{16,24},{24,16},{1,9},{9,1},{17,25},{25,17},{2,10},{10... | collective-permute-start | bytes 221192 | tf_op jit(solution)/shard_map/ppermute | solution.py:383
  9.4 0.0 collective-permute-done
  9.4 2.7 %collective-permute-start.1 = (bf16[512,128]{1,0:T(8,128)(2,1)S(1)}, bf16[512,128]{1,0:T(8,128)(2,1)S(1)}, u32[]{:S(2)}, u32[]{:S(2)}) collective-permute-start(bf16[512,128]{1,0:T(8,128)(2,1)S(1)} %pad_maximum_fusion.1), channel_id=1, source_target_pairs={{0,4},{1,5},{2,6},{3,7},{4,0},{5,1},{6,2},{7,3},{8,12},{9,13},{10,... | collective-permute-start | bytes 393224 | tf_op jit(solution)/shard_map/ppermute | solution.py:380
  12.0 8.9 %near.2.refs_6_ = f32[256,128]{1,0:T(8,128)S(1)} custom-call(s32[8,256]{1,0:T(8,128)S(1)} %get-tuple-element.42.plan_ref, f32[2,256,128]{2,1,0:T(8,128)S(1)} %get-tuple-element.54.rows_ref, f32[6,256,128]{2,1,0:T(8,128)S(1)} %get-tuple-element.55.coords_ref, bf16[32,128,128]{2,1,0:T(8,128)(2,1)S(1)} %get-tuple-element.56.left_ref), custom_call_target="tpu_custom_call" | custom-call | flops 200000000 | bytes 1000000 | tf_op jit(solution)/shard_map/near/pallas_call | solution.py:417
  20.9 0.0 collective-permute-done.3
  20.9 0.0 collective-permute-done.1
  21.0 0.0 copy-start.1
  21.0 0.0 copy-start.2
  21.0 0.1 collective-permute-start.2
  21.1 2.0 %collective-permute-start.4 = (bf16[288,128]{1,0:T(8,128)(2,1)S(1)}, bf16[288,128]{1,0:T(8,128)(2,1)S(1)}, u32[]{:S(2)}, u32[]{:S(2)}) collective-permute-start(bf16[288,128]{1,0:T(8,128)(2,1)S(1)} %constant_dynamic-update-slice_fusion), channel_id=1, source_target_pairs={{0,16},{8,24},{16,0},{24,8},{1,17},{9,25},{17,1},{25,9},{2,18},{10... | collective-permute-start | bytes 221192 | tf_op jit(solution)/shard_map/ppermute | solution.py:383
  23.1 0.0 copy-done.1
  23.1 0.0 copy-done.2
  23.1 0.1 copy.14
  23.2 0.1 reshape.9.refs_0_
  23.4 0.0 copy-start
  23.4 6.3 %near.3.refs_7_ = f32[256,128]{1,0:T(8,128)S(1)} custom-call(s32[8,256]{1,0:T(8,128)S(1)} %get-tuple-element.42.plan_ref, f32[2,256,128]{2,1,0:T(8,128)S(1)} %get-tuple-element.54.rows_ref, f32[6,256,128]{2,1,0:T(8,128)S(1)} %get-tuple-element.55.coords_ref, bf16[32,128,128]{2,1,0:T(8,128)(2,1)S(1)} %get-tuple-element.56.left_ref), custom_call_target="tpu_custom_call" | custom-call | flops 200000000 | bytes 1000000 | tf_op jit(solution)/shard_map/near/pallas_call | solution.py:417
  29.7 0.0 collective-permute-done.4
  29.7 0.0 collective-permute-done.2.refs_5_
  29.8 0.0 copy-done
  29.8 3.2 %far.1 = f32[256,128]{1,0:T(8,128)} custom-call(s32[16,128]{1,0:T(8,128)S(1)} %reshape.9.refs_0_, s32[2,128]{1,0:T(2,128)S(1)} %get-tuple-element.33.refs_0_.refs_1_, bf16[2048,128]{1,0:T(8,128)(2,1)S(1)} %bitcast.19, bf16[128,128]{1,0:T(8,128)(2,1)S(1)} %get-tuple-element.34.refs_3_, bf16[1024,128]{1,0:T(8,128)(2,1)S(1)} %pad_maximum_fusion.refs_4_, ...), custom_call_target="tpu_custom_call" | custom-call | flops 3000000000 | bytes 2000000 | tf_op jit(solution)/shard_map/far/pallas_call | solution.py:475
  (9 shorter events, 0.1 us)
Async XLA Ops:
  1.3 8.1 %collective-permute-start = (bf16[256,128]{1,0:T(8,128)(2,1)S(1)}, bf16[256,128]{1,0:T(8,128)(2,1)S(1)}, u32[]{:S(2)}, u32[]{:S(2)}) collective-permute-start(bf16[256,128]{1,0:T(8,128)(2,1)S(1)} %get-tuple-element.35.refs_2_), channel_id=1, source_target_pairs={{0,2},{1,3},{2,0},{3,1},{4,6},{5,7},{6,4},{7,5},{8,10},{9,11},{10,... | collective-permute-start | bytes 196616 | tf_op jit(solution)/shard_map/ppermute | solution.py:380
  7.8 13.1 %collective-permute-start.3 = (bf16[288,128]{1,0:T(8,128)(2,1)S(1)}, bf16[288,128]{1,0:T(8,128)(2,1)S(1)}, u32[]{:S(2)}, u32[]{:S(2)}) collective-permute-start(bf16[288,128]{1,0:T(8,128)(2,1)S(1)} %pad_maximum_fusion.2), channel_id=1, source_target_pairs={{0,8},{8,0},{16,24},{24,16},{1,9},{9,1},{17,25},{25,17},{2,10},{10... | collective-permute-start | bytes 221192 | tf_op jit(solution)/shard_map/ppermute | solution.py:383
  9.4 11.6 %collective-permute-start.1 = (bf16[512,128]{1,0:T(8,128)(2,1)S(1)}, bf16[512,128]{1,0:T(8,128)(2,1)S(1)}, u32[]{:S(2)}, u32[]{:S(2)}) collective-permute-start(bf16[512,128]{1,0:T(8,128)(2,1)S(1)} %pad_maximum_fusion.1), channel_id=1, source_target_pairs={{0,4},{1,5},{2,6},{3,7},{4,0},{5,1},{6,2},{7,3},{8,12},{9,13},{10,... | collective-permute-start | bytes 393224 | tf_op jit(solution)/shard_map/ppermute | solution.py:380
  21.0 2.1 %copy-start.1 = (s32[256,8]{0,1:T(8,128)S(1)}, s32[256,8]{0,1:T(8,128)}, u32[]{:S(2)}) copy-start(s32[256,8]{0,1:T(8,128)} %param.20) | copy-start | bytes 24580
  21.0 2.1 %copy-start.2 = (s32[256,8]{0,1:T(8,128)S(1)}, s32[256,8]{0,1:T(8,128)}, u32[]{:S(2)}) copy-start(s32[256,8]{0,1:T(8,128)} %param.19) | copy-start | bytes 24580
  21.0 8.7 %collective-permute-start.2 = (bf16[1024,128]{1,0:T(8,128)(2,1)S(1)}, bf16[1024,128]{1,0:T(8,128)(2,1)S(1)}, u32[]{:S(2)}, u32[]{:S(2)}) collective-permute-start(bf16[1024,128]{1,0:T(8,128)(2,1)S(1)} %pad_maximum_fusion.refs_4_), channel_id=1, source_target_pairs={{0,1},{1,0},{2,3},{3,2},{4,5},{5,4},{6,7},{7,6},{8,9},{9,8},{10,11... | collective-permute-start | bytes 786440 | tf_op jit(solution)/shard_map/ppermute | solution.py:380
  21.1 8.6 %collective-permute-start.4 = (bf16[288,128]{1,0:T(8,128)(2,1)S(1)}, bf16[288,128]{1,0:T(8,128)(2,1)S(1)}, u32[]{:S(2)}, u32[]{:S(2)}) collective-permute-start(bf16[288,128]{1,0:T(8,128)(2,1)S(1)} %constant_dynamic-update-slice_fusion), channel_id=1, source_target_pairs={{0,16},{8,24},{16,0},{24,8},{1,17},{9,25},{17,1},{25,9},{2,18},{10... | collective-permute-start | bytes 221192 | tf_op jit(solution)/shard_map/ppermute | solution.py:383
  23.4 6.4 %copy-start = (bf16[16,128,128]{2,1,0:T(8,128)(2,1)S(1)}, bf16[16,128,128]{2,1,0:T(8,128)(2,1)}, u32[]{:S(2)}) copy-start(bf16[16,128,128]{2,1,0:T(8,128)(2,1)} %param.16) | copy-start | bytes 1572868

commit v13 on v11

--- a/solution.py
+++ b/solution.py
@@ -196,12 +196,11 @@
     out_ref[...] = jnp.zeros_like(out_ref)
 
     def build(g, carry):
-        rows = pl.ds(pl.multiple_of(g * 8, 8), 8)
-        tile = [coords_ref[f, rows, :] for f in range(6)]
         for r in range(8):
+            row = pl.ds(g * 8 + r, 1)
             for c in range(3):
-                h = jnp.broadcast_to(tile[2 * c][r : r + 1], (8, LANES))
-                m = jnp.broadcast_to(tile[2 * c + 1][r : r + 1], (8, LANES))
+                h = jnp.broadcast_to(coords_ref[2 * c, row, :], (8, LANES))
+                m = jnp.broadcast_to(coords_ref[2 * c + 1, row, :], (8, LANES))
                 right[g * 8 + r, 16 * c : 16 * c + 16, :] = jnp.concatenate(
                     [h, m], axis=0
                 ).astype(BF16)

time: 31.2 us -> 31.2 us (level)
  no operation moved by 1% of the time
where the time goes in v13:
time: 31.2 us; the launch traced here: 31.1 us
  Pallas kernels  21.5 us (69%)
  starting transfers between devices  9.06 us (29%)
    pallas_call x2, Pallas kernels, near_piece(): pl.pallas_call(functools.partial(near_kernel, start=start, stop=stop), ou...  13.7 us
    ppermute x3, starting transfers between devices, over_cube(): return lax.ppermute(value, 'cube', [(i, i ^ k) for i in range(n_cube)])  5.82 us
    pallas_call x1, Pallas kernels, body(): pl.pallas_call(plan_kernel, out_shape=(jax.ShapeDtypeStruct((8, boxes), j...  3.36 us
    ppermute x2, starting transfers between devices, over_oct(): return lax.ppermute(value, 'oct', [(i, i ^ k) for i in range(n_oct)])  3.24 us
    pallas_call x1, Pallas kernels, body(): pl.pallas_call(functools.partial(far_kernel, blocks=n_cube, fanin=klist,...  3.2 us
    pallas_call x1, Pallas kernels, body(): pl.pallas_call(functools.partial(front_kernel, extra=len(handed)), out_sh...  1.3 us
  transfers between devices with their start and end apart: 5, of which 0 were waited for; matrix products, arithmetic and copies ran while one was open for 1% of the time, Pallas kernels for 55%

profile of v13, /device:TPU:0, one launch (start us, length us, event | category | flops | bytes accessed | tf_op | source)
XLA Modules:
  0.0 31.1 jit_solution(10857490957096287014)
XLA Ops:
  0.0 1.3 %front.1 = (f32[256,128]{1,0:T(8,128)S(1)}, s32[2,128]{1,0:T(2,128)S(1)}, bf16[256,128]{1,0:T(8,128)(2,1)S(1)}, s32[4,256]{1,0:T(4,128)S(1)}, f32[3,256,128]{2,1...) custom-call(bf16[256,128]{1,0:T(8,128)(2,1)} %refs_0_.1, ...), custom_call_target="tpu_custom_call" | custom-call | flops 10000000 | bytes 300000 | tf_op jit(solution)/shard_map/front/pallas_call | solution.py:355
  1.3 3.1 %collective-permute-start = (bf16[256,128]{1,0:T(8,128)(2,1)S(1)}, bf16[256,128]{1,0:T(8,128)(2,1)S(1)}, u32[]{:S(2)}, u32[]{:S(2)}) collective-permute-start(bf16[256,128]{1,0:T(8,128)(2,1)S(1)} %get-tuple-element.35.refs_2_), channel_id=1, source_target_pairs={{0,2},{1,3},{2,0},{3,1},{4,6},{5,7},{6,4},{7,5},{8,10},{9,11},{10,... | collective-permute-start | bytes 196616 | tf_op jit(solution)/shard_map/ppermute | solution.py:378
  4.4 3.4 %plan.1 = (s32[8,256]{1,0:T(8,128)S(1)}, f32[2,256,128]{2,1,0:T(8,128)S(1)}, f32[6,256,128]{2,1,0:T(8,128)S(1)}, bf16[32,128,128]{2,1,0:T(8,128)(2,1)S(1)}, bf16[4,144,128]{2,1,0:T(8,128)(2,1)S(1)}) custom-call(s32[2,128]{1,0:T(2,128)S(1)} %get-tuple-element.33.refs_0_.refs_1_, f32[256,128]{1,0:T(8,128)S(1)} %get-tuple-element.36.refs_1_, ...), custom_call_target="tpu_custom_call" | custom-call | flops 1000000000 | bytes 2000000 | tf_op jit(solution)/shard_map/plan/pallas_call | solution.py:387
  7.8 1.6 %collective-permute-start.3 = (bf16[288,128]{1,0:T(8,128)(2,1)S(1)}, bf16[288,128]{1,0:T(8,128)(2,1)S(1)}, u32[]{:S(2)}, u32[]{:S(2)}) collective-permute-start(bf16[288,128]{1,0:T(8,128)(2,1)S(1)} %pad_maximum_fusion.2), channel_id=1, source_target_pairs={{0,8},{8,0},{16,24},{24,16},{1,9},{9,1},{17,25},{25,17},{2,10},{10... | collective-permute-start | bytes 221192 | tf_op jit(solution)/shard_map/ppermute | solution.py:381
  9.4 0.0 collective-permute-done
  9.4 2.7 %collective-permute-start.1 = (bf16[512,128]{1,0:T(8,128)(2,1)S(1)}, bf16[512,128]{1,0:T(8,128)(2,1)S(1)}, u32[]{:S(2)}, u32[]{:S(2)}) collective-permute-start(bf16[512,128]{1,0:T(8,128)(2,1)S(1)} %pad_maximum_fusion.1), channel_id=1, source_target_pairs={{0,4},{1,5},{2,6},{3,7},{4,0},{5,1},{6,2},{7,3},{8,12},{9,13},{10,... | collective-permute-start | bytes 393224 | tf_op jit(solution)/shard_map/ppermute | solution.py:378
  12.0 8.0 %near.2.refs_6_ = f32[256,128]{1,0:T(8,128)S(1)} custom-call(s32[8,256]{1,0:T(8,128)S(1)} %get-tuple-element.42.plan_ref, f32[2,256,128]{2,1,0:T(8,128)S(1)} %get-tuple-element.54.rows_ref, f32[6,256,128]{2,1,0:T(8,128)S(1)} %get-tuple-element.55.coords_ref, bf16[32,128,128]{2,1,0:T(8,128)(2,1)S(1)} %get-tuple-element.56.left_ref), custom_call_target="tpu_custom_call" | custom-call | flops 200000000 | bytes 1000000 | tf_op jit(solution)/shard_map/near/pallas_call | solution.py:415
  20.1 0.0 collective-permute-done.3
  20.1 0.0 collective-permute-done.1
  20.1 0.0 copy-start.1
  20.2 0.0 copy-start.2
  20.2 0.1 collective-permute-start.2
  20.3 1.7 %collective-permute-start.4 = (bf16[288,128]{1,0:T(8,128)(2,1)S(1)}, bf16[288,128]{1,0:T(8,128)(2,1)S(1)}, u32[]{:S(2)}, u32[]{:S(2)}) collective-permute-start(bf16[288,128]{1,0:T(8,128)(2,1)S(1)} %constant_dynamic-update-slice_fusion), channel_id=1, source_target_pairs={{0,16},{8,24},{16,0},{24,8},{1,17},{9,25},{17,1},{25,9},{2,18},{10... | collective-permute-start | bytes 221192 | tf_op jit(solution)/shard_map/ppermute | solution.py:381
  22.0 0.0 copy-done.1
  22.0 0.0 copy-done.2
  22.0 0.1 copy.14
  22.1 0.1 reshape.9.refs_0_
  22.2 0.0 copy-start
  22.2 5.6 %near.3.refs_7_ = f32[256,128]{1,0:T(8,128)S(1)} custom-call(s32[8,256]{1,0:T(8,128)S(1)} %get-tuple-element.42.plan_ref, f32[2,256,128]{2,1,0:T(8,128)S(1)} %get-tuple-element.54.rows_ref, f32[6,256,128]{2,1,0:T(8,128)S(1)} %get-tuple-element.55.coords_ref, bf16[32,128,128]{2,1,0:T(8,128)(2,1)S(1)} %get-tuple-element.56.left_ref), custom_call_target="tpu_custom_call" | custom-call | flops 200000000 | bytes 1000000 | tf_op jit(solution)/shard_map/near/pallas_call | solution.py:415
  27.9 0.0 collective-permute-done.4
  27.9 0.0 collective-permute-done.2.refs_5_
  27.9 0.0 copy-done
  27.9 3.2 %far.1 = f32[256,128]{1,0:T(8,128)} custom-call(s32[16,128]{1,0:T(8,128)S(1)} %reshape.9.refs_0_, s32[2,128]{1,0:T(2,128)S(1)} %get-tuple-element.33.refs_0_.refs_1_, bf16[2048,128]{1,0:T(8,128)(2,1)S(1)} %bitcast.19, bf16[128,128]{1,0:T(8,128)(2,1)S(1)} %get-tuple-element.34.refs_3_, bf16[1024,128]{1,0:T(8,128)(2,1)S(1)} %pad_maximum_fusion.refs_4_, ...), custom_call_target="tpu_custom_call" | custom-call | flops 3000000000 | bytes 2000000 | tf_op jit(solution)/shard_map/far/pallas_call | solution.py:473
  (9 shorter events, 0.1 us)
Async XLA Ops:
  1.3 8.1 %collective-permute-start = (bf16[256,128]{1,0:T(8,128)(2,1)S(1)}, bf16[256,128]{1,0:T(8,128)(2,1)S(1)}, u32[]{:S(2)}, u32[]{:S(2)}) collective-permute-start(bf16[256,128]{1,0:T(8,128)(2,1)S(1)} %get-tuple-element.35.refs_2_), channel_id=1, source_target_pairs={{0,2},{1,3},{2,0},{3,1},{4,6},{5,7},{6,4},{7,5},{8,10},{9,11},{10,... | collective-permute-start | bytes 196616 | tf_op jit(solution)/shard_map/ppermute | solution.py:378
  7.8 12.3 %collective-permute-start.3 = (bf16[288,128]{1,0:T(8,128)(2,1)S(1)}, bf16[288,128]{1,0:T(8,128)(2,1)S(1)}, u32[]{:S(2)}, u32[]{:S(2)}) collective-permute-start(bf16[288,128]{1,0:T(8,128)(2,1)S(1)} %pad_maximum_fusion.2), channel_id=1, source_target_pairs={{0,8},{8,0},{16,24},{24,16},{1,9},{9,1},{17,25},{25,17},{2,10},{10... | collective-permute-start | bytes 221192 | tf_op jit(solution)/shard_map/ppermute | solution.py:381
  9.4 10.7 %collective-permute-start.1 = (bf16[512,128]{1,0:T(8,128)(2,1)S(1)}, bf16[512,128]{1,0:T(8,128)(2,1)S(1)}, u32[]{:S(2)}, u32[]{:S(2)}) collective-permute-start(bf16[512,128]{1,0:T(8,128)(2,1)S(1)} %pad_maximum_fusion.1), channel_id=1, source_target_pairs={{0,4},{1,5},{2,6},{3,7},{4,0},{5,1},{6,2},{7,3},{8,12},{9,13},{10,... | collective-permute-start | bytes 393224 | tf_op jit(solution)/shard_map/ppermute | solution.py:378
  20.1 1.8 %copy-start.1 = (s32[256,8]{0,1:T(8,128)S(1)}, s32[256,8]{0,1:T(8,128)}, u32[]{:S(2)}) copy-start(s32[256,8]{0,1:T(8,128)} %param.20) | copy-start | bytes 24580
  20.2 1.8 %copy-start.2 = (s32[256,8]{0,1:T(8,128)S(1)}, s32[256,8]{0,1:T(8,128)}, u32[]{:S(2)}) copy-start(s32[256,8]{0,1:T(8,128)} %param.19) | copy-start | bytes 24580
  20.2 7.7 %collective-permute-start.2 = (bf16[1024,128]{1,0:T(8,128)(2,1)S(1)}, bf16[1024,128]{1,0:T(8,128)(2,1)S(1)}, u32[]{:S(2)}, u32[]{:S(2)}) collective-permute-start(bf16[1024,128]{1,0:T(8,128)(2,1)S(1)} %pad_maximum_fusion.refs_4_), channel_id=1, source_target_pairs={{0,1},{1,0},{2,3},{3,2},{4,5},{5,4},{6,7},{7,6},{8,9},{9,8},{10,11... | collective-permute-start | bytes 786440 | tf_op jit(solution)/shard_map/ppermute | solution.py:378
  20.3 7.6 %collective-permute-start.4 = (bf16[288,128]{1,0:T(8,128)(2,1)S(1)}, bf16[288,128]{1,0:T(8,128)(2,1)S(1)}, u32[]{:S(2)}, u32[]{:S(2)}) collective-permute-start(bf16[288,128]{1,0:T(8,128)(2,1)S(1)} %constant_dynamic-update-slice_fusion), channel_id=1, source_target_pairs={{0,16},{8,24},{16,0},{24,8},{1,17},{9,25},{17,1},{25,9},{2,18},{10... | collective-permute-start | bytes 221192 | tf_op jit(solution)/shard_map/ppermute | solution.py:381
  22.2 5.7 %copy-start = (bf16[16,128,128]{2,1,0:T(8,128)(2,1)S(1)}, bf16[16,128,128]{2,1,0:T(8,128)(2,1)}, u32[]{:S(2)}) copy-start(bf16[16,128,128]{2,1,0:T(8,128)(2,1)} %param.16) | copy-start | bytes 1572868

commit v14 on v13

--- a/solution.py
+++ b/solution.py
@@ -195,14 +195,20 @@
     knear = 4
     out_ref[...] = jnp.zeros_like(out_ref)
 
+    zero8 = jnp.zeros((8, LANES), F32)
+
     def build(g, carry):
+        n = rows_ref[0, pl.ds(pl.multiple_of(g * 8, 8), 8), :]
+        n1 = n.astype(BF16).astype(F32)
+        n2 = (n - n1).astype(BF16).astype(F32)
+        norms = [n1, n2, n - n1 - n2]
         for r in range(8):
             row = pl.ds(g * 8 + r, 1)
-            for c in range(3):
-                h = jnp.broadcast_to(coords_ref[2 * c, row, :], (8, LANES))
-                m = jnp.broadcast_to(coords_ref[2 * c + 1, row, :], (8, LANES))
-                right[g * 8 + r, 16 * c : 16 * c + 16, :] = jnp.concatenate(
-                    [h, m], axis=0
+            wide = [jnp.broadcast_to(coords_ref[f, row, :], (8, LANES)) for f in range(6)]
+            wide += [jnp.broadcast_to(v[r : r + 1], (8, LANES)) for v in norms] + [zero8]
+            for i in range(5):
+                right[g * 8 + r, 16 * i : 16 * i + 16, :] = jnp.concatenate(
+                    wide[2 * i : 2 * i + 2], axis=0
                 ).astype(BF16)
         return carry
 
@@ -210,28 +216,33 @@
 
     ones = jnp.where(iota((32, LANES), 0) < 24, 1.0, 0.0).astype(BF16)
 
+    none = jnp.zeros((96, LANES), BF16)
+
     def operand(box):
-        x, y, z = [right[box, 16 * c : 16 * c + 16, :] for c in range(3)]
-        return jnp.concatenate([x, x, y, y, z, z, ones], axis=0)
+        x, y, z, n, t = [right[box, 16 * c : 16 * c + 16, :] for c in range(5)]
+        return jnp.concatenate([x, x, y, y, z, z, ones, n, t, none], axis=0)
 
     def team(depth, g, carry):
         masks = [
             jnp.where((iota((depth, LANES), 1) & 7) == j, 1.0, 0.0).astype(BF16) for j in range(8)
         ]
-        eye = iota((depth, LANES), 0) == iota((depth, LANES), 1)
+        lane = iota((depth, LANES), 1)
+        units = [
+            jnp.where(((lane & 7) == j) & (lane < 24), 1.0, 0.0).astype(BF16) for j in range(8)
+        ]
+        eye = iota((depth, LANES), 0) == lane
         for e in range(TEAM // 8):
             turned = left_ref[g * (TEAM // 8) + e, 0:depth, :]
             for r in range(8):
                 place = g * TEAM + e * 8 + r
-                lhs = turned * masks[r]
+                lhs = jnp.concatenate([turned * masks[r], units[r]], axis=1)
                 acc = None
                 for k in range(0, knear, 2):
                     pair = [plan_ref[k + i, place] for i in range(2)]
                     dist = dot(lhs, jnp.concatenate([operand(b) for b in pair], axis=1))
                     for i in range(2):
-                        shift = rows_ref[0, pl.ds(pair[i], 1), :]
                         q = rows_ref[1, pl.ds(pair[i], 1), :]
-                        term = lax.rsqrt(dist[:, i * LANES : (i + 1) * LANES] + shift) * q
+                        term = lax.rsqrt(dist[:, i * LANES : (i + 1) * LANES]) * q
                         acc = term if acc is None else acc + term
                 total = jnp.sum(acc, axis=1, keepdims=True)
                 out_ref[pl.ds(plan_ref[knear + 1, place], 1), :] = jnp.sum(
@@ -417,7 +428,7 @@
             out_shape=jax.ShapeDtypeStruct((boxes, panels), F32),
             in_specs=[SMEM, VMEM, VMEM, VMEM],
             out_specs=VMEM,
-            scratch_shapes=[pltpu.VMEM((boxes, 48, panels), BF16)],
+            scratch_shapes=[pltpu.VMEM((boxes, 80, panels), BF16)],
             compiler_params=pltpu.CompilerParams(vmem_limit_bytes=12 * MIB),
             cost_estimate=pl.CostEstimate(
                 flops=200_000_000, bytes_accessed=1_000_000, transcendentals=0

time: 31.2 us -> 31.7 us (1.016)
  Pallas kernels: 21.5 us -> 22.1 us
    pallas_call x2, Pallas kernels: 13.7 us -> 14.2 us  [near_piece(): pl.pallas_call(functools.partial(near_kernel, start=start, stop=stop), ou...]
  transfers between devices with their start and end apart: 5 -> 5, of which waited for: 0 -> 0; matrix products, arithmetic and copies ran while one was open for 1% -> 1% of each run, Pallas kernels for 55% -> 56%
where the time goes in v14:
time: 31.7 us; the launch traced here: 31.5 us
  Pallas kernels  22.1 us (70%)
  starting transfers between devices  8.93 us (28%)
    pallas_call x2, Pallas kernels, near_piece(): pl.pallas_call(functools.partial(near_kernel, start=start, stop=stop), ou...  14.2 us
    ppermute x3, starting transfers between devices, over_cube(): return lax.ppermute(value, 'cube', [(i, i ^ k) for i in range(n_cube)])  5.82 us
    pallas_call x1, Pallas kernels, body(): pl.pallas_call(plan_kernel, out_shape=(jax.ShapeDtypeStruct((8, boxes), j...  3.36 us
    pallas_call x1, Pallas kernels, body(): pl.pallas_call(functools.partial(far_kernel, blocks=n_cube, fanin=klist,...  3.2 us
    ppermute x2, starting transfers between devices, over_oct(): return lax.ppermute(value, 'oct', [(i, i ^ k) for i in range(n_oct)])  3.11 us
    pallas_call x1, Pallas kernels, body(): pl.pallas_call(functools.partial(front_kernel, extra=len(handed)), out_sh...  1.3 us
  transfers between devices with their start and end apart: 5, of which 0 were waited for; matrix products, arithmetic and copies ran while one was open for 1% of the time, Pallas kernels for 56%

profile of v14, /device:TPU:0, one launch (start us, length us, event | category | flops | bytes accessed | tf_op | source)
XLA Modules:
  0.0 31.5 jit_solution(2459350758098471851)
XLA Ops:
  0.0 1.3 %front.1 = (f32[256,128]{1,0:T(8,128)S(1)}, s32[2,128]{1,0:T(2,128)S(1)}, bf16[256,128]{1,0:T(8,128)(2,1)S(1)}, s32[4,256]{1,0:T(4,128)S(1)}, f32[3,256,128]{2,1...) custom-call(bf16[256,128]{1,0:T(8,128)(2,1)} %refs_0_.1, ...), custom_call_target="tpu_custom_call" | custom-call | flops 10000000 | bytes 300000 | tf_op jit(solution)/shard_map/front/pallas_call | solution.py:366
  1.3 3.1 %collective-permute-start = (bf16[256,128]{1,0:T(8,128)(2,1)S(1)}, bf16[256,128]{1,0:T(8,128)(2,1)S(1)}, u32[]{:S(2)}, u32[]{:S(2)}) collective-permute-start(bf16[256,128]{1,0:T(8,128)(2,1)S(1)} %get-tuple-element.35.refs_2_), channel_id=1, source_target_pairs={{0,2},{1,3},{2,0},{3,1},{4,6},{5,7},{6,4},{7,5},{8,10},{9,11},{10,... | collective-permute-start | bytes 196616 | tf_op jit(solution)/shard_map/ppermute | solution.py:389
  4.4 3.4 %plan.1 = (s32[8,256]{1,0:T(8,128)S(1)}, f32[2,256,128]{2,1,0:T(8,128)S(1)}, f32[6,256,128]{2,1,0:T(8,128)S(1)}, bf16[32,128,128]{2,1,0:T(8,128)(2,1)S(1)}, bf16[4,144,128]{2,1,0:T(8,128)(2,1)S(1)}) custom-call(s32[2,128]{1,0:T(2,128)S(1)} %get-tuple-element.33.refs_0_.refs_1_, f32[256,128]{1,0:T(8,128)S(1)} %get-tuple-element.36.refs_1_, ...), custom_call_target="tpu_custom_call" | custom-call | flops 1000000000 | bytes 2000000 | tf_op jit(solution)/shard_map/plan/pallas_call | solution.py:398
  7.8 1.6 %collective-permute-start.3 = (bf16[288,128]{1,0:T(8,128)(2,1)S(1)}, bf16[288,128]{1,0:T(8,128)(2,1)S(1)}, u32[]{:S(2)}, u32[]{:S(2)}) collective-permute-start(bf16[288,128]{1,0:T(8,128)(2,1)S(1)} %pad_maximum_fusion.2), channel_id=1, source_target_pairs={{0,8},{8,0},{16,24},{24,16},{1,9},{9,1},{17,25},{25,17},{2,10},{10... | collective-permute-start | bytes 221192 | tf_op jit(solution)/shard_map/ppermute | solution.py:392
  9.4 0.0 collective-permute-done
  9.4 2.7 %collective-permute-start.1 = (bf16[512,128]{1,0:T(8,128)(2,1)S(1)}, bf16[512,128]{1,0:T(8,128)(2,1)S(1)}, u32[]{:S(2)}, u32[]{:S(2)}) collective-permute-start(bf16[512,128]{1,0:T(8,128)(2,1)S(1)} %pad_maximum_fusion.1), channel_id=1, source_target_pairs={{0,4},{1,5},{2,6},{3,7},{4,0},{5,1},{6,2},{7,3},{8,12},{9,13},{10,... | collective-permute-start | bytes 393224 | tf_op jit(solution)/shard_map/ppermute | solution.py:389
  12.0 8.6 %near.2.refs_6_ = f32[256,128]{1,0:T(8,128)S(1)} custom-call(s32[8,256]{1,0:T(8,128)S(1)} %get-tuple-element.42.plan_ref, f32[2,256,128]{2,1,0:T(8,128)S(1)} %get-tuple-element.54.rows_ref, f32[6,256,128]{2,1,0:T(8,128)S(1)} %get-tuple-element.55.coords_ref, bf16[32,128,128]{2,1,0:T(8,128)(2,1)S(1)} %get-tuple-element.56.left_ref), custom_call_target="tpu_custom_call" | custom-call | flops 200000000 | bytes 1000000 | tf_op jit(solution)/shard_map/near/pallas_call | solution.py:426
  20.6 0.0 collective-permute-done.3
  20.6 0.0 collective-permute-done.1
  20.7 0.0 copy-start.1
  20.7 0.0 copy-start.2
  20.7 0.1 collective-permute-start.2
  20.8 1.6 %collective-permute-start.4 = (bf16[288,128]{1,0:T(8,128)(2,1)S(1)}, bf16[288,128]{1,0:T(8,128)(2,1)S(1)}, u32[]{:S(2)}, u32[]{:S(2)}) collective-permute-start(bf16[288,128]{1,0:T(8,128)(2,1)S(1)} %constant_dynamic-update-slice_fusion), channel_id=1, source_target_pairs={{0,16},{8,24},{16,0},{24,8},{1,17},{9,25},{17,1},{25,9},{2,18},{10... | collective-permute-start | bytes 221192 | tf_op jit(solution)/shard_map/ppermute | solution.py:392
  22.4 0.0 copy-done.1
  22.4 0.0 copy-done.2
  22.4 0.1 copy.14
  22.5 0.1 reshape.9.refs_0_
  22.6 0.0 copy-start
  22.6 5.7 %near.3.refs_7_ = f32[256,128]{1,0:T(8,128)S(1)} custom-call(s32[8,256]{1,0:T(8,128)S(1)} %get-tuple-element.42.plan_ref, f32[2,256,128]{2,1,0:T(8,128)S(1)} %get-tuple-element.54.rows_ref, f32[6,256,128]{2,1,0:T(8,128)S(1)} %get-tuple-element.55.coords_ref, bf16[32,128,128]{2,1,0:T(8,128)(2,1)S(1)} %get-tuple-element.56.left_ref), custom_call_target="tpu_custom_call" | custom-call | flops 200000000 | bytes 1000000 | tf_op jit(solution)/shard_map/near/pallas_call | solution.py:426
  28.3 0.0 collective-permute-done.4
  28.3 0.0 collective-permute-done.2.refs_5_
  28.3 0.0 copy-done
  28.3 3.2 %far.1 = f32[256,128]{1,0:T(8,128)} custom-call(s32[16,128]{1,0:T(8,128)S(1)} %reshape.9.refs_0_, s32[2,128]{1,0:T(2,128)S(1)} %get-tuple-element.33.refs_0_.refs_1_, bf16[2048,128]{1,0:T(8,128)(2,1)S(1)} %bitcast.19, bf16[128,128]{1,0:T(8,128)(2,1)S(1)} %get-tuple-element.34.refs_3_, bf16[1024,128]{1,0:T(8,128)(2,1)S(1)} %pad_maximum_fusion.refs_4_, ...), custom_call_target="tpu_custom_call" | custom-call | flops 3000000000 | bytes 2000000 | tf_op jit(solution)/shard_map/far/pallas_call | solution.py:484
  (9 shorter events, 0.1 us)
Async XLA Ops:
  1.3 8.1 %collective-permute-start = (bf16[256,128]{1,0:T(8,128)(2,1)S(1)}, bf16[256,128]{1,0:T(8,128)(2,1)S(1)}, u32[]{:S(2)}, u32[]{:S(2)}) collective-permute-start(bf16[256,128]{1,0:T(8,128)(2,1)S(1)} %get-tuple-element.35.refs_2_), channel_id=1, source_target_pairs={{0,2},{1,3},{2,0},{3,1},{4,6},{5,7},{6,4},{7,5},{8,10},{9,11},{10,... | collective-permute-start | bytes 196616 | tf_op jit(solution)/shard_map/ppermute | solution.py:389
  7.8 12.8 %collective-permute-start.3 = (bf16[288,128]{1,0:T(8,128)(2,1)S(1)}, bf16[288,128]{1,0:T(8,128)(2,1)S(1)}, u32[]{:S(2)}, u32[]{:S(2)}) collective-permute-start(bf16[288,128]{1,0:T(8,128)(2,1)S(1)} %pad_maximum_fusion.2), channel_id=1, source_target_pairs={{0,8},{8,0},{16,24},{24,16},{1,9},{9,1},{17,25},{25,17},{2,10},{10... | collective-permute-start | bytes 221192 | tf_op jit(solution)/shard_map/ppermute | solution.py:392
  9.4 11.3 %collective-permute-start.1 = (bf16[512,128]{1,0:T(8,128)(2,1)S(1)}, bf16[512,128]{1,0:T(8,128)(2,1)S(1)}, u32[]{:S(2)}, u32[]{:S(2)}) collective-permute-start(bf16[512,128]{1,0:T(8,128)(2,1)S(1)} %pad_maximum_fusion.1), channel_id=1, source_target_pairs={{0,4},{1,5},{2,6},{3,7},{4,0},{5,1},{6,2},{7,3},{8,12},{9,13},{10,... | collective-permute-start | bytes 393224 | tf_op jit(solution)/shard_map/ppermute | solution.py:389
  20.7 1.7 %copy-start.1 = (s32[256,8]{0,1:T(8,128)S(1)}, s32[256,8]{0,1:T(8,128)}, u32[]{:S(2)}) copy-start(s32[256,8]{0,1:T(8,128)} %param.20) | copy-start | bytes 24580
  20.7 1.7 %copy-start.2 = (s32[256,8]{0,1:T(8,128)S(1)}, s32[256,8]{0,1:T(8,128)}, u32[]{:S(2)}) copy-start(s32[256,8]{0,1:T(8,128)} %param.19) | copy-start | bytes 24580
  20.7 7.6 %collective-permute-start.2 = (bf16[1024,128]{1,0:T(8,128)(2,1)S(1)}, bf16[1024,128]{1,0:T(8,128)(2,1)S(1)}, u32[]{:S(2)}, u32[]{:S(2)}) collective-permute-start(bf16[1024,128]{1,0:T(8,128)(2,1)S(1)} %pad_maximum_fusion.refs_4_), channel_id=1, source_target_pairs={{0,1},{1,0},{2,3},{3,2},{4,5},{5,4},{6,7},{7,6},{8,9},{9,8},{10,11... | collective-permute-start | bytes 786440 | tf_op jit(solution)/shard_map/ppermute | solution.py:389
  20.8 7.5 %collective-permute-start.4 = (bf16[288,128]{1,0:T(8,128)(2,1)S(1)}, bf16[288,128]{1,0:T(8,128)(2,1)S(1)}, u32[]{:S(2)}, u32[]{:S(2)}) collective-permute-start(bf16[288,128]{1,0:T(8,128)(2,1)S(1)} %constant_dynamic-update-slice_fusion), channel_id=1, source_target_pairs={{0,16},{8,24},{16,0},{24,8},{1,17},{9,25},{17,1},{25,9},{2,18},{10... | collective-permute-start | bytes 221192 | tf_op jit(solution)/shard_map/ppermute | solution.py:392
  22.6 5.7 %copy-start = (bf16[16,128,128]{2,1,0:T(8,128)(2,1)S(1)}, bf16[16,128,128]{2,1,0:T(8,128)(2,1)}, u32[]{:S(2)}) copy-start(bf16[16,128,128]{2,1,0:T(8,128)(2,1)} %param.16) | copy-start | bytes 1572868

commit v15 on v13

--- a/solution.py
+++ b/solution.py
@@ -319,7 +319,7 @@
 
 
 PIECES = 2
-TEAM = 16
+TEAM = 32
 STEP = 16
 
 
@@ -409,7 +409,7 @@
     )(counts, strength, multipole, *handed, in_hbm(operators))
 
     teams = boxes // TEAM
-    cut = teams * 11 // 16
+    cut = teams * 3 // 4
 
     def near_piece(start, stop, tables):
         return pl.pallas_call(

time: 31.2 us -> 29.8 us (0.955)
  Pallas kernels: 21.5 us -> 20.1 us
    pallas_call x2, Pallas kernels: 13.7 us -> 12.3 us  [near_piece(): pl.pallas_call(functools.partial(near_kernel, start=start, stop=stop), ou...]
  transfers between devices with their start and end apart: 5 -> 5, of which waited for: 0 -> 0; matrix products, arithmetic and copies ran while one was open for 1% -> 1% of each run, Pallas kernels for 55% -> 53%
where the time goes in v15:
time: 29.8 us; the launch traced here: 29.6 us
  Pallas kernels  20.1 us (67%)
  starting transfers between devices  8.96 us (30%)
  local copies, waits for them, and re-layouts  0.31 us (1%)
    pallas_call x2, Pallas kernels, near_piece(): pl.pallas_call(functools.partial(near_kernel, start=start, stop=stop), ou...  12.3 us
    ppermute x3, starting transfers between devices, over_cube(): return lax.ppermute(value, 'cube', [(i, i ^ k) for i in range(n_cube)])  5.82 us
    pallas_call x1, Pallas kernels, body(): pl.pallas_call(plan_kernel, out_shape=(jax.ShapeDtypeStruct((8, boxes), j...  3.36 us
    pallas_call x1, Pallas kernels, body(): pl.pallas_call(functools.partial(far_kernel, blocks=n_cube, fanin=klist,...  3.18 us
    ppermute x2, starting transfers between devices, over_oct(): return lax.ppermute(value, 'oct', [(i, i ^ k) for i in range(n_oct)])  3.14 us
    pallas_call x1, Pallas kernels, body(): pl.pallas_call(functools.partial(front_kernel, extra=len(handed)), out_sh...  1.3 us
  transfers between devices with their start and end apart: 5, of which 0 were waited for; matrix products, arithmetic and copies ran while one was open for 1% of the time, Pallas kernels for 53%

profile of v15, /device:TPU:0, one launch (start us, length us, event | category | flops | bytes accessed | tf_op | source)
XLA Modules:
  0.0 29.6 jit_solution(3071542113604486425)
XLA Ops:
  0.0 1.3 %front.1 = (f32[256,128]{1,0:T(8,128)S(1)}, s32[2,128]{1,0:T(2,128)S(1)}, bf16[256,128]{1,0:T(8,128)(2,1)S(1)}, s32[4,256]{1,0:T(4,128)S(1)}, f32[3,256,128]{2,1...) custom-call(bf16[256,128]{1,0:T(8,128)(2,1)} %refs_0_.1, ...), custom_call_target="tpu_custom_call" | custom-call | flops 10000000 | bytes 300000 | tf_op jit(solution)/shard_map/front/pallas_call | solution.py:355
  1.3 3.1 %collective-permute-start = (bf16[256,128]{1,0:T(8,128)(2,1)S(1)}, bf16[256,128]{1,0:T(8,128)(2,1)S(1)}, u32[]{:S(2)}, u32[]{:S(2)}) collective-permute-start(bf16[256,128]{1,0:T(8,128)(2,1)S(1)} %get-tuple-element.35.refs_2_), channel_id=1, source_target_pairs={{0,2},{1,3},{2,0},{3,1},{4,6},{5,7},{6,4},{7,5},{8,10},{9,11},{10,... | collective-permute-start | bytes 196616 | tf_op jit(solution)/shard_map/ppermute | solution.py:378
  4.4 3.4 %plan.1 = (s32[8,256]{1,0:T(8,128)S(1)}, f32[2,256,128]{2,1,0:T(8,128)S(1)}, f32[6,256,128]{2,1,0:T(8,128)S(1)}, bf16[32,128,128]{2,1,0:T(8,128)(2,1)S(1)}, bf16[4,144,128]{2,1,0:T(8,128)(2,1)S(1)}) custom-call(s32[2,128]{1,0:T(2,128)S(1)} %get-tuple-element.33.refs_0_.refs_1_, f32[256,128]{1,0:T(8,128)S(1)} %get-tuple-element.36.refs_1_, ...), custom_call_target="tpu_custom_call" | custom-call | flops 1000000000 | bytes 2000000 | tf_op jit(solution)/shard_map/plan/pallas_call | solution.py:387
  7.8 1.6 %collective-permute-start.3 = (bf16[288,128]{1,0:T(8,128)(2,1)S(1)}, bf16[288,128]{1,0:T(8,128)(2,1)S(1)}, u32[]{:S(2)}, u32[]{:S(2)}) collective-permute-start(bf16[288,128]{1,0:T(8,128)(2,1)S(1)} %pad_maximum_fusion.2), channel_id=1, source_target_pairs={{0,8},{8,0},{16,24},{24,16},{1,9},{9,1},{17,25},{25,17},{2,10},{10... | collective-permute-start | bytes 221192 | tf_op jit(solution)/shard_map/ppermute | solution.py:381
  9.4 0.0 collective-permute-done
  9.4 2.7 %collective-permute-start.1 = (bf16[512,128]{1,0:T(8,128)(2,1)S(1)}, bf16[512,128]{1,0:T(8,128)(2,1)S(1)}, u32[]{:S(2)}, u32[]{:S(2)}) collective-permute-start(bf16[512,128]{1,0:T(8,128)(2,1)S(1)} %pad_maximum_fusion.1), channel_id=1, source_target_pairs={{0,4},{1,5},{2,6},{3,7},{4,0},{5,1},{6,2},{7,3},{8,12},{9,13},{10,... | collective-permute-start | bytes 393224 | tf_op jit(solution)/shard_map/ppermute | solution.py:378
  12.0 7.8 %near.2.refs_6_ = f32[256,128]{1,0:T(8,128)S(1)} custom-call(s32[8,256]{1,0:T(8,128)S(1)} %get-tuple-element.42.plan_ref, f32[2,256,128]{2,1,0:T(8,128)S(1)} %get-tuple-element.54.rows_ref, f32[6,256,128]{2,1,0:T(8,128)S(1)} %get-tuple-element.55.coords_ref, bf16[32,128,128]{2,1,0:T(8,128)(2,1)S(1)} %get-tuple-element.56.left_ref), custom_call_target="tpu_custom_call" | custom-call | flops 200000000 | bytes 1000000 | tf_op jit(solution)/shard_map/near/pallas_call | solution.py:415
  19.9 0.0 collective-permute-done.3
  19.9 0.0 collective-permute-done.1
  19.9 0.0 copy-start.1
  20.0 0.0 copy-start.2
  20.0 0.1 collective-permute-start.2
  20.1 1.6 %collective-permute-start.4 = (bf16[288,128]{1,0:T(8,128)(2,1)S(1)}, bf16[288,128]{1,0:T(8,128)(2,1)S(1)}, u32[]{:S(2)}, u32[]{:S(2)}) collective-permute-start(bf16[288,128]{1,0:T(8,128)(2,1)S(1)} %constant_dynamic-update-slice_fusion), channel_id=1, source_target_pairs={{0,16},{8,24},{16,0},{24,8},{1,17},{9,25},{17,1},{25,9},{2,18},{10... | collective-permute-start | bytes 221192 | tf_op jit(solution)/shard_map/ppermute | solution.py:381
  21.7 0.0 copy-done.1
  21.7 0.0 copy-done.2
  21.7 0.1 copy.14
  21.8 0.1 reshape.9.refs_0_
  21.9 0.0 copy-start
  21.9 4.5 %near.3.refs_7_ = f32[256,128]{1,0:T(8,128)S(1)} custom-call(s32[8,256]{1,0:T(8,128)S(1)} %get-tuple-element.42.plan_ref, f32[2,256,128]{2,1,0:T(8,128)S(1)} %get-tuple-element.54.rows_ref, f32[6,256,128]{2,1,0:T(8,128)S(1)} %get-tuple-element.55.coords_ref, bf16[32,128,128]{2,1,0:T(8,128)(2,1)S(1)} %get-tuple-element.56.left_ref), custom_call_target="tpu_custom_call" | custom-call | flops 200000000 | bytes 1000000 | tf_op jit(solution)/shard_map/near/pallas_call | solution.py:415
  26.4 0.0 collective-permute-done.4
  26.4 0.0 collective-permute-done.2.refs_5_
  26.4 0.0 copy-done
  26.4 3.2 %far.1 = f32[256,128]{1,0:T(8,128)} custom-call(s32[16,128]{1,0:T(8,128)S(1)} %reshape.9.refs_0_, s32[2,128]{1,0:T(2,128)S(1)} %get-tuple-element.33.refs_0_.refs_1_, bf16[2048,128]{1,0:T(8,128)(2,1)S(1)} %bitcast.19, bf16[128,128]{1,0:T(8,128)(2,1)S(1)} %get-tuple-element.34.refs_3_, bf16[1024,128]{1,0:T(8,128)(2,1)S(1)} %pad_maximum_fusion.refs_4_, ...), custom_call_target="tpu_custom_call" | custom-call | flops 3000000000 | bytes 2000000 | tf_op jit(solution)/shard_map/far/pallas_call | solution.py:473
  (9 shorter events, 0.1 us)
Async XLA Ops:
  1.3 8.1 %collective-permute-start = (bf16[256,128]{1,0:T(8,128)(2,1)S(1)}, bf16[256,128]{1,0:T(8,128)(2,1)S(1)}, u32[]{:S(2)}, u32[]{:S(2)}) collective-permute-start(bf16[256,128]{1,0:T(8,128)(2,1)S(1)} %get-tuple-element.35.refs_2_), channel_id=1, source_target_pairs={{0,2},{1,3},{2,0},{3,1},{4,6},{5,7},{6,4},{7,5},{8,10},{9,11},{10,... | collective-permute-start | bytes 196616 | tf_op jit(solution)/shard_map/ppermute | solution.py:378
  7.8 12.1 %collective-permute-start.3 = (bf16[288,128]{1,0:T(8,128)(2,1)S(1)}, bf16[288,128]{1,0:T(8,128)(2,1)S(1)}, u32[]{:S(2)}, u32[]{:S(2)}) collective-permute-start(bf16[288,128]{1,0:T(8,128)(2,1)S(1)} %pad_maximum_fusion.2), channel_id=1, source_target_pairs={{0,8},{8,0},{16,24},{24,16},{1,9},{9,1},{17,25},{25,17},{2,10},{10... | collective-permute-start | bytes 221192 | tf_op jit(solution)/shard_map/ppermute | solution.py:381
  9.4 10.5 %collective-permute-start.1 = (bf16[512,128]{1,0:T(8,128)(2,1)S(1)}, bf16[512,128]{1,0:T(8,128)(2,1)S(1)}, u32[]{:S(2)}, u32[]{:S(2)}) collective-permute-start(bf16[512,128]{1,0:T(8,128)(2,1)S(1)} %pad_maximum_fusion.1), channel_id=1, source_target_pairs={{0,4},{1,5},{2,6},{3,7},{4,0},{5,1},{6,2},{7,3},{8,12},{9,13},{10,... | collective-permute-start | bytes 393224 | tf_op jit(solution)/shard_map/ppermute | solution.py:378
  19.9 1.7 %copy-start.1 = (s32[256,8]{0,1:T(8,128)S(1)}, s32[256,8]{0,1:T(8,128)}, u32[]{:S(2)}) copy-start(s32[256,8]{0,1:T(8,128)} %param.20) | copy-start | bytes 24580
  20.0 1.7 %copy-start.2 = (s32[256,8]{0,1:T(8,128)S(1)}, s32[256,8]{0,1:T(8,128)}, u32[]{:S(2)}) copy-start(s32[256,8]{0,1:T(8,128)} %param.19) | copy-start | bytes 24580
  20.0 6.4 %collective-permute-start.2 = (bf16[1024,128]{1,0:T(8,128)(2,1)S(1)}, bf16[1024,128]{1,0:T(8,128)(2,1)S(1)}, u32[]{:S(2)}, u32[]{:S(2)}) collective-permute-start(bf16[1024,128]{1,0:T(8,128)(2,1)S(1)} %pad_maximum_fusion.refs_4_), channel_id=1, source_target_pairs={{0,1},{1,0},{2,3},{3,2},{4,5},{5,4},{6,7},{7,6},{8,9},{9,8},{10,11... | collective-permute-start | bytes 786440 | tf_op jit(solution)/shard_map/ppermute | solution.py:378
  20.1 6.3 %collective-permute-start.4 = (bf16[288,128]{1,0:T(8,128)(2,1)S(1)}, bf16[288,128]{1,0:T(8,128)(2,1)S(1)}, u32[]{:S(2)}, u32[]{:S(2)}) collective-permute-start(bf16[288,128]{1,0:T(8,128)(2,1)S(1)} %constant_dynamic-update-slice_fusion), channel_id=1, source_target_pairs={{0,16},{8,24},{16,0},{24,8},{1,17},{9,25},{17,1},{25,9},{2,18},{10... | collective-permute-start | bytes 221192 | tf_op jit(solution)/shard_map/ppermute | solution.py:381
  21.9 4.5 %copy-start = (bf16[16,128,128]{2,1,0:T(8,128)(2,1)S(1)}, bf16[16,128,128]{2,1,0:T(8,128)(2,1)}, u32[]{:S(2)}) copy-start(bf16[16,128,128]{2,1,0:T(8,128)(2,1)} %param.16) | copy-start | bytes 1572868
